TPU v7x, 768 devices: a whole 4x8x12 slice. The times are simulated.
768 devices in a mesh: rows: 48 (over x, z), cols: 16 (over y, core).
Axes of the slice: x: 4, y: 8, z: 12, core: 2. Of those that a mesh axis runs over, the one named last changes fastest.
Arguments:
- features: bfloat16 [98304, 512], P(('rows', 'cols')), may hold values from -6 to 6
- blocks: bfloat16 [48, 512, 128, 128], P('rows', 'cols'), may hold values from -0.15625 to 0.15625
- block_rows: int32 [48, 512], P('rows', 'cols'), may hold values from 0 to 15
- block_cols: int32 [48, 512], P('rows', 'cols'), may hold values from 0 to 6
- block_count: int32 [48, 16], P('rows', 'cols'), may hold values from 1 to 32, as said below
- send_rows: int32 [48, 768, 16], P('rows', 'cols'), may hold values from 0 to 127
Outputs:
- diffused: bfloat16 [98304, 512], P(('rows', 'cols'))
- diffused_two: bfloat16 [98304, 512], P(('rows', 'cols'))
Inputs may be any that keep to these rules, and one draw needn't show every extreme that they name: `block_count`: some device has 32 live tiles.
All inputs are finite; a program needn't handle non-finite values.
Results may differ from a plain program's by a relative error of at most 0.025.
Values may be sent and summed in bfloat16 or wider, within the bound.
No kernel may reach another device: no remote copies, remote signals or barrier semaphores. Data moves between devices by JAX's collectives and lax.ppermute only.
A program may use at most 32 MiB of HBM per device.

v0:
```python
import jax
import jax.numpy as jnp
from jax import lax
from jax.sharding import PartitionSpec as P

GRP = 8


def add_range(total, tiles_held, rows_held, cols_held, first, last, lowest, space):
    group_size = GRP
    begin = first // group_size
    finish = (last + group_size - 1) // group_size
    upper = total.shape[0] - 1

    def step(index, carry):
        start = index * group_size
        group = lax.dynamic_slice_in_dim(tiles_held, start, group_size, 0)
        rows_now = lax.dynamic_slice_in_dim(rows_held, start, group_size, 0)
        cols_now = lax.dynamic_slice_in_dim(cols_held, start, group_size, 0)
        position = start + jnp.arange(group_size, dtype=jnp.int32)
        wanted = (position >= first) & (position < last)
        prods = jnp.einsum(
            "kij,kjf->kif", group, space[cols_now], preferred_element_type=jnp.float32
        )
        prods = jnp.where(wanted[:, None, None], prods, 0.0)
        target = jnp.clip(rows_now - lowest, 0, upper)
        return carry.at[target].add(prods)

    return lax.fori_loop(begin, finish, step, total)


def on_device(features, blocks, block_rows, block_cols, block_count, send_rows):
    held = blocks[0]
    count = block_count[0, 0]
    lists = send_rows[0]
    tile = held.shape[1]
    width = features.shape[1]
    own_rows = features.shape[0]
    slab_tiles = lax.axis_size("cols") * (own_rows // tile)
    slots = held.shape[0]
    live = jnp.arange(slots, dtype=jnp.int32) < count
    sort_key = jnp.where(live, block_rows[0], slab_tiles)
    order = jnp.argsort(sort_key, stable=True)
    sorted_tiles = held[order]
    sorted_rows = sort_key[order]
    sorted_cols = block_cols[0][order]

    def spread(field):
        picked = field[lists]
        fetched = lax.all_to_all(picked, "rows", split_axis=0, concat_axis=0, tiled=True)
        space = jnp.concatenate(
            [field.reshape(-1, tile, width), fetched.reshape(-1, tile, width)], 0
        )
        partial_value = jnp.zeros((slab_tiles, tile, width), jnp.float32)
        partial_value = add_range(
            partial_value, sorted_tiles, sorted_rows, sorted_cols, 0, count, 0, space
        )
        summed = lax.psum_scatter(
            partial_value.reshape(-1, width).astype(jnp.bfloat16),
            "cols",
            scatter_dimension=0,
            tiled=True,
        )
        return summed

    diffused = spread(features)
    return (diffused, spread(diffused))


def solution(mesh):
    placed = (
        P(("rows", "cols"), None),
        P("rows", "cols", None, None),
        P("rows", "cols"),
        P("rows", "cols"),
        P("rows", "cols"),
        P("rows", "cols", None),
    )
    return jax.shard_map(
        on_device,
        mesh=mesh,
        in_specs=placed,
        out_specs=(P(("rows", "cols"), None), P(("rows", "cols"), None)),
        check_vma=False,
    )
```

profile of v0, /device:TPU:1, one launch (start us, length us, event | category | flops | bytes accessed | tf_op | source)
XLA Modules:
  0.0 325.5 jit_solution(8602709071452484805)
XLA Ops:
  8.2 4.3 %gather_fusion.5 = bf16[768,512]{1,0:T(8,128)(2,1)} fusion(bf16[128,512]{1,0:T(8,128)(2,1)} %param.10, s32[1024]{0:T(1024)S(1)} %pad_clamp_fusion.2), kind=kCustom, calls=%fused_computation.5 | custom fusion | bytes 1575936 | tf_op jit(solution)/shard_map/gather | solution.py:49
  12.4 19.0 %all-to-all-start = ((bf16[48,16,512]{2,1,0:T(8,128)(2,1)}), bf16[48,16,512]{2,1,0:T(8,128)(2,1)S(1)}, u32[]{:S(2)}, u32[]{:S(2)}) async-start(bf16[48,16,512]{2,1,0:T(8,128)(2,1)} %bitcast.6), calls=%async_computation | async-start | bytes 1572864 | tf_op jit(solution)/shard_map/all_to_all | solution.py:50
  32.2 1.6 sort.17
  35.2 1.7 gather_fusion.3
  36.9 24.0 %all-to-all-done = bf16[48,16,512]{2,1,0:T(8,128)(2,1)S(1)} async-done(((bf16[48,16,512]{2,1,0:T(8,128)(2,1)}), bf16[48,16,512]{2,1,0:T(8,128)(2,1)S(1)}, u32[]{:S(2)}, u32[]{:S(2)}) %all-to-all-start) | async-done | bytes 786464 | tf_op jit(solution)/shard_map/all_to_all | solution.py:50
  60.8 1.0 pad_maximum_fusion
  61.9 2.5 broadcast.68.clone
  64.3 9.4 %while.20 = (s32[]{:T(128)}, f32[16,128,512]{2,1,0:T(8,128)}, s32[]{:T(128)}, s32[32]{0:T(128)S(1)}, s32[]{:T(128)}, /*index=5*/bf16[32,128,128]{2,1,0:T(8,128)(...) while((s32[]{:T(128)}, f32[16,128,512]{2,1,0:T(8,128)}, ...), condition=%wide.region_3.4_spmd, body=%wide.region_1.3_spmd.sunk | while | flops 135267424 | bytes 11800995 | solution.py:29
  65.1 2.8 gather_fusion
  67.9 1.7 convolution_select_fusion.4
  69.6 4.2 %scatter_fusion = f32[16,128,512]{2,1,0:T(8,128)} fusion(f32[16,128,512]{2,1,0:T(8,128)} %get-tuple-element.249, s32[8]{0:T(128)S(1)} %get-tuple-element.224, f32[8,128,512]{2,1,0:T(8,128)S(1)} %convolution_select_fusion.4), kind=kCustom, calls=%fused_computation.7.clone.1 | custom fusion | flops 524288 | bytes 6291488 | tf_op jit(solution)/shard_map/while/body/scatter-add | solution.py:27
  73.8 3.8 %convert_element_type.12 = bf16[16,128,512]{2,1,0:T(8,128)(2,1)} convert(f32[16,128,512]{2,1,0:T(8,128)} %get-tuple-element.90) | non-fusion elementwise | flops 1048576 | bytes 6291456 | tf_op jit(solution)/shard_map/convert_element_type | solution.py:59
  77.6 89.6 %reduce-scatter.3.cloned.1.call-done = bf16[128,512]{1,0:T(8,128)(2,1)} async-done(((bf16[2048,512]{1,0:T(8,128)(2,1)}), bf16[128,512]{1,0:T(8,128)(2,1)}) %reduce-scatter.3.cloned.1.call-update) | async-done | bytes 131088 | tf_op jit(solution)/shard_map/reduce_scatter | solution.py:58
  167.2 4.4 %gather_fusion.6 = bf16[768,512]{1,0:T(8,128)(2,1)} fusion(bf16[128,512]{1,0:T(8,128)(2,1)} %reduce-scatter.3.cloned.1.call-done, s32[1024]{0:T(1024)S(1)} %pad_clamp_fusion.2), kind=kCustom, calls=%fused_computation.6 | custom fusion | bytes 1575936 | tf_op jit(solution)/shard_map/gather | solution.py:49
  171.6 11.5 %all-to-all-start.1 = ((bf16[48,16,512]{2,1,0:T(8,128)(2,1)}), bf16[48,16,512]{2,1,0:T(8,128)(2,1)S(1)}, u32[]{:S(2)}, u32[]{:S(2)}) async-start(bf16[48,16,512]{2,1,0:T(8,128)(2,1)} %bitcast.10), calls=%async_computation.2 | async-start | bytes 1572864 | tf_op jit(solution)/shard_map/all_to_all | solution.py:50
  183.1 26.5 %all-to-all-done.1 = bf16[48,16,512]{2,1,0:T(8,128)(2,1)S(1)} async-done(((bf16[48,16,512]{2,1,0:T(8,128)(2,1)}), bf16[48,16,512]{2,1,0:T(8,128)(2,1)S(1)}, u32[]{:S(2)}, u32[]{:S(2)}) %all-to-all-start.1) | async-done | bytes 786464 | tf_op jit(solution)/shard_map/all_to_all | solution.py:50
  209.6 1.0 pad_maximum_fusion.1
  210.6 2.5 broadcast.68
  213.1 9.4 %while.21 = (s32[]{:T(128)}, f32[16,128,512]{2,1,0:T(8,128)}, s32[]{:T(128)}, s32[32]{0:T(128)S(1)}, s32[]{:T(128)}, /*index=5*/bf16[32,128,128]{2,1,0:T(8,128)(...) while((s32[]{:T(128)}, f32[16,128,512]{2,1,0:T(8,128)}, ...), condition=%wide.region_7.8_spmd, body=%wide.region_5.7_spmd.sunk | while | flops 135267424 | bytes 11800995 | solution.py:29
  213.9 2.8 gather_fusion.1
  216.6 1.7 convolution_select_fusion.5
  218.4 4.2 %scatter_fusion.1 = f32[16,128,512]{2,1,0:T(8,128)} fusion(f32[16,128,512]{2,1,0:T(8,128)} %get-tuple-element.285, s32[8]{0:T(128)S(1)} %get-tuple-element.234, f32[8,128,512]{2,1,0:T(8,128)S(1)} %convolution_select_fusion.5), kind=kCustom, calls=%fused_computation.8.clone.1 | custom fusion | flops 524288 | bytes 6291488 | tf_op jit(solution)/shard_map/while/body/scatter-add | solution.py:27
  222.5 3.8 %convert_element_type.14 = bf16[16,128,512]{2,1,0:T(8,128)(2,1)} convert(f32[16,128,512]{2,1,0:T(8,128)} %get-tuple-element.91) | non-fusion elementwise | flops 1048576 | bytes 6291456 | tf_op jit(solution)/shard_map/convert_element_type | solution.py:59
  226.4 92.3 %reduce-scatter.5.cloned.1.call-done = bf16[128,512]{1,0:T(8,128)(2,1)} async-done(((bf16[2048,512]{1,0:T(8,128)(2,1)}), bf16[128,512]{1,0:T(8,128)(2,1)}) %reduce-scatter.5.cloned.1.call-update) | async-done | bytes 131088 | tf_op jit(solution)/shard_map/reduce_scatter | solution.py:58
  (30 shorter events, 4.0 us)
Async XLA Ops:
  7.2 28.0 %copy-start = (bf16[1,32,128,128]{3,2,1,0:T(8,128)(2,1)S(1)}, bf16[1,32,128,128]{3,2,1,0:T(8,128)(2,1)}, u32[]{:S(2)}) copy-start(bf16[1,32,128,128]{3,2,1,0:T(8,128)(2,1)} %param.11) | copy-start | bytes 3145732
  8.1 24.0 %copy-start.4 = (s32[1,32]{1,0:T(1,128)S(1)}, s32[1,32]{1,0:T(1,128)}, u32[]{:S(2)}) copy-start(s32[1,32]{1,0:T(1,128)} %param.12) | copy-start | bytes 388
  12.4 22.0 %copy-start.1 = (s32[1,32]{1,0:T(1,128)S(1)}, s32[1,32]{1,0:T(1,128)}, u32[]{:S(2)}) copy-start(s32[1,32]{1,0:T(1,128)} %param.13) | copy-start | bytes 388
  12.4 48.4 %copy-start.2 = (bf16[128,512]{1,0:T(8,128)(2,1)S(1)}, bf16[128,512]{1,0:T(8,128)(2,1)}, u32[]{:S(2)}) copy-start(bf16[128,512]{1,0:T(8,128)(2,1)} %param.10) | copy-start | bytes 393220
  12.4 48.4 %all-to-all-start = ((bf16[48,16,512]{2,1,0:T(8,128)(2,1)}), bf16[48,16,512]{2,1,0:T(8,128)(2,1)S(1)}, u32[]{:S(2)}, u32[]{:S(2)}) async-start(bf16[48,16,512]{2,1,0:T(8,128)(2,1)} %bitcast.6), calls=%async_computation | async-start | bytes 1572864 | tf_op jit(solution)/shard_map/all_to_all | solution.py:50
  31.4 135.8 %reduce-scatter.3.cloned.1.call-start = ((), (), s32[]{:S(2)}) async-start(), calls=%async_computation.4 | async-start | bytes 2228224 | tf_op jit(solution)/shard_map/reduce_scatter | solution.py:58
  167.2 42.4 %copy-start.3 = (bf16[128,512]{1,0:T(8,128)(2,1)S(1)}, bf16[128,512]{1,0:T(8,128)(2,1)}, u32[]{:S(2)}) copy-start(bf16[128,512]{1,0:T(8,128)(2,1)} %reduce-scatter.3.cloned.1.call-done) | copy-start | bytes 393220
  171.6 38.1 %all-to-all-start.1 = ((bf16[48,16,512]{2,1,0:T(8,128)(2,1)}), bf16[48,16,512]{2,1,0:T(8,128)(2,1)S(1)}, u32[]{:S(2)}, u32[]{:S(2)}) async-start(bf16[48,16,512]{2,1,0:T(8,128)(2,1)} %bitcast.10), calls=%async_computation.2 | async-start | bytes 1572864 | tf_op jit(solution)/shard_map/all_to_all | solution.py:50
  183.1 135.6 %reduce-scatter.5.cloned.1.call-start = ((), (), s32[]{:S(2)}) async-start(), calls=%async_computation.5 | async-start | bytes 2228224 | tf_op jit(solution)/shard_map/reduce_scatter | solution.py:58
Sparse Core Ops, SparseCore 0:
  77.7 89.4 reduce-scatter.2
  226.5 92.0 reduce-scatter.4
where the time goes:
time: 327 us; the launch traced here: 325 us
  waiting for transfers between devices  232 us (71%)
  starting transfers between devices  30.5 us (9%)
  local copies, waits for them, and re-layouts  22.4 us (7%)
  other arithmetic  21.9 us (7%)
  between operations  14.8 us (5%)
  matrix products  3.46 us (1%)
    reduce_scatter x2, waiting for transfers between devices, spread(): lax.psum_scatter(partial_value.reshape(-1, width).astype(jnp.bfloat16), '...  182 us
    all_to_all x2, waiting for transfers between devices, spread(): lax.all_to_all(picked, 'rows', split_axis=0, concat_axis=0, tiled=True)  50.5 us
    all_to_all x2, starting transfers between devices, spread(): lax.all_to_all(picked, 'rows', split_axis=0, concat_axis=0, tiled=True)  30.5 us
    gather x2, local copies, waits for them, and re-layouts, spread(): picked = field[lists]  8.64 us
    scatter-add x2, other arithmetic, step(): return carry.at[target].add(prods)  8.35 us
    convert_element_type x2, other arithmetic, spread(): partial_value.reshape(-1, width).astype(jnp.bfloat16)  7.61 us
  transfers between devices with their start and end apart: 4, of which 4 were waited for; matrix products, arithmetic and copies ran while one was open for 1% of the time, Pallas kernels for 0%

commit v1 on v0

v1 whole, which is shorter than its diff:
```python
import functools

import jax
import jax.numpy as jnp
from jax import lax
from jax.experimental import pallas as pl
from jax.experimental.pallas import tpu as pltpu
from jax.sharding import Mesh, PartitionSpec as P

GRP = 4
PAIR = [(0, 1), (1, 0)]


def build_kernel(slots, cap, meta_ref, own_ref, other_ref, out_ref, total, spread):
    tile = own_ref.shape[1]
    cells_down, cells_across = total.shape[0], total.shape[1]
    source = lax.broadcasted_iota(jnp.int32, (tile, 2 * tile), 0)
    place = lax.broadcasted_iota(jnp.int32, (tile, 2 * tile), 1)
    for side in range(2):
        plain = side * tile + source
        mixed = (source // cap) * (2 * cap) + side * cap + source % cap
        spread[2 * side] = jnp.where(place == plain, 1.0, 0.0).astype(jnp.bfloat16)
        spread[2 * side + 1] = jnp.where(place == mixed, 1.0, 0.0).astype(jnp.bfloat16)

    def clear(s, carry):
        for t in range(cells_across):
            total[s, t] = jnp.zeros((tile, 2 * tile), jnp.float32)
        return carry

    lax.fori_loop(0, cells_down, clear, 0)
    for side, ref in enumerate((own_ref, other_ref)):
        count = meta_ref[side, 2 * slots]

        def group(index, carry, side=side, ref=ref, count=count):
            found = []
            for step in range(GRP):
                k = index * GRP + step
                col = meta_ref[side, slots + k]
                held = jnp.where(k < count, ref[k], jnp.zeros((tile, tile), ref.dtype))
                kind = 2 * side + jnp.minimum(col, 1)
                moved = jnp.dot(held, spread[kind], preferred_element_type=jnp.float32)
                found.append((meta_ref[side, k], col, moved))
            for row, col, moved in found:
                total[row, col] += moved
            return carry

        lax.fori_loop(0, (count + GRP - 1) // GRP, group, 0)

    def store(s, carry):
        for t in range(cells_across):
            rows = pl.ds(pl.multiple_of(s * tile, tile), tile)
            out_ref[rows, pl.ds(t * 2 * tile, 2 * tile)] = total[s, t].astype(out_ref.dtype)
        return carry

    lax.fori_loop(0, cells_down, store, 0)


def build(meta, own, other, slab_tiles, space_tiles, cap):
    slots, tile = own.shape[0], own.shape[1]
    shape = (slab_tiles * tile, space_tiles * 2 * tile)
    return pl.pallas_call(
        functools.partial(build_kernel, slots, cap),
        out_shape=jax.ShapeDtypeStruct(shape, jnp.bfloat16),
        in_specs=[
            pl.BlockSpec(memory_space=pltpu.SMEM),
            pl.BlockSpec(memory_space=pltpu.VMEM),
            pl.BlockSpec(memory_space=pltpu.VMEM),
        ],
        out_specs=pl.BlockSpec(memory_space=pltpu.VMEM),
        scratch_shapes=[
            pltpu.VMEM((slab_tiles, space_tiles, tile, 2 * tile), jnp.float32),
            pltpu.VMEM((4, tile, 2 * tile), jnp.bfloat16),
        ],
        compiler_params=pltpu.CompilerParams(vmem_limit_bytes=40 * 1024 * 1024),
        cost_estimate=pl.CostEstimate(
            flops=4 * slots * tile * tile * 2 * tile,
            bytes_accessed=8 * shape[0] * shape[1],
            transcendentals=0,
        ),
    )(meta, own, other)


def on_device(features, blocks, block_rows, block_cols, block_count, send_rows):
    held = blocks[0]
    slots, tile = held.shape[0], held.shape[1]
    rows, width = features.shape
    half = width // 2
    cap = send_rows.shape[2]
    owners = lax.axis_size("rows")
    slab_tiles = 2 * lax.axis_size("y")
    space_tiles = 1 + owners * cap // tile
    core = lax.axis_index("core")

    def swap(value):
        return lax.ppermute(value, "core", PAIR)

    low, high = features[:, :half], features[:, half:]
    mine = jnp.where(core == 0, low, high)
    theirs = swap(jnp.where(core == 0, high, low))
    own_field = jnp.concatenate([mine, theirs], 0)

    lists = send_rows[0].reshape(-1)
    numbers = jnp.concatenate([block_rows[0], block_cols[0], block_count[0], lists])
    numbers = jnp.pad(numbers, (0, -numbers.shape[0] % 128))
    both = jnp.stack([numbers, swap(numbers)])
    wanted = both[:, 2 * slots + 1 : 2 * slots + 1 + lists.shape[0]]
    wanted = wanted + jnp.array([[0], [rows]], jnp.int32)
    wanted = wanted.reshape(2, owners, cap).transpose(1, 0, 2).reshape(-1, 1)
    picker = (wanted == lax.broadcasted_iota(jnp.int32, (1, 2 * rows), 1)).astype(jnp.bfloat16)

    meta = both[:, : 2 * slots + 1]
    swapped = lax.broadcasted_iota(jnp.int32, meta.shape, 1) < slots
    meta = jnp.where(swapped, meta ^ core, meta)
    matrix = build(meta, held, swap(held), slab_tiles, space_tiles, cap)

    def hop(field):
        picked = jnp.dot(picker, field, preferred_element_type=jnp.bfloat16)
        fetched = lax.all_to_all(
            picked.reshape(owners, 2 * cap, half), "rows", 0, 0, tiled=True
        )
        space = jnp.concatenate([field, fetched.reshape(-1, half)], 0)
        partial_value = jnp.dot(matrix, space, preferred_element_type=jnp.bfloat16)
        parts = lax.all_to_all(
            partial_value.reshape(-1, 2 * rows, half), "y", 0, 0, tiled=True
        )
        return jnp.sum(parts.astype(jnp.float32), 0).astype(jnp.bfloat16)

    def whole(field):
        kept, other = field[:rows], swap(field[rows:])
        return jnp.concatenate(
            [jnp.where(core == 0, kept, other), jnp.where(core == 0, other, kept)], 1
        )

    first = hop(own_field)
    second = hop(first)
    return (whole(first), whole(second))


def solution(mesh):
    inner = Mesh(
        mesh.devices.reshape(mesh.shape["rows"], -1, 2), ("rows", "y", "core")
    )
    cols = ("y", "core")
    placed = (
        P(("rows", "y", "core"), None),
        P("rows", cols, None, None),
        P("rows", cols),
        P("rows", cols),
        P("rows", cols),
        P("rows", cols, None),
    )
    return jax.shard_map(
        on_device,
        mesh=inner,
        in_specs=placed,
        out_specs=(P(("rows", "y", "core"), None), P(("rows", "y", "core"), None)),
        check_vma=False,
    )
```

time: 327 us -> 186 us (0.57)
  waiting for transfers between devices: 232 us -> 73 us
  blocking collectives: 0 us -> 41.1 us
  other arithmetic: 21.9 us -> 3.39 us
  local copies, waits for them, and re-layouts: 22.4 us -> 4.18 us
  starting transfers between devices: 30.5 us -> 45.2 us
  between operations: 14.8 us -> 1.57 us
  matrix products: 3.46 us -> 14.1 us
    reduce_scatter x2 -> x0, waiting for transfers between devices: 182 us -> none  [spread(): lax.psum_scatter(partial_value.reshape(-1, width).astype(jnp.bfloat16), '...]
    all_to_all x0 -> x1, blocking collectives: none -> 41.1 us  [hop(): lax.all_to_all(picked.reshape(owners, 2 * cap, half), 'rows', 0, 0, tiled...]
    ppermute x0 -> x5, starting transfers between devices: none -> 25.9 us  [swap(): return lax.ppermute(value, 'core', PAIR)]
    all_to_all x2 -> x3, waiting for transfers between devices: 50.5 us -> 68.8 us  [the longest x2 48.4 us: hop(): lax.all_to_all(partial_value.reshape(-1, 2 * rows, half), 'y', 0, 0, tile...]
    gather x7 -> x0, local copies, waits for them, and re-layouts: 17.3 us -> none  [the longest x2 8.64 us: spread(): picked = field[lists]]
    all_to_all x2 -> x3, starting transfers between devices: 30.5 us -> 19.4 us  [the longest x2 10.4 us: hop(): lax.all_to_all(partial_value.reshape(-1, 2 * rows, half), 'y', 0, 0, tile...]
    dot_general x2 -> x4, matrix products: 3.46 us -> 14.1 us  [the longest x2 12.4 us: hop(): partial_value = jnp.dot(matrix, space, preferred_element_type=jnp.bfloat16)]
    scatter-add x2 -> x0, other arithmetic: 8.35 us -> none  [step(): return carry.at[target].add(prods)]
  transfers between devices with their start and end apart: 4 -> 8, of which waited for: 4 -> 7; matrix products, arithmetic and copies ran while one was open for 1% -> 1% of each run, Pallas kernels for 0% -> 2%
where the time goes in v1:
time: 186 us; the launch traced here: 185 us
  waiting for transfers between devices  73 us (39%)
  starting transfers between devices  45.2 us (24%)
  blocking collectives  41.1 us (22%)
  matrix products  14.1 us (8%)
  local copies, waits for them, and re-layouts  4.18 us (2%)
  other arithmetic  3.39 us (2%)
  Pallas kernels  2.84 us (2%)
    all_to_all x2, waiting for transfers between devices, hop(): lax.all_to_all(partial_value.reshape(-1, 2 * rows, half), 'y', 0, 0, tile...  48.4 us
    all_to_all x1, blocking collectives, hop(): lax.all_to_all(picked.reshape(owners, 2 * cap, half), 'rows', 0, 0, tiled...  41.1 us
    ppermute x5, starting transfers between devices, swap(): return lax.ppermute(value, 'core', PAIR)  25.9 us
    all_to_all x1, waiting for transfers between devices, hop(): lax.all_to_all(picked.reshape(owners, 2 * cap, half), 'rows', 0, 0, tiled...  20.4 us
    dot_general x2, matrix products, hop(): partial_value = jnp.dot(matrix, space, preferred_element_type=jnp.bfloat16)  12.4 us
    all_to_all x2, starting transfers between devices, hop(): lax.all_to_all(partial_value.reshape(-1, 2 * rows, half), 'y', 0, 0, tile...  10.4 us
    all_to_all x1, starting transfers between devices, hop(): lax.all_to_all(picked.reshape(owners, 2 * cap, half), 'rows', 0, 0, tiled...  9 us
    ppermute x5, waiting for transfers between devices, swap(): return lax.ppermute(value, 'core', PAIR)  4.17 us
  transfers between devices with their start and end apart: 8, of which 7 were waited for; matrix products, arithmetic and copies ran while one was open for 1% of the time, Pallas kernels for 2%

profile of v1, /device:TPU:1, one launch (start us, length us, event | category | flops | bytes accessed | tf_op | source)
XLA Modules:
  0.0 185.4 jit_solution(16748495600924838514)
XLA Ops:
  1.4 0.8 copy.9
  2.2 0.8 pad_add_fusion.1
  3.0 12.4 %collective-permute-start = (s32[896]{0:T(1024)S(1)}, s32[896]{0:T(1024)S(1)}, u32[]{:S(2)}, u32[]{:S(2)}) collective-permute-start(s32[896]{0:T(1024)S(1)} %pad.4), channel_id=1, source_target_pairs={{0,1},{1,0},{2,3},{3,2},{4,5},{5,4},{6,7},{7,6},{8,9},{9,8},{10,11... | collective-permute-start | bytes 10760 | tf_op jit(solution)/shard_map/ppermute | solution.py:95
  15.4 0.9 broadcast_select_fusion.5
  16.3 1.9 %collective-permute-start.2 = (bf16[128,256]{1,0:T(8,128)(2,1)S(1)}, bf16[128,256]{1,0:T(8,128)(2,1)S(1)}, u32[]{:S(2)}, u32[]{:S(2)}) collective-permute-start(bf16[128,256]{1,0:T(8,128)(2,1)S(1)} %get-tuple-element.7), channel_id=1, source_target_pairs={{0,1},{1,0},{2,3},{3,2},{4,5},{5,4},{6,7},{7,6},{8,9},{9,8},{10,11... | collective-permute-start | bytes 196616 | tf_op jit(solution)/shard_map/ppermute | solution.py:95
  18.6 0.8 collective-permute-done.2
  19.5 1.3 fusion
  20.8 9.0 %all-to-all-start = ((bf16[48,32,256]{2,1,0:T(8,128)(2,1)}), bf16[48,32,256]{2,1,0:T(8,128)(2,1)S(1)}, u32[]{:S(2)}, u32[]{:S(2)}) async-start(bf16[48,32,256]{2,1,0:T(8,128)(2,1)} %bitcast.5), calls=%async_computation | async-start | bytes 1572864 | tf_op jit(solution)/shard_map/all_to_all | solution.py:118
  29.8 2.3 %collective-permute-start.1 = (bf16[32,128,128]{2,1,0:T(8,128)(2,1)S(1)}, bf16[32,128,128]{2,1,0:T(8,128)(2,1)S(1)}, u32[]{:S(2)}, u32[]{:S(2)}) collective-permute-start(bf16[32,128,128]{2,1,0:T(8,128)(2,1)S(1)} %bitcast.17), channel_id=1, source_target_pairs={{0,1},{1,0},{2,3},{3,2},{4,5},{5,4},{6,7},{7,6},{8,9},{9,8},{10,11... | collective-permute-start | bytes 3145736 | tf_op jit(solution)/shard_map/ppermute | solution.py:95
  32.2 2.2 %collective-permute-done.1.other_ref = bf16[32,128,128]{2,1,0:T(8,128)(2,1)S(1)} collective-permute-done((bf16[32,128,128]{2,1,0:T(8,128)(2,1)S(1)}, bf16[32,128,128]{2,1,0:T(8,128)(2,1)S(1)}, u32[]{:S(2)}, u32[]{:S(2)}) %collective-permute-start.1) | collective-permute-done | bytes 1048608 | tf_op jit(solution)/shard_map/ppermute | solution.py:95
  34.4 2.8 %shard_map.86 = bf16[2048,1792]{1,0:T(8,128)(2,1)S(1)} custom-call(s32[2,65]{1,0:T(2,128)S(1)} %xor_select_fusion.meta_ref, bf16[32,128,128]{2,1,0:T(8,128)(2,1)S(1)} %bitcast.18, bf16[32,128,128]{2,1,0:T(8,128)(2,1)S(1)} %collective-permute-done.1.other_ref), custom_call_target="tpu_custom_call" | custom-call | flops 536870912 | bytes 29360128 | tf_op jit(solution)/shard_map/pallas_call | solution.py:61
  37.3 2.9 %copy-done = bf16[2048,1792]{1,0:T(8,128)(2,1)} copy-done((bf16[2048,1792]{1,0:T(8,128)(2,1)}, bf16[2048,1792]{1,0:T(8,128)(2,1)S(1)}, u32[]{:S(2)}) %copy-start) | copy-done | bytes 7340056
  40.2 20.4 %all-to-all-done = bf16[48,32,256]{2,1,0:T(8,128)(2,1)S(1)} async-done(((bf16[48,32,256]{2,1,0:T(8,128)(2,1)}), bf16[48,32,256]{2,1,0:T(8,128)(2,1)S(1)}, u32[]{:S(2)}, u32[]{:S(2)}) %all-to-all-start) | async-done | bytes 786464 | tf_op jit(solution)/shard_map/all_to_all | solution.py:118
  60.6 6.2 %fusion.2 = bf16[2048,256]{1,0:T(8,128)(2,1)} fusion(bf16[2048,1792]{1,0:T(8,128)(2,1)} %copy-done, bf16[1536,256]{1,0:T(8,128)(2,1)S(1)} %bitcast.19, bf16[128,256]{1,0:T(8,128)(2,1)S(1)} %collective-permute-done.2, bf16[128,256]{1,0:T(8,128)(2,1)S(1)} %get-tuple-element.6), kind=kOutput, calls=%fused_computation.4 | convolution fusion | flops 1881800704 | bytes 9306112 | tf_op jit(solution)/shard_map/dot_general | solution.py:122
  66.8 6.8 %all-to-all-start.1 = ((bf16[8,256,256]{2,1,0:T(8,128)(2,1)}), bf16[8,256,256]{2,1,0:T(8,128)(2,1)S(1)}, u32[]{:S(2)}, u32[]{:S(2)}) async-start(bf16[8,256,256]{2,1,0:T(8,128)(2,1)} %bitcast.7), calls=%async_computation.1 | async-start | bytes 2097152 | tf_op jit(solution)/shard_map/all_to_all | solution.py:123
  73.8 26.9 %all-to-all-done.1 = bf16[8,256,256]{2,1,0:T(8,128)(2,1)S(1)} async-done(((bf16[8,256,256]{2,1,0:T(8,128)(2,1)}), bf16[8,256,256]{2,1,0:T(8,128)(2,1)S(1)}, u32[]{:S(2)}, u32[]{:S(2)}) %all-to-all-start.1) | async-done | bytes 1048608 | tf_op jit(solution)/shard_map/all_to_all | solution.py:123
  101.3 41.1 %all_to_all.20 = bf16[48,32,256]{2,1,0:T(8,128)(2,1)S(1)} all-to-all(bf16[48,32,256]{2,1,0:T(8,128)(2,1)S(1)} %fusion.1), channel_id=1, replica_groups=mesh['rows'=48,'y'=8,'core'=2] {'rows'}, dimensions={0} | all-to-all | bytes 1572864 | tf_op jit(solution)/shard_map/all_to_all | solution.py:118
  142.4 6.2 %fusion.8 = bf16[2048,256]{1,0:T(8,128)(2,1)} fusion(bf16[2048,1792]{1,0:T(8,128)(2,1)} %copy-done, bf16[1536,256]{1,0:T(8,128)(2,1)S(1)} %bitcast.20, bf16[256,256]{1,0:T(8,128)(2,1)S(1)} %reduce_sum.24), kind=kOutput, calls=%fused_computation.10 | convolution fusion | flops 1880883200 | bytes 9306112 | tf_op jit(solution)/shard_map/dot_general | solution.py:122
  148.6 3.6 %all-to-all-start.3 = ((bf16[8,256,256]{2,1,0:T(8,128)(2,1)}), bf16[8,256,256]{2,1,0:T(8,128)(2,1)S(1)}, u32[]{:S(2)}, u32[]{:S(2)}) async-start(bf16[8,256,256]{2,1,0:T(8,128)(2,1)} %bitcast.11), calls=%async_computation.3 | async-start | bytes 2097152 | tf_op jit(solution)/shard_map/all_to_all | solution.py:123
  152.1 4.7 %collective-permute-start.3 = (bf16[128,256]{1,0:T(8,128)(2,1)S(1)}, bf16[128,256]{1,0:T(8,128)(2,1)S(1)}, u32[]{:S(2)}, u32[]{:S(2)}) collective-permute-start(bf16[128,256]{1,0:T(8,128)(2,1)S(1)} %slice.33), channel_id=1, source_target_pairs={{0,1},{1,0},{2,3},{3,2},{4,5},{5,4},{6,7},{7,6},{8,9},{9,8},{10,11... | collective-permute-start | bytes 196616 | tf_op jit(solution)/shard_map/ppermute | solution.py:95
  156.9 0.9 collective-permute-done.3
  157.8 21.4 %all-to-all-done.3 = bf16[8,256,256]{2,1,0:T(8,128)(2,1)S(1)} async-done(((bf16[8,256,256]{2,1,0:T(8,128)(2,1)}), bf16[8,256,256]{2,1,0:T(8,128)(2,1)S(1)}, u32[]{:S(2)}, u32[]{:S(2)}) %all-to-all-start.3) | async-done | bytes 1048608 | tf_op jit(solution)/shard_map/all_to_all | solution.py:123
  179.3 4.5 %collective-permute-start.4 = (bf16[128,256]{1,0:T(8,128)(2,1)S(1)}, bf16[128,256]{1,0:T(8,128)(2,1)S(1)}, u32[]{:S(2)}, u32[]{:S(2)}) collective-permute-start(bf16[128,256]{1,0:T(8,128)(2,1)S(1)} %slice.35), channel_id=1, source_target_pairs={{0,1},{1,0},{2,3},{3,2},{4,5},{5,4},{6,7},{7,6},{8,9},{9,8},{10,11... | collective-permute-start | bytes 196616 | tf_op jit(solution)/shard_map/ppermute | solution.py:95
  183.8 0.7 pad_maximum_fusion
  (26 shorter events, 2.2 us)
Async XLA Ops:
  0.6 29.2 %copy-start.1 = (bf16[1,32,128,128]{3,2,1,0:T(8,128)(2,1)S(1)}, bf16[1,32,128,128]{3,2,1,0:T(8,128)(2,1)}, u32[]{:S(2)}) copy-start(bf16[1,32,128,128]{3,2,1,0:T(8,128)(2,1)} %param.8) | copy-start | bytes 3145732
  3.0 15.3 %collective-permute-start = (s32[896]{0:T(1024)S(1)}, s32[896]{0:T(1024)S(1)}, u32[]{:S(2)}, u32[]{:S(2)}) collective-permute-start(s32[896]{0:T(1024)S(1)} %pad.4), channel_id=1, source_target_pairs={{0,1},{1,0},{2,3},{3,2},{4,5},{5,4},{6,7},{7,6},{8,9},{9,8},{10,11... | collective-permute-start | bytes 10760 | tf_op jit(solution)/shard_map/ppermute | solution.py:95
  16.3 3.1 %collective-permute-start.2 = (bf16[128,256]{1,0:T(8,128)(2,1)S(1)}, bf16[128,256]{1,0:T(8,128)(2,1)S(1)}, u32[]{:S(2)}, u32[]{:S(2)}) collective-permute-start(bf16[128,256]{1,0:T(8,128)(2,1)S(1)} %get-tuple-element.7), channel_id=1, source_target_pairs={{0,1},{1,0},{2,3},{3,2},{4,5},{5,4},{6,7},{7,6},{8,9},{9,8},{10,11... | collective-permute-start | bytes 196616 | tf_op jit(solution)/shard_map/ppermute | solution.py:95
  20.8 39.9 %all-to-all-start = ((bf16[48,32,256]{2,1,0:T(8,128)(2,1)}), bf16[48,32,256]{2,1,0:T(8,128)(2,1)S(1)}, u32[]{:S(2)}, u32[]{:S(2)}) async-start(bf16[48,32,256]{2,1,0:T(8,128)(2,1)} %bitcast.5), calls=%async_computation | async-start | bytes 1572864 | tf_op jit(solution)/shard_map/all_to_all | solution.py:118
  29.8 4.6 %collective-permute-start.1 = (bf16[32,128,128]{2,1,0:T(8,128)(2,1)S(1)}, bf16[32,128,128]{2,1,0:T(8,128)(2,1)S(1)}, u32[]{:S(2)}, u32[]{:S(2)}) collective-permute-start(bf16[32,128,128]{2,1,0:T(8,128)(2,1)S(1)} %bitcast.17), channel_id=1, source_target_pairs={{0,1},{1,0},{2,3},{3,2},{4,5},{5,4},{6,7},{7,6},{8,9},{9,8},{10,11... | collective-permute-start | bytes 3145736 | tf_op jit(solution)/shard_map/ppermute | solution.py:95
  37.3 2.9 %copy-start = (bf16[2048,1792]{1,0:T(8,128)(2,1)}, bf16[2048,1792]{1,0:T(8,128)(2,1)S(1)}, u32[]{:S(2)}) copy-start(bf16[2048,1792]{1,0:T(8,128)(2,1)S(1)} %shard_map.86) | copy-start | bytes 22020100
  66.8 33.9 %all-to-all-start.1 = ((bf16[8,256,256]{2,1,0:T(8,128)(2,1)}), bf16[8,256,256]{2,1,0:T(8,128)(2,1)S(1)}, u32[]{:S(2)}, u32[]{:S(2)}) async-start(bf16[8,256,256]{2,1,0:T(8,128)(2,1)} %bitcast.7), calls=%async_computation.1 | async-start | bytes 2097152 | tf_op jit(solution)/shard_map/all_to_all | solution.py:123
  148.6 30.6 %all-to-all-start.3 = ((bf16[8,256,256]{2,1,0:T(8,128)(2,1)}), bf16[8,256,256]{2,1,0:T(8,128)(2,1)S(1)}, u32[]{:S(2)}, u32[]{:S(2)}) async-start(bf16[8,256,256]{2,1,0:T(8,128)(2,1)} %bitcast.11), calls=%async_computation.3 | async-start | bytes 2097152 | tf_op jit(solution)/shard_map/all_to_all | solution.py:123
  152.1 5.6 %collective-permute-start.3 = (bf16[128,256]{1,0:T(8,128)(2,1)S(1)}, bf16[128,256]{1,0:T(8,128)(2,1)S(1)}, u32[]{:S(2)}, u32[]{:S(2)}) collective-permute-start(bf16[128,256]{1,0:T(8,128)(2,1)S(1)} %slice.33), channel_id=1, source_target_pairs={{0,1},{1,0},{2,3},{3,2},{4,5},{5,4},{6,7},{7,6},{8,9},{9,8},{10,11... | collective-permute-start | bytes 196616 | tf_op jit(solution)/shard_map/ppermute | solution.py:95
  179.3 5.4 %collective-permute-start.4 = (bf16[128,256]{1,0:T(8,128)(2,1)S(1)}, bf16[128,256]{1,0:T(8,128)(2,1)S(1)}, u32[]{:S(2)}, u32[]{:S(2)}) collective-permute-start(bf16[128,256]{1,0:T(8,128)(2,1)S(1)} %slice.35), channel_id=1, source_target_pairs={{0,1},{1,0},{2,3},{3,2},{4,5},{5,4},{6,7},{7,6},{8,9},{9,8},{10,11... | collective-permute-start | bytes 196616 | tf_op jit(solution)/shard_map/ppermute | solution.py:95

commit v2 on v1

v2 whole, which is shorter than its diff:
```python
import functools

import jax
import jax.numpy as jnp
from jax import lax
from jax.experimental import pallas as pl
from jax.experimental.pallas import tpu as pltpu
from jax.sharding import Mesh, PartitionSpec as P

GRP = 4
STEP_ROWS = 256
PAIR = [(0, 1), (1, 0)]
VMEM_BYTES = 40 * 1024 * 1024


def build_kernel(slots, meta_ref, own_ref, other_ref, out_ref, total):
    tile = own_ref.shape[1]
    cells_down, cells_across = total.shape[0], total.shape[1]

    def clear(s, carry):
        for t in range(cells_across):
            total[s, t] = jnp.zeros((tile, 2 * tile), jnp.float32)
        return carry

    lax.fori_loop(0, cells_down, clear, 0)
    for side, ref in enumerate((own_ref, other_ref)):
        count = meta_ref[side, 2 * slots]
        lanes = pl.ds(side * tile, tile)

        def group(index, carry, side=side, ref=ref, count=count, lanes=lanes):
            for step in range(GRP):
                k = index * GRP + step
                held = jnp.where(k < count, ref[k].astype(jnp.float32), 0.0)
                total[meta_ref[side, k], meta_ref[side, slots + k], :, lanes] += held
            return carry

        lax.fori_loop(0, (count + GRP - 1) // GRP, group, 0)

    def store(s, carry):
        rows = pl.ds(pl.multiple_of(s * tile, tile), tile)
        for t in range(cells_across):
            out_ref[rows, pl.ds(t * 2 * tile, 2 * tile)] = total[s, t].astype(out_ref.dtype)
        return carry

    lax.fori_loop(0, cells_down, store, 0)


def build(meta, own, other, slab_tiles, space_tiles):
    slots, tile = own.shape[0], own.shape[1]
    shape = (slab_tiles * tile, space_tiles * 2 * tile)
    return pl.pallas_call(
        functools.partial(build_kernel, slots),
        out_shape=jax.ShapeDtypeStruct(shape, jnp.bfloat16),
        in_specs=[
            pl.BlockSpec(memory_space=pltpu.SMEM),
            pl.BlockSpec(memory_space=pltpu.VMEM),
            pl.BlockSpec(memory_space=pltpu.VMEM),
        ],
        out_specs=pl.BlockSpec(memory_space=pltpu.VMEM),
        scratch_shapes=[
            pltpu.VMEM((slab_tiles, space_tiles, tile, 2 * tile), jnp.float32),
        ],
        compiler_params=pltpu.CompilerParams(vmem_limit_bytes=VMEM_BYTES),
        cost_estimate=pl.CostEstimate(
            flops=4 * slots * tile * tile,
            bytes_accessed=8 * shape[0] * shape[1],
            transcendentals=0,
        ),
    )(meta, own, other)


def multiply_kernel(cap, matrix_ref, field_ref, *refs):
    *pieces, out_ref, space = refs
    both = field_ref.shape[0]
    tile = both // 2

    @pl.when(pl.program_id(0) == 0)
    def _():
        space[pl.ds(0, both), :] = field_ref[...]
        fetched_tiles = space.shape[0] // both - 1
        if len(pieces) == 2:
            for side, piece in enumerate(pieces):
                for t in range(fetched_tiles):
                    space[pl.ds((t + 1) * both + side * tile, tile), :] = piece[pl.ds(t * tile, tile), :]
        else:
            per_tile = tile // cap
            for owner in range(fetched_tiles * per_tile):
                t, place = divmod(owner, per_tile)
                for side in range(2):
                    space[pl.ds((t + 1) * both + side * tile + place * cap, cap), :] = pieces[0][
                        pl.ds((2 * owner + side) * cap, cap), :
                    ]

    out_ref[...] = jnp.dot(
        matrix_ref[...], space[...], preferred_element_type=jnp.float32
    ).astype(out_ref.dtype)


def multiply(matrix, field, pieces, cap):
    height, depth = matrix.shape
    width = field.shape[1]
    held = [pl.BlockSpec(v.shape, lambda i: (0, 0)) for v in (field, *pieces)]
    return pl.pallas_call(
        functools.partial(multiply_kernel, cap),
        grid=(height // STEP_ROWS,),
        out_shape=jax.ShapeDtypeStruct((height, width), jnp.bfloat16),
        in_specs=[pl.BlockSpec((STEP_ROWS, depth), lambda i: (i, 0)), *held],
        out_specs=pl.BlockSpec((STEP_ROWS, width), lambda i: (i, 0)),
        scratch_shapes=[pltpu.VMEM((depth, width), jnp.bfloat16)],
        compiler_params=pltpu.CompilerParams(vmem_limit_bytes=VMEM_BYTES),
        cost_estimate=pl.CostEstimate(
            flops=2 * height * depth * width,
            bytes_accessed=2 * (height * depth + depth * width + height * width),
            transcendentals=0,
        ),
    )(matrix, field, *pieces)


def one_hot(wanted, extent):
    place = lax.broadcasted_iota(jnp.int32, (1, extent), 1)
    return (wanted.reshape(-1, 1) == place).astype(jnp.bfloat16)


def on_device(features, blocks, block_rows, block_cols, block_count, send_rows):
    held = blocks[0]
    slots, tile = held.shape[0], held.shape[1]
    rows, width = features.shape
    half = width // 2
    cap = send_rows.shape[2]
    owners = lax.axis_size("rows")
    slab_tiles = 2 * lax.axis_size("y")
    space_tiles = 1 + owners * cap // tile
    core = lax.axis_index("core")

    def swap(value):
        return lax.ppermute(value, "core", PAIR)

    def exchange(picked):
        got = lax.all_to_all(picked.reshape(owners, -1, half), "rows", 0, 0, tiled=True)
        return got.reshape(-1, half)

    def pick(chosen, field):
        return jnp.dot(chosen, field, preferred_element_type=jnp.bfloat16)

    low, high = features[:, :half], features[:, half:]
    mine = jnp.where(core == 0, low, high)
    theirs = swap(jnp.where(core == 0, high, low))
    own_field = jnp.concatenate([mine, theirs], 0)

    lists = send_rows[0].reshape(-1)
    numbers = jnp.concatenate([block_rows[0], block_cols[0], block_count[0], lists])
    numbers = jnp.pad(numbers, (0, -numbers.shape[0] % 128))
    both = jnp.stack([numbers, swap(numbers)])
    both_lists = both[:, 2 * slots + 1 : 2 * slots + 1 + lists.shape[0]]
    mixed = both_lists + jnp.array([[0], [rows]], jnp.int32)
    mixed = mixed.reshape(2, owners, cap).transpose(1, 0, 2)
    picker = one_hot(mixed, 2 * rows)

    meta = both[:, : 2 * slots + 1]
    is_row = lax.broadcasted_iota(jnp.int32, meta.shape, 1) < slots
    meta = jnp.where(is_row, meta ^ core, meta)
    other_held = swap(held)

    def in_one(operands):
        own_field, picker, both_lists, meta, held, other_held = operands
        fetched = exchange(pick(picker, own_field))
        matrix = build(meta, held, other_held, slab_tiles, space_tiles)
        return matrix, multiply(matrix, own_field, (fetched,), cap)

    def in_two(operands):
        own_field, picker, both_lists, meta, held, other_held = operands
        pieces = tuple(
            exchange(pick(one_hot(both_lists[side], rows), own_field[side * rows : (side + 1) * rows]))
            for side in range(2)
        )
        matrix = build(meta, held, other_held, slab_tiles, space_tiles)
        return matrix, multiply(matrix, own_field, pieces, cap)

    matrix, partial_value = lax.cond(
        core == 0, in_one, in_two, (own_field, picker, both_lists, meta, held, other_held)
    )

    def combine(partial_value):
        parts = lax.all_to_all(
            partial_value.reshape(-1, 2 * rows, half), "y", 0, 0, tiled=True
        )
        return jnp.sum(parts.astype(jnp.float32), 0).astype(jnp.bfloat16)

    first = combine(partial_value)
    fetched = exchange(pick(picker, first))
    second = combine(multiply(matrix, first, (fetched,), cap))
    others = swap(jnp.stack([first[rows:], second[rows:]])).reshape(2 * rows, half)

    def whole(kept, other):
        return jnp.concatenate(
            [jnp.where(core == 0, kept, other), jnp.where(core == 0, other, kept)], 1
        )

    return (whole(first[:rows], others[:rows]), whole(second[:rows], others[rows:]))


def solution(mesh):
    inner = Mesh(
        mesh.devices.reshape(mesh.shape["rows"], -1, 2), ("rows", "y", "core")
    )
    cols = ("y", "core")
    placed = (
        P(("rows", "y", "core"), None),
        P("rows", cols, None, None),
        P("rows", cols),
        P("rows", cols),
        P("rows", cols),
        P("rows", cols, None),
    )
    return jax.shard_map(
        on_device,
        mesh=inner,
        in_specs=placed,
        out_specs=(P(("rows", "y", "core"), None), P(("rows", "y", "core"), None)),
        check_vma=False,
    )
```

time: 186 us -> 170 us (0.914)
  Pallas kernels: 2.84 us -> 20.7 us
  blocking collectives: 41.1 us -> 27.6 us
  matrix products: 14.1 us -> 2.59 us
  waiting for transfers between devices: 73 us -> 62.5 us
  starting transfers between devices: 45.2 us -> 48.2 us
  local copies, waits for them, and re-layouts: 4.18 us -> 2.28 us
    pallas_call x1 -> x3, Pallas kernels: 2.84 us -> 20.7 us  [the longest x2 15.1 us: multiply(): pl.pallas_call(functools.partial(multiply_kernel, cap), grid=(height // S...]
    all_to_all x1, blocking collectives: 41.1 us -> 27.6 us  [exchange(): lax.all_to_all(picked.reshape(owners, -1, half), 'rows', 0, 0, tiled=True)]
    dot_general x4 -> x3, matrix products: 14.1 us -> 2.59 us  [pick(): return jnp.dot(chosen, field, preferred_element_type=jnp.bfloat16)]
    all_to_all x3 -> x4, starting transfers between devices: 19.4 us -> 29.6 us  [the longest x2 19.2 us: exchange(): lax.all_to_all(picked.reshape(owners, -1, half), 'rows', 0, 0, tiled=True)]
    all_to_all x3 -> x4, waiting for transfers between devices: 68.8 us -> 60.3 us  [the longest x2 34.6 us: combine(): lax.all_to_all(partial_value.reshape(-1, 2 * rows, half), 'y', 0, 0, tile...]
    ppermute x5 -> x4, starting transfers between devices: 25.9 us -> 18.7 us  [swap(): return lax.ppermute(value, 'core', PAIR)]
    ppermute x5 -> x4, waiting for transfers between devices: 4.17 us -> 2.2 us  [swap(): return lax.ppermute(value, 'core', PAIR)]
    unnamed x5, local copies, waits for them, and re-layouts: 3.71 us -> 1.79 us
  transfers between devices with their start and end apart: 8 -> 8, of which waited for: 7 -> 6; matrix products, arithmetic and copies ran while one was open for 1% -> 2% of each run, Pallas kernels for 2% -> 3%
where the time goes in v2:
time: 170 us; the launch traced here: 169 us
  waiting for transfers between devices  62.5 us (37%)
  starting transfers between devices  48.2 us (28%)
  blocking collectives  27.6 us (16%)
  Pallas kernels  20.7 us (12%)
  other arithmetic  3.96 us (2%)
  matrix products  2.59 us (2%)
  local copies, waits for them, and re-layouts  2.28 us (1%)
    all_to_all x2, waiting for transfers between devices, combine(): lax.all_to_all(partial_value.reshape(-1, 2 * rows, half), 'y', 0, 0, tile...  34.6 us
    all_to_all x1, blocking collectives, exchange(): lax.all_to_all(picked.reshape(owners, -1, half), 'rows', 0, 0, tiled=True)  27.6 us
    all_to_all x2, waiting for transfers between devices, exchange(): lax.all_to_all(picked.reshape(owners, -1, half), 'rows', 0, 0, tiled=True)  25.7 us
    all_to_all x2, starting transfers between devices, exchange(): lax.all_to_all(picked.reshape(owners, -1, half), 'rows', 0, 0, tiled=True)  19.2 us
    ppermute x4, starting transfers between devices, swap(): return lax.ppermute(value, 'core', PAIR)  18.7 us
    pallas_call x2, Pallas kernels, multiply(): pl.pallas_call(functools.partial(multiply_kernel, cap), grid=(height // S...  15.1 us
    all_to_all x2, starting transfers between devices, combine(): lax.all_to_all(partial_value.reshape(-1, 2 * rows, half), 'y', 0, 0, tile...  10.4 us
    pallas_call x1, Pallas kernels, build(): pl.pallas_call(functools.partial(build_kernel, slots), out_shape=jax.Shap...  5.6 us
  transfers between devices with their start and end apart: 8, of which 6 were waited for; matrix products, arithmetic and copies ran while one was open for 2% of the time, Pallas kernels for 3%

profile of v2, /device:TPU:1, one launch (start us, length us, event | category | flops | bytes accessed | tf_op | source)
XLA Modules:
  0.0 169.5 jit_solution(12231473217723762486)
XLA Ops:
  3.0 12.4 %collective-permute-start = (s32[896]{0:T(1024)S(1)}, s32[896]{0:T(1024)S(1)}, u32[]{:S(2)}, u32[]{:S(2)}) collective-permute-start(s32[896]{0:T(1024)S(1)} %pad.4), channel_id=1, source_target_pairs={{0,1},{1,0},{2,3},{3,2},{4,5},{5,4},{6,7},{7,6},{8,9},{9,8},{10,11... | collective-permute-start | bytes 10760 | tf_op jit(solution)/shard_map/ppermute | solution.py:136
  15.4 0.9 broadcast_select_fusion.4
  16.3 1.9 %collective-permute-start.2 = (bf16[128,256]{1,0:T(8,128)(2,1)S(1)}, bf16[128,256]{1,0:T(8,128)(2,1)S(1)}, u32[]{:S(2)}, u32[]{:S(2)}) collective-permute-start(bf16[128,256]{1,0:T(8,128)(2,1)S(1)} %get-tuple-element.52), channel_id=1, source_target_pairs={{0,1},{1,0},{2,3},{3,2},{4,5},{5,4},{6,7},{7,6},{8,9},{9,8},{10,11... | collective-permute-start | bytes 196616 | tf_op jit(solution)/shard_map/ppermute | solution.py:136
  18.2 2.4 %collective-permute-start.1 = (bf16[32,128,128]{2,1,0:T(8,128)(2,1)}, bf16[32,128,128]{2,1,0:T(8,128)(2,1)S(1)}, u32[]{:S(2)}, u32[]{:S(2)}) collective-permute-start(bf16[32,128,128]{2,1,0:T(8,128)(2,1)} %bitcast.43), channel_id=1, source_target_pairs={{0,1},{1,0},{2,3},{3,2},{4,5},{5,4},{6,7},{7,6},{8,9},{9,8},{10,11... | collective-permute-start | bytes 3145736 | tf_op jit(solution)/shard_map/ppermute | solution.py:136
  21.0 1.2 fusion.4
  22.2 0.9 collective-permute-done.1
  23.1 59.8 %conditional.1 = (bf16[2048,1792]{1,0:T(8,128)(2,1)}, bf16[2048,256]{1,0:T(8,128)(2,1)S(1)}) conditional(s32[]{:T(128)} %convert_element_type.6, (s32[2,65]{1,0:T(2,128)S(1)}, bf16[32,128,128]{2,1,0:T(8,128)(2,1)S(1)}, bf16[32,128,128]{2,1,0:T(8,128)(2,1)S(1)}, s32[2,768]{1,0:T(2,128)S(1)}, bf16[128,256]{1,0:T(8,128)(2,1)S(1)}, ...), branch_computations={%region_0.1_spmd, %region_1.2_spmd} | conditional | flops 2082471936 | bytes 42729520 | solution.py:179
  23.2 1.1 fusion.1
  24.2 9.0 %all-to-all-start.1 = ((bf16[48,16,256]{2,1,0:T(8,128)(2,1)}), bf16[48,16,256]{2,1,0:T(8,128)(2,1)S(1)}, u32[]{:S(2)}, u32[]{:S(2)}) async-start(bf16[48,16,256]{2,1,0:T(8,128)(2,1)} %bitcast.2), calls=%async_computation.1 | async-start | bytes 786432 | tf_op jit(solution)/shard_map/cond/branch_0_fun/all_to_all | solution.py:139
  33.2 1.1 fusion
  34.3 16.1 %all-to-all-done.1 = bf16[48,16,256]{2,1,0:T(8,128)(2,1)S(1)} async-done(((bf16[48,16,256]{2,1,0:T(8,128)(2,1)}), bf16[48,16,256]{2,1,0:T(8,128)(2,1)S(1)}, u32[]{:S(2)}, u32[]{:S(2)}) %all-to-all-start.1) | async-done | bytes 393248 | tf_op jit(solution)/shard_map/cond/branch_0_fun/all_to_all | solution.py:139
  50.4 10.2 %all-to-all-start = ((bf16[48,16,256]{2,1,0:T(8,128)(2,1)}), bf16[48,16,256]{2,1,0:T(8,128)(2,1)S(1)}, u32[]{:S(2)}, u32[]{:S(2)}) async-start(bf16[48,16,256]{2,1,0:T(8,128)(2,1)} %bitcast), calls=%async_computation | async-start | bytes 786432 | tf_op jit(solution)/shard_map/cond/branch_0_fun/all_to_all | solution.py:139
  60.6 5.6 %branch_0_fun.2.matrix_ref = bf16[2048,1792]{1,0:T(8,128)(2,1)} custom-call(s32[2,65]{1,0:T(2,128)S(1)} %get-tuple-element.24.meta_ref, bf16[32,128,128]{2,1,0:T(8,128)(2,1)S(1)} %get-tuple-element.25.own_ref, bf16[32,128,128]{2,1,0:T(8,128)(2,1)S(1)} %get-tuple-element.26.other_ref), custom_call_target="tpu_custom_call" | custom-call | flops 2097152 | bytes 29360128 | tf_op jit(solution)/shard_map/cond/branch_0_fun/pallas_call | solution.py:51
  66.2 9.6 %all-to-all-done = bf16[48,16,256]{2,1,0:T(8,128)(2,1)S(1)} async-done(((bf16[48,16,256]{2,1,0:T(8,128)(2,1)}), bf16[48,16,256]{2,1,0:T(8,128)(2,1)S(1)}, u32[]{:S(2)}, u32[]{:S(2)}) %all-to-all-start) | async-done | bytes 393248 | tf_op jit(solution)/shard_map/cond/branch_0_fun/all_to_all | solution.py:139
  75.8 7.1 %branch_0_fun.3 = bf16[2048,256]{1,0:T(8,128)(2,1)S(1)} custom-call(bf16[2048,1792]{1,0:T(8,128)(2,1)} %branch_0_fun.2.matrix_ref, bf16[256,256]{1,0:T(8,128)(2,1)S(1)} %get-tuple-element.27.field_ref, bf16[768,256]{1,0:T(8,128)(2,1)S(1)} %bitcast.42, bf16[768,256]{1,0:T(8,128)(2,1)S(1)} %bitcast.41), custom_call_target="tpu_custom_call" | custom-call | flops 1879048192 | bytes 9306112 | tf_op jit(solution)/shard_map/cond/branch_0_fun/pallas_call | solution.py:103
  82.9 1.0 copy-done.1
  83.9 6.8 %all-to-all-start.3 = ((bf16[8,256,256]{2,1,0:T(8,128)(2,1)}), bf16[8,256,256]{2,1,0:T(8,128)(2,1)S(1)}, u32[]{:S(2)}, u32[]{:S(2)}) async-start(bf16[8,256,256]{2,1,0:T(8,128)(2,1)} %bitcast.46), calls=%async_computation.3 | async-start | bytes 2097152 | tf_op jit(solution)/shard_map/all_to_all | solution.py:184
  90.9 17.7 %all-to-all-done.3 = bf16[8,256,256]{2,1,0:T(8,128)(2,1)S(1)} async-done(((bf16[8,256,256]{2,1,0:T(8,128)(2,1)}), bf16[8,256,256]{2,1,0:T(8,128)(2,1)S(1)}, u32[]{:S(2)}, u32[]{:S(2)}) %all-to-all-start.3) | async-done | bytes 1048608 | tf_op jit(solution)/shard_map/all_to_all | solution.py:184
  109.1 27.6 %all_to_all.27 = bf16[48,32,256]{2,1,0:T(8,128)(2,1)S(1)} all-to-all(bf16[48,32,256]{2,1,0:T(8,128)(2,1)S(1)} %fusion.5), channel_id=1, replica_groups=mesh['rows'=48,'y'=8,'core'=2] {'rows'}, dimensions={0} | all-to-all | bytes 1572864 | tf_op jit(solution)/shard_map/all_to_all | solution.py:139
  136.7 8.0 %shard_map.86 = bf16[2048,256]{1,0:T(8,128)(2,1)} custom-call(bf16[2048,1792]{1,0:T(8,128)(2,1)} %get-tuple-element.41.matrix_ref, bf16[256,256]{1,0:T(8,128)(2,1)S(1)} %reduce_sum.24.field_ref, bf16[1536,256]{1,0:T(8,128)(2,1)S(1)} %bitcast.40), custom_call_target="tpu_custom_call" | custom-call | flops 1879048192 | bytes 9306112 | tf_op jit(solution)/shard_map/pallas_call | solution.py:103
  144.8 3.6 %all-to-all-start.5 = ((bf16[8,256,256]{2,1,0:T(8,128)(2,1)}), bf16[8,256,256]{2,1,0:T(8,128)(2,1)S(1)}, u32[]{:S(2)}, u32[]{:S(2)}) async-start(bf16[8,256,256]{2,1,0:T(8,128)(2,1)} %bitcast.16), calls=%async_computation.5 | async-start | bytes 2097152 | tf_op jit(solution)/shard_map/all_to_all | solution.py:184
  148.3 17.0 %all-to-all-done.5 = bf16[8,256,256]{2,1,0:T(8,128)(2,1)S(1)} async-done(((bf16[8,256,256]{2,1,0:T(8,128)(2,1)}), bf16[8,256,256]{2,1,0:T(8,128)(2,1)S(1)}, u32[]{:S(2)}, u32[]{:S(2)}) %all-to-all-start.5) | async-done | bytes 1048608 | tf_op jit(solution)/shard_map/all_to_all | solution.py:184
  165.5 1.9 %collective-permute-start.3 = (bf16[2,128,256]{2,1,0:T(8,128)(2,1)S(1)}, bf16[2,128,256]{2,1,0:T(8,128)(2,1)S(1)}, u32[]{:S(2)}, u32[]{:S(2)}) collective-permute-start(bf16[2,128,256]{2,1,0:T(8,128)(2,1)S(1)} %pad_maximum_fusion.1), channel_id=1, source_target_pairs={{0,1},{1,0},{2,3},{3,2},{4,5},{5,4},{6,7},{7,6},{8,9},{9,8},{10,11... | collective-permute-start | bytes 393224 | tf_op jit(solution)/shard_map/ppermute | solution.py:136
  167.4 1.3 collective-permute-done.3
  (30 shorter events, 3.6 us)
Async XLA Ops:
  0.6 22.5 %copy-start = (bf16[1,32,128,128]{3,2,1,0:T(8,128)(2,1)S(1)}, bf16[1,32,128,128]{3,2,1,0:T(8,128)(2,1)}, u32[]{:S(2)}) copy-start(bf16[1,32,128,128]{3,2,1,0:T(8,128)(2,1)} %param.10) | copy-start | bytes 3145732
  3.0 17.7 %collective-permute-start = (s32[896]{0:T(1024)S(1)}, s32[896]{0:T(1024)S(1)}, u32[]{:S(2)}, u32[]{:S(2)}) collective-permute-start(s32[896]{0:T(1024)S(1)} %pad.4), channel_id=1, source_target_pairs={{0,1},{1,0},{2,3},{3,2},{4,5},{5,4},{6,7},{7,6},{8,9},{9,8},{10,11... | collective-permute-start | bytes 10760 | tf_op jit(solution)/shard_map/ppermute | solution.py:136
  16.3 5.9 %collective-permute-start.2 = (bf16[128,256]{1,0:T(8,128)(2,1)S(1)}, bf16[128,256]{1,0:T(8,128)(2,1)S(1)}, u32[]{:S(2)}, u32[]{:S(2)}) collective-permute-start(bf16[128,256]{1,0:T(8,128)(2,1)S(1)} %get-tuple-element.52), channel_id=1, source_target_pairs={{0,1},{1,0},{2,3},{3,2},{4,5},{5,4},{6,7},{7,6},{8,9},{9,8},{10,11... | collective-permute-start | bytes 196616 | tf_op jit(solution)/shard_map/ppermute | solution.py:136
  18.2 4.9 %collective-permute-start.1 = (bf16[32,128,128]{2,1,0:T(8,128)(2,1)}, bf16[32,128,128]{2,1,0:T(8,128)(2,1)S(1)}, u32[]{:S(2)}, u32[]{:S(2)}) collective-permute-start(bf16[32,128,128]{2,1,0:T(8,128)(2,1)} %bitcast.43), channel_id=1, source_target_pairs={{0,1},{1,0},{2,3},{3,2},{4,5},{5,4},{6,7},{7,6},{8,9},{9,8},{10,11... | collective-permute-start | bytes 3145736 | tf_op jit(solution)/shard_map/ppermute | solution.py:136
  24.2 26.2 %all-to-all-start.1 = ((bf16[48,16,256]{2,1,0:T(8,128)(2,1)}), bf16[48,16,256]{2,1,0:T(8,128)(2,1)S(1)}, u32[]{:S(2)}, u32[]{:S(2)}) async-start(bf16[48,16,256]{2,1,0:T(8,128)(2,1)} %bitcast.2), calls=%async_computation.1 | async-start | bytes 786432 | tf_op jit(solution)/shard_map/cond/branch_0_fun/all_to_all | solution.py:139
  50.4 25.4 %all-to-all-start = ((bf16[48,16,256]{2,1,0:T(8,128)(2,1)}), bf16[48,16,256]{2,1,0:T(8,128)(2,1)S(1)}, u32[]{:S(2)}, u32[]{:S(2)}) async-start(bf16[48,16,256]{2,1,0:T(8,128)(2,1)} %bitcast), calls=%async_computation | async-start | bytes 786432 | tf_op jit(solution)/shard_map/cond/branch_0_fun/all_to_all | solution.py:139
  82.9 1.0 copy-start.1
  83.9 24.6 %all-to-all-start.3 = ((bf16[8,256,256]{2,1,0:T(8,128)(2,1)}), bf16[8,256,256]{2,1,0:T(8,128)(2,1)S(1)}, u32[]{:S(2)}, u32[]{:S(2)}) async-start(bf16[8,256,256]{2,1,0:T(8,128)(2,1)} %bitcast.46), calls=%async_computation.3 | async-start | bytes 2097152 | tf_op jit(solution)/shard_map/all_to_all | solution.py:184
  144.8 20.5 %all-to-all-start.5 = ((bf16[8,256,256]{2,1,0:T(8,128)(2,1)}), bf16[8,256,256]{2,1,0:T(8,128)(2,1)S(1)}, u32[]{:S(2)}, u32[]{:S(2)}) async-start(bf16[8,256,256]{2,1,0:T(8,128)(2,1)} %bitcast.16), calls=%async_computation.5 | async-start | bytes 2097152 | tf_op jit(solution)/shard_map/all_to_all | solution.py:184
  165.5 3.2 %collective-permute-start.3 = (bf16[2,128,256]{2,1,0:T(8,128)(2,1)S(1)}, bf16[2,128,256]{2,1,0:T(8,128)(2,1)S(1)}, u32[]{:S(2)}, u32[]{:S(2)}) collective-permute-start(bf16[2,128,256]{2,1,0:T(8,128)(2,1)S(1)} %pad_maximum_fusion.1), channel_id=1, source_target_pairs={{0,1},{1,0},{2,3},{3,2},{4,5},{5,4},{6,7},{7,6},{8,9},{9,8},{10,11... | collective-permute-start | bytes 393224 | tf_op jit(solution)/shard_map/ppermute | solution.py:136

commit v3 on v1

v3 whole, which is shorter than its diff:
```python
import functools

import jax
import jax.numpy as jnp
from jax import lax
from jax.experimental import pallas as pl
from jax.experimental.pallas import tpu as pltpu
from jax.sharding import Mesh, PartitionSpec as P

GRP = 16
PAIR = [(0, 1), (1, 0)]
VMEM_BYTES = 24 * 1024 * 1024


def product_kernel(slots, cap, meta_ref, own_ref, other_ref, field_ref, *refs):
    *pieces, out_ref, total, space = refs
    tile = own_ref.shape[1]
    tiles = space.shape[0] // 2
    for side in range(2):
        space[side * tiles] = field_ref[pl.ds(side * tile, tile), :]
        for t in range(tiles - 1):
            if len(pieces) == 2:
                space[side * tiles + 1 + t] = pieces[side][pl.ds(t * tile, tile), :]
                continue
            for place in range(tile // cap):
                owner = t * (tile // cap) + place
                space[side * tiles + 1 + t, pl.ds(place * cap, cap), :] = pieces[0][
                    pl.ds((2 * owner + side) * cap, cap), :
                ]
    total[...] = jnp.zeros_like(total)
    for side, ref in enumerate((own_ref, other_ref)):
        count = meta_ref[side, 2 * slots]

        def group(index, carry, side=side, ref=ref, count=count):
            products = []
            for step in range(GRP):
                k = index * GRP + step
                held = jnp.where(k < count, ref[k], jnp.zeros((tile, tile), ref.dtype))
                source = space[side * tiles + meta_ref[side, slots + k]]
                product = jnp.dot(held, source, preferred_element_type=jnp.float32)
                products.append((meta_ref[side, k], product))
            for row, product in products:
                total[row] += product
            return carry

        lax.fori_loop(0, (count + GRP - 1) // GRP, group, 0)
    for row in range(total.shape[0]):
        out_ref[pl.ds(row * tile, tile), :] = total[row].astype(out_ref.dtype)


def product(meta, own, other, field, pieces, slab_tiles, cap):
    slots, tile = own.shape[0], own.shape[1]
    width = field.shape[1]
    tiles = 2 + sum(v.shape[0] for v in pieces) // tile
    anywhere = pl.BlockSpec(memory_space=pltpu.VMEM)
    return pl.pallas_call(
        functools.partial(product_kernel, slots, cap),
        out_shape=jax.ShapeDtypeStruct((slab_tiles * tile, width), jnp.bfloat16),
        in_specs=[pl.BlockSpec(memory_space=pltpu.SMEM)] + [anywhere] * (3 + len(pieces)),
        out_specs=anywhere,
        scratch_shapes=[
            pltpu.VMEM((slab_tiles, tile, width), jnp.float32),
            pltpu.VMEM((tiles, tile, width), jnp.bfloat16),
        ],
        compiler_params=pltpu.CompilerParams(vmem_limit_bytes=VMEM_BYTES),
        cost_estimate=pl.CostEstimate(
            flops=4 * slots * tile * tile * width,
            bytes_accessed=2 * (2 * slots * tile * tile + (tiles + slab_tiles) * tile * width),
            transcendentals=0,
        ),
    )(meta, own, other, field, *pieces)


def one_hot(wanted, extent):
    place = lax.broadcasted_iota(jnp.int32, (1, extent), 1)
    return (wanted.reshape(-1, 1) == place).astype(jnp.bfloat16)


def on_device(features, blocks, block_rows, block_cols, block_count, send_rows):
    held = blocks[0]
    slots, tile = held.shape[0], held.shape[1]
    rows, width = features.shape
    half = width // 2
    cap = send_rows.shape[2]
    owners = lax.axis_size("rows")
    slab_tiles = 2 * lax.axis_size("y")
    core = lax.axis_index("core")

    def swap(value):
        return lax.ppermute(value, "core", PAIR)

    def exchange(picked):
        got = lax.all_to_all(picked.reshape(owners, -1, half), "rows", 0, 0, tiled=True)
        return got.reshape(-1, half)

    def pick(chosen, field):
        return jnp.dot(chosen, field, preferred_element_type=jnp.bfloat16)

    low, high = features[:, :half], features[:, half:]
    mine = jnp.where(core == 0, low, high)
    theirs = swap(jnp.where(core == 0, high, low))
    own_field = jnp.concatenate([mine, theirs], 0)

    lists = send_rows[0].reshape(-1)
    numbers = jnp.concatenate([block_rows[0], block_cols[0], block_count[0], lists])
    numbers = jnp.pad(numbers, (0, -numbers.shape[0] % 128))
    both = jnp.stack([numbers, swap(numbers)])
    both_lists = both[:, 2 * slots + 1 : 2 * slots + 1 + lists.shape[0]]
    mixed = both_lists + jnp.array([[0], [rows]], jnp.int32)
    mixed = mixed.reshape(2, owners, cap).transpose(1, 0, 2).reshape(-1)

    meta = both[:, : 2 * slots + 1]
    is_row = lax.broadcasted_iota(jnp.int32, meta.shape, 1) < slots
    meta = jnp.where(is_row, meta ^ core, meta)
    other_held = swap(held)

    def multiply(field, pieces, meta, held, other_held):
        partial_value = product(meta, held, other_held, field, pieces, slab_tiles, cap)
        parts = lax.all_to_all(
            partial_value.reshape(-1, 2 * rows, half), "y", 0, 0, tiled=True
        )
        return jnp.sum(parts.astype(jnp.float32), 0).astype(jnp.bfloat16)

    def in_one(operands):
        own_field, mixed, both_lists, *tiles = operands
        fetched = exchange(pick(one_hot(mixed, 2 * rows), own_field))
        return multiply(own_field, (fetched,), *tiles)

    def in_two(operands):
        own_field, mixed, both_lists, *tiles = operands
        pieces = tuple(
            exchange(pick(one_hot(both_lists[side], rows), own_field[side * rows : (side + 1) * rows]))
            for side in range(2)
        )
        return multiply(own_field, pieces, *tiles)

    tiles = (meta, held, other_held)
    first = lax.optimization_barrier(
        lax.cond(core == 0, in_one, in_two, (own_field, mixed, both_lists, *tiles))
    )
    fetched = exchange(pick(one_hot(mixed, 2 * rows), first))
    second = multiply(first, (fetched,), *tiles)
    others = swap(jnp.stack([first[rows:], second[rows:]])).reshape(2 * rows, half)

    def whole(kept, other):
        return jnp.concatenate(
            [jnp.where(core == 0, kept, other), jnp.where(core == 0, other, kept)], 1
        )

    return (whole(first[:rows], others[:rows]), whole(second[:rows], others[rows:]))


def solution(mesh):
    inner = Mesh(
        mesh.devices.reshape(mesh.shape["rows"], -1, 2), ("rows", "y", "core")
    )
    cols = ("y", "core")
    placed = (
        P(("rows", "y", "core"), None),
        P("rows", cols, None, None),
        P("rows", cols),
        P("rows", cols),
        P("rows", cols),
        P("rows", cols, None),
    )
    return jax.shard_map(
        on_device,
        mesh=inner,
        in_specs=placed,
        out_specs=(P(("rows", "y", "core"), None), P(("rows", "y", "core"), None)),
        check_vma=False,
    )
```

time: 186 us -> 159 us (0.85)
  waiting for transfers between devices: 73 us -> 40 us
  blocking collectives: 41.1 us -> 73.5 us
  starting transfers between devices: 45.2 us -> 31.4 us
  matrix products: 14.1 us -> 1.81 us
  Pallas kernels: 2.84 us -> 5.32 us
  local copies, waits for them, and re-layouts: 4.18 us -> 2.28 us
    all_to_all x1 -> x3, blocking collectives: 41.1 us -> 73.5 us  [the longest x2 49.1 us: exchange(): lax.all_to_all(picked.reshape(owners, -1, half), 'rows', 0, 0, tiled=True)]
    all_to_all x3 -> x2, waiting for transfers between devices: 68.8 us -> 38 us  [the longest x1 20.5 us: exchange(): lax.all_to_all(picked.reshape(owners, -1, half), 'rows', 0, 0, tiled=True)]
    dot_general x4 -> x3, matrix products: 14.1 us -> 1.81 us  [pick(): return jnp.dot(chosen, field, preferred_element_type=jnp.bfloat16)]
    ppermute x5 -> x4, starting transfers between devices: 25.9 us -> 18.7 us  [swap(): return lax.ppermute(value, 'core', PAIR)]
    all_to_all x3 -> x2, starting transfers between devices: 19.4 us -> 12.7 us  [the longest x1 9.13 us: exchange(): lax.all_to_all(picked.reshape(owners, -1, half), 'rows', 0, 0, tiled=True)]
    pallas_call x1 -> x2, Pallas kernels: 2.84 us -> 5.32 us  [product(): pl.pallas_call(functools.partial(product_kernel, slots, cap), out_shape=j...]
    unnamed x5, local copies, waits for them, and re-layouts: 3.71 us -> 1.33 us
    ppermute x5 -> x4, waiting for transfers between devices: 4.17 us -> 2.09 us  [swap(): return lax.ppermute(value, 'core', PAIR)]
  transfers between devices with their start and end apart: 8 -> 6, of which waited for: 7 -> 4; matrix products, arithmetic and copies ran while one was open for 1% -> 2% of each run, Pallas kernels for 2% -> 0%
where the time goes in v3:
time: 159 us
  blocking collectives  73.5 us (46%)
  waiting for transfers between devices  40 us (25%)
  starting transfers between devices  31.4 us (20%)
  Pallas kernels  5.32 us (3%)
  other arithmetic  2.8 us (2%)
  local copies, waits for them, and re-layouts  2.28 us (1%)
  matrix products  1.81 us (1%)
    all_to_all x2, blocking collectives, exchange(): lax.all_to_all(picked.reshape(owners, -1, half), 'rows', 0, 0, tiled=True)  49.1 us
    all_to_all x1, blocking collectives, multiply(): lax.all_to_all(partial_value.reshape(-1, 2 * rows, half), 'y', 0, 0, tile...  24.4 us
    all_to_all x1, waiting for transfers between devices, exchange(): lax.all_to_all(picked.reshape(owners, -1, half), 'rows', 0, 0, tiled=True)  20.5 us
    ppermute x4, starting transfers between devices, swap(): return lax.ppermute(value, 'core', PAIR)  18.7 us
    all_to_all x1, waiting for transfers between devices, multiply(): lax.all_to_all(partial_value.reshape(-1, 2 * rows, half), 'y', 0, 0, tile...  17.5 us
    all_to_all x1, starting transfers between devices, exchange(): lax.all_to_all(picked.reshape(owners, -1, half), 'rows', 0, 0, tiled=True)  9.13 us
    pallas_call x2, Pallas kernels, product(): pl.pallas_call(functools.partial(product_kernel, slots, cap), out_shape=j...  5.32 us
    all_to_all x1, starting transfers between devices, multiply(): lax.all_to_all(partial_value.reshape(-1, 2 * rows, half), 'y', 0, 0, tile...  3.56 us
  transfers between devices with their start and end apart: 6, of which 4 were waited for; matrix products, arithmetic and copies ran while one was open for 2% of the time, Pallas kernels for 0%

profile of v3, /device:TPU:1, one launch (start us, length us, event | category | flops | bytes accessed | tf_op | source)
XLA Modules:
  0.0 158.6 jit_solution(5454250564473764209)
XLA Ops:
  0.6 12.4 %collective-permute-start.2 = (bf16[32,128,128]{2,1,0:T(8,128)(2,1)}, bf16[32,128,128]{2,1,0:T(8,128)(2,1)S(1)}, u32[]{:S(2)}, u32[]{:S(2)}) collective-permute-start(bf16[32,128,128]{2,1,0:T(8,128)(2,1)} %bitcast.43), channel_id=1, source_target_pairs={{0,1},{1,0},{2,3},{3,2},{4,5},{5,4},{6,7},{7,6},{8,9},{9,8},{10,11... | collective-permute-start | bytes 3145736 | tf_op jit(solution)/shard_map/ppermute | solution.py:90
  13.1 0.9 broadcast_select_fusion.4
  14.0 1.9 %collective-permute-start.1 = (bf16[128,256]{1,0:T(8,128)(2,1)S(1)}, bf16[128,256]{1,0:T(8,128)(2,1)S(1)}, u32[]{:S(2)}, u32[]{:S(2)}) collective-permute-start(bf16[128,256]{1,0:T(8,128)(2,1)S(1)} %get-tuple-element.57), channel_id=1, source_target_pairs={{0,1},{1,0},{2,3},{3,2},{4,5},{5,4},{6,7},{7,6},{8,9},{9,8},{10,11... | collective-permute-start | bytes 196616 | tf_op jit(solution)/shard_map/ppermute | solution.py:90
  15.9 0.8 copy.10
  17.4 0.8 pad_add_fusion
  18.2 2.4 %collective-permute-start = (s32[896]{0:T(1024)S(1)}, s32[896]{0:T(1024)S(1)}, u32[]{:S(2)}, u32[]{:S(2)}) collective-permute-start(s32[896]{0:T(1024)S(1)} %pad.4), channel_id=1, source_target_pairs={{0,1},{1,0},{2,3},{3,2},{4,5},{5,4},{6,7},{7,6},{8,9},{9,8},{10,11... | collective-permute-start | bytes 10760 | tf_op jit(solution)/shard_map/ppermute | solution.py:90
  20.6 0.8 collective-permute-done
  21.6 0.7 eq.70
  22.3 79.8 %conditional.1 = (bf16[8,256,256]{2,1,0:T(8,128)(2,1)S(1)}) conditional(s32[]{:T(128)} %convert_element_type.2, (s32[2,768]{1,0:T(2,128)S(1)}, bf16[128,256]{1,0:T(8,128)(2,1)S(1)}, bf16[128,256]{1,0:T(8,128)(2,1)S(1)}, s32[2,65]{1,0:T(2,128)S(1)}, bf16[32,128,128]{2,1,0:T(8,128)(2,1)}, /*index=5*/bf16[32,128,128]{2,1,0:T(8,128)(2,1)S(1)}, ...), branch_computations={%region_0.1_spmd, %region_1.2_spmd} | conditional | flops 738590720 | bytes 13256772 | solution.py:139
  22.4 1.1 fusion.2
  23.5 9.1 %all-to-all-start = ((bf16[48,16,256]{2,1,0:T(8,128)(2,1)}), bf16[48,16,256]{2,1,0:T(8,128)(2,1)S(1)}, u32[]{:S(2)}, u32[]{:S(2)}) async-start(bf16[48,16,256]{2,1,0:T(8,128)(2,1)} %bitcast), calls=%async_computation | async-start | bytes 786432 | tf_op jit(solution)/shard_map/cond/branch_0_fun/all_to_all | solution.py:93
  32.9 20.5 %all-to-all-done = bf16[48,16,256]{2,1,0:T(8,128)(2,1)S(1)} async-done(((bf16[48,16,256]{2,1,0:T(8,128)(2,1)}), bf16[48,16,256]{2,1,0:T(8,128)(2,1)S(1)}, u32[]{:S(2)}, u32[]{:S(2)}) %all-to-all-start) | async-done | bytes 393248 | tf_op jit(solution)/shard_map/cond/branch_0_fun/all_to_all | solution.py:93
  53.4 22.2 %all_to_all.30 = bf16[48,16,256]{2,1,0:T(8,128)(2,1)S(1)} all-to-all(bf16[48,16,256]{2,1,0:T(8,128)(2,1)S(1)} %bitcast.47), channel_id=1, replica_groups=mesh['rows'=48,'y'=8,'core'=2] {'rows'}, dimensions={0} | all-to-all | bytes 786432 | tf_op jit(solution)/shard_map/cond/branch_0_fun/all_to_all | solution.py:93
  75.6 2.2 %branch_0_fun.1 = bf16[2048,256]{1,0:T(8,128)(2,1)S(1)} custom-call(s32[2,65]{1,0:T(2,128)S(1)} %get-tuple-element.28.meta_ref, bf16[32,128,128]{2,1,0:T(8,128)(2,1)S(1)} %copy-done.1, bf16[32,128,128]{2,1,0:T(8,128)(2,1)S(1)} %get-tuple-element.30.other_ref, bf16[256,256]{1,0:T(8,128)(2,1)S(1)} %get-tuple-element.31.field_ref, ...), custom_call_target="tpu_custom_call" | custom-call | flops 536870912 | bytes 4063232 | tf_op jit(solution)/shard_map/cond/branch_0_fun/pallas_call | solution.py:56
  77.8 24.4 %all_to_all.31 = bf16[8,256,256]{2,1,0:T(8,128)(2,1)S(1)} all-to-all(bf16[8,256,256]{2,1,0:T(8,128)(2,1)S(1)} %bitcast.37), channel_id=1, replica_groups=mesh['rows'=48,'y'=8,'core'=2] {'y'}, dimensions={0} | all-to-all | bytes 2097152 | tf_op jit(solution)/shard_map/cond/branch_0_fun/all_to_all | solution.py:119
  102.3 0.5 copy-done.3
  102.8 0.4 fusion.6
  103.3 26.9 %all_to_all.34 = bf16[48,32,256]{2,1,0:T(8,128)(2,1)S(1)} all-to-all(bf16[48,32,256]{2,1,0:T(8,128)(2,1)S(1)} %bitcast.49), channel_id=1, replica_groups=mesh['rows'=48,'y'=8,'core'=2] {'rows'}, dimensions={0} | all-to-all | bytes 1572864 | tf_op jit(solution)/shard_map/all_to_all | solution.py:93
  130.2 3.1 %shard_map.86 = bf16[2048,256]{1,0:T(8,128)(2,1)} custom-call(s32[2,65]{1,0:T(2,128)S(1)} %xor_select_fusion.meta_ref, bf16[32,128,128]{2,1,0:T(8,128)(2,1)S(1)} %bitcast.46, bf16[32,128,128]{2,1,0:T(8,128)(2,1)S(1)} %collective-permute-done.2.other_ref, bf16[256,256]{1,0:T(8,128)(2,1)S(1)} %reduce_sum.31.field_ref, bf16[1536,256]{1,0:T(8,128)(2,1)S(1)} %bitcast.39), custom_call_target="tpu_custom_call" | custom-call | flops 536870912 | bytes 4063232 | tf_op jit(solution)/shard_map/pallas_call | solution.py:56
  133.3 3.6 %all-to-all-start.6 = ((bf16[8,256,256]{2,1,0:T(8,128)(2,1)}), bf16[8,256,256]{2,1,0:T(8,128)(2,1)S(1)}, u32[]{:S(2)}, u32[]{:S(2)}) async-start(bf16[8,256,256]{2,1,0:T(8,128)(2,1)} %bitcast.16), calls=%async_computation.6 | async-start | bytes 2097152 | tf_op jit(solution)/shard_map/all_to_all | solution.py:119
  136.9 17.5 %all-to-all-done.6 = bf16[8,256,256]{2,1,0:T(8,128)(2,1)S(1)} async-done(((bf16[8,256,256]{2,1,0:T(8,128)(2,1)}), bf16[8,256,256]{2,1,0:T(8,128)(2,1)S(1)}, u32[]{:S(2)}, u32[]{:S(2)}) %all-to-all-start.6) | async-done | bytes 1048608 | tf_op jit(solution)/shard_map/all_to_all | solution.py:119
  154.6 1.9 %collective-permute-start.3 = (bf16[2,128,256]{2,1,0:T(8,128)(2,1)S(1)}, bf16[2,128,256]{2,1,0:T(8,128)(2,1)S(1)}, u32[]{:S(2)}, u32[]{:S(2)}) collective-permute-start(bf16[2,128,256]{2,1,0:T(8,128)(2,1)S(1)} %pad_maximum_fusion.1), channel_id=1, source_target_pairs={{0,1},{1,0},{2,3},{3,2},{4,5},{5,4},{6,7},{7,6},{8,9},{9,8},{10,11... | collective-permute-start | bytes 393224 | tf_op jit(solution)/shard_map/ppermute | solution.py:90
  156.5 1.3 collective-permute-done.3
  157.8 0.7 pad_maximum_fusion.2
  (26 shorter events, 1.0 us)
Async XLA Ops:
  0.6 21.7 %collective-permute-start.2 = (bf16[32,128,128]{2,1,0:T(8,128)(2,1)}, bf16[32,128,128]{2,1,0:T(8,128)(2,1)S(1)}, u32[]{:S(2)}, u32[]{:S(2)}) collective-permute-start(bf16[32,128,128]{2,1,0:T(8,128)(2,1)} %bitcast.43), channel_id=1, source_target_pairs={{0,1},{1,0},{2,3},{3,2},{4,5},{5,4},{6,7},{7,6},{8,9},{9,8},{10,11... | collective-permute-start | bytes 3145736 | tf_op jit(solution)/shard_map/ppermute | solution.py:90
  14.0 8.4 %collective-permute-start.1 = (bf16[128,256]{1,0:T(8,128)(2,1)S(1)}, bf16[128,256]{1,0:T(8,128)(2,1)S(1)}, u32[]{:S(2)}, u32[]{:S(2)}) collective-permute-start(bf16[128,256]{1,0:T(8,128)(2,1)S(1)} %get-tuple-element.57), channel_id=1, source_target_pairs={{0,1},{1,0},{2,3},{3,2},{4,5},{5,4},{6,7},{7,6},{8,9},{9,8},{10,11... | collective-permute-start | bytes 196616 | tf_op jit(solution)/shard_map/ppermute | solution.py:90
  18.2 3.2 %collective-permute-start = (s32[896]{0:T(1024)S(1)}, s32[896]{0:T(1024)S(1)}, u32[]{:S(2)}, u32[]{:S(2)}) collective-permute-start(s32[896]{0:T(1024)S(1)} %pad.4), channel_id=1, source_target_pairs={{0,1},{1,0},{2,3},{3,2},{4,5},{5,4},{6,7},{7,6},{8,9},{9,8},{10,11... | collective-permute-start | bytes 10760 | tf_op jit(solution)/shard_map/ppermute | solution.py:90
  23.5 52.1 %copy-start.1 = (bf16[32,128,128]{2,1,0:T(8,128)(2,1)S(1)}, bf16[32,128,128]{2,1,0:T(8,128)(2,1)}, u32[]{:S(2)}) copy-start(bf16[32,128,128]{2,1,0:T(8,128)(2,1)} %get-tuple-element.29.own_ref) | copy-start | bytes 3145732 | tf_op jit(solution)/shard_map/cond
  23.5 30.0 %all-to-all-start = ((bf16[48,16,256]{2,1,0:T(8,128)(2,1)}), bf16[48,16,256]{2,1,0:T(8,128)(2,1)S(1)}, u32[]{:S(2)}, u32[]{:S(2)}) async-start(bf16[48,16,256]{2,1,0:T(8,128)(2,1)} %bitcast), calls=%async_computation | async-start | bytes 786432 | tf_op jit(solution)/shard_map/cond/branch_0_fun/all_to_all | solution.py:93
  102.1 0.7 copy-start.3
  102.8 27.4 %copy-start = (bf16[1,32,128,128]{3,2,1,0:T(8,128)(2,1)S(1)}, bf16[1,32,128,128]{3,2,1,0:T(8,128)(2,1)}, u32[]{:S(2)}) copy-start(bf16[1,32,128,128]{3,2,1,0:T(8,128)(2,1)} %param.10) | copy-start | bytes 3145732
  133.3 21.0 %all-to-all-start.6 = ((bf16[8,256,256]{2,1,0:T(8,128)(2,1)}), bf16[8,256,256]{2,1,0:T(8,128)(2,1)S(1)}, u32[]{:S(2)}, u32[]{:S(2)}) async-start(bf16[8,256,256]{2,1,0:T(8,128)(2,1)} %bitcast.16), calls=%async_computation.6 | async-start | bytes 2097152 | tf_op jit(solution)/shard_map/all_to_all | solution.py:119
  154.6 3.2 %collective-permute-start.3 = (bf16[2,128,256]{2,1,0:T(8,128)(2,1)S(1)}, bf16[2,128,256]{2,1,0:T(8,128)(2,1)S(1)}, u32[]{:S(2)}, u32[]{:S(2)}) collective-permute-start(bf16[2,128,256]{2,1,0:T(8,128)(2,1)S(1)} %pad_maximum_fusion.1), channel_id=1, source_target_pairs={{0,1},{1,0},{2,3},{3,2},{4,5},{5,4},{6,7},{7,6},{8,9},{9,8},{10,11... | collective-permute-start | bytes 393224 | tf_op jit(solution)/shard_map/ppermute | solution.py:90

commit v4 on v3

--- a/solution.py
+++ b/solution.py
@@ -12,12 +12,16 @@
 VMEM_BYTES = 24 * 1024 * 1024
 
 
-def product_kernel(slots, cap, meta_ref, own_ref, other_ref, field_ref, *refs):
-    *pieces, out_ref, total, space = refs
+def product_kernel(slots, cap, fields, meta_ref, own_ref, other_ref, *refs):
+    field, pieces = refs[:fields], refs[fields:-3]
+    out_ref, total, space = refs[-3:]
     tile = own_ref.shape[1]
     tiles = space.shape[0] // 2
     for side in range(2):
-        space[side * tiles] = field_ref[pl.ds(side * tile, tile), :]
+        if fields == 2:
+            space[side * tiles] = field[side][...]
+        else:
+            space[side * tiles] = field[0][pl.ds(side * tile, tile), :]
         for t in range(tiles - 1):
             if len(pieces) == 2:
                 space[side * tiles + 1 + t] = pieces[side][pl.ds(t * tile, tile), :]
@@ -50,13 +54,13 @@
 
 def product(meta, own, other, field, pieces, slab_tiles, cap):
     slots, tile = own.shape[0], own.shape[1]
-    width = field.shape[1]
+    width = field[0].shape[1]
     tiles = 2 + sum(v.shape[0] for v in pieces) // tile
     anywhere = pl.BlockSpec(memory_space=pltpu.VMEM)
     return pl.pallas_call(
-        functools.partial(product_kernel, slots, cap),
+        functools.partial(product_kernel, slots, cap, len(field)),
         out_shape=jax.ShapeDtypeStruct((slab_tiles * tile, width), jnp.bfloat16),
-        in_specs=[pl.BlockSpec(memory_space=pltpu.SMEM)] + [anywhere] * (3 + len(pieces)),
+        in_specs=[pl.BlockSpec(memory_space=pltpu.SMEM)] + [anywhere] * (2 + len(field) + len(pieces)),
         out_specs=anywhere,
         scratch_shapes=[
             pltpu.VMEM((slab_tiles, tile, width), jnp.float32),
@@ -68,7 +72,7 @@
             bytes_accessed=2 * (2 * slots * tile * tile + (tiles + slab_tiles) * tile * width),
             transcendentals=0,
         ),
-    )(meta, own, other, field, *pieces)
+    )(meta, own, other, *field, *pieces)
 
 
 def one_hot(wanted, extent):
@@ -97,22 +101,25 @@
         return jnp.dot(chosen, field, preferred_element_type=jnp.bfloat16)
 
     low, high = features[:, :half], features[:, half:]
-    mine = jnp.where(core == 0, low, high)
-    theirs = swap(jnp.where(core == 0, high, low))
-    own_field = jnp.concatenate([mine, theirs], 0)
+    mine, theirs = jnp.where(core == 0, low, high), jnp.where(core == 0, high, low)
+    lists = send_rows[0].reshape(-1)
+    every_row = jnp.arange(rows, dtype=jnp.int32)
+    numbers = jnp.concatenate([block_rows, block_cols, block_count], 1)
+    numbers = jnp.pad(numbers, ((0, cap - 1), (0, half - owners - numbers.shape[1])))
+    numbers = jnp.concatenate([send_rows[0].T, numbers], 1)
+    sent = pick(one_hot(jnp.concatenate([lists, every_row]), rows), theirs)
+    given = swap(jnp.concatenate([sent, numbers.astype(jnp.bfloat16)], 0))
+    picked = pick(one_hot(lists, rows), mine)
+    other_held = swap(held)
+    ends = lists.shape[0], lists.shape[0] + rows
 
-    lists = send_rows[0].reshape(-1)
-    numbers = jnp.concatenate([block_rows[0], block_cols[0], block_count[0], lists])
-    numbers = jnp.pad(numbers, (0, -numbers.shape[0] % 128))
-    both = jnp.stack([numbers, swap(numbers)])
-    both_lists = both[:, 2 * slots + 1 : 2 * slots + 1 + lists.shape[0]]
-    mixed = both_lists + jnp.array([[0], [rows]], jnp.int32)
-    mixed = mixed.reshape(2, owners, cap).transpose(1, 0, 2).reshape(-1)
-
-    meta = both[:, : 2 * slots + 1]
-    is_row = lax.broadcasted_iota(jnp.int32, meta.shape, 1) < slots
-    meta = jnp.where(is_row, meta ^ core, meta)
-    other_held = swap(held)
+    def places(given, numbers):
+        both = jnp.stack([numbers, given[ends[1] :].astype(jnp.int32)])
+        meta = both[:, 0, owners : owners + 2 * slots + 1]
+        is_row = lax.broadcasted_iota(jnp.int32, meta.shape, 1) < slots
+        meta = jnp.where(is_row, meta ^ core, meta)
+        wanted = both[:, :, :owners] + jnp.array([[[0]], [[rows]]], jnp.int32)
+        return meta, wanted.transpose(2, 0, 1).reshape(-1)
 
     def multiply(field, pieces, meta, held, other_held):
         partial_value = product(meta, held, other_held, field, pieces, slab_tiles, cap)
@@ -122,24 +129,23 @@
         return jnp.sum(parts.astype(jnp.float32), 0).astype(jnp.bfloat16)
 
     def in_one(operands):
-        own_field, mixed, both_lists, *tiles = operands
-        fetched = exchange(pick(one_hot(mixed, 2 * rows), own_field))
-        return multiply(own_field, (fetched,), *tiles)
+        mine, picked, given, numbers, *tiles = operands
+        meta, wanted = places(given, numbers)
+        mixed = [v.reshape(owners, cap, half) for v in (picked, given[: ends[0]])]
+        fetched = exchange(jnp.concatenate(mixed, 1))
+        return multiply((mine, given[ends[0] : ends[1]]), (fetched,), meta, *tiles), meta, wanted
 
     def in_two(operands):
-        own_field, mixed, both_lists, *tiles = operands
-        pieces = tuple(
-            exchange(pick(one_hot(both_lists[side], rows), own_field[side * rows : (side + 1) * rows]))
-            for side in range(2)
-        )
-        return multiply(own_field, pieces, *tiles)
+        mine, picked, given, numbers, *tiles = operands
+        meta, wanted = places(given, numbers)
+        pieces = exchange(picked), exchange(given[: ends[0]])
+        return multiply((mine, given[ends[0] : ends[1]]), pieces, meta, *tiles), meta, wanted
 
-    tiles = (meta, held, other_held)
-    first = lax.optimization_barrier(
-        lax.cond(core == 0, in_one, in_two, (own_field, mixed, both_lists, *tiles))
+    first, meta, wanted = lax.optimization_barrier(
+        lax.cond(core == 0, in_one, in_two, (mine, picked, given, numbers, held, other_held))
     )
-    fetched = exchange(pick(one_hot(mixed, 2 * rows), first))
-    second = multiply(first, (fetched,), *tiles)
+    fetched = exchange(pick(one_hot(wanted, 2 * rows), first))
+    second = multiply((first,), (fetched,), meta, held, other_held)
     others = swap(jnp.stack([first[rows:], second[rows:]])).reshape(2 * rows, half)
 
     def whole(kept, other):

time: 159 us -> 159 us (level)
  blocking collectives: 73.5 us -> 27.7 us
  waiting for transfers between devices: 40 us -> 67.1 us
  starting transfers between devices: 31.4 us -> 46.8 us
    all_to_all x1 -> x0, blocking collectives: 24.4 us -> none  [multiply(): lax.all_to_all(partial_value.reshape(-1, 2 * rows, half), 'y', 0, 0, tile...]
    all_to_all x2 -> x1, blocking collectives: 49.1 us -> 27.7 us  [exchange(): lax.all_to_all(picked.reshape(owners, -1, half), 'rows', 0, 0, tiled=True)]
    all_to_all x1 -> x2, waiting for transfers between devices: 17.5 us -> 34.6 us  [multiply(): lax.all_to_all(partial_value.reshape(-1, 2 * rows, half), 'y', 0, 0, tile...]
    all_to_all x1 -> x2, starting transfers between devices: 9.13 us -> 20 us  [exchange(): lax.all_to_all(picked.reshape(owners, -1, half), 'rows', 0, 0, tiled=True)]
    all_to_all x1 -> x2, waiting for transfers between devices: 20.5 us -> 30.5 us  [exchange(): lax.all_to_all(picked.reshape(owners, -1, half), 'rows', 0, 0, tiled=True)]
    all_to_all x1 -> x2, starting transfers between devices: 3.56 us -> 10.4 us  [multiply(): lax.all_to_all(partial_value.reshape(-1, 2 * rows, half), 'y', 0, 0, tile...]
    ppermute x4 -> x3, starting transfers between devices: 18.7 us -> 16.4 us  [swap(): return lax.ppermute(value, 'core', PAIR)]
  transfers between devices with their start and end apart: 6 -> 7, of which waited for: 4 -> 6; matrix products, arithmetic and copies ran while one was open for 2% -> 4% of each run, Pallas kernels for 0% -> 0%
where the time goes in v4:
time: 159 us; the launch traced here: 158 us
  waiting for transfers between devices  67.1 us (42%)
  starting transfers between devices  46.8 us (29%)
  blocking collectives  27.7 us (17%)
  Pallas kernels  6.4 us (4%)
  other arithmetic  4.01 us (3%)
  matrix products  2.8 us (2%)
  local copies, waits for them, and re-layouts  1.91 us (1%)
    all_to_all x2, waiting for transfers between devices, multiply(): lax.all_to_all(partial_value.reshape(-1, 2 * rows, half), 'y', 0, 0, tile...  34.6 us
    all_to_all x2, waiting for transfers between devices, exchange(): lax.all_to_all(picked.reshape(owners, -1, half), 'rows', 0, 0, tiled=True)  30.5 us
    all_to_all x1, blocking collectives, exchange(): lax.all_to_all(picked.reshape(owners, -1, half), 'rows', 0, 0, tiled=True)  27.7 us
    all_to_all x2, starting transfers between devices, exchange(): lax.all_to_all(picked.reshape(owners, -1, half), 'rows', 0, 0, tiled=True)  20 us
    ppermute x3, starting transfers between devices, swap(): return lax.ppermute(value, 'core', PAIR)  16.4 us
    all_to_all x2, starting transfers between devices, multiply(): lax.all_to_all(partial_value.reshape(-1, 2 * rows, half), 'y', 0, 0, tile...  10.4 us
    pallas_call x2, Pallas kernels, product(): pl.pallas_call(functools.partial(product_kernel, slots, cap, len(field)),...  6.4 us
  transfers between devices with their start and end apart: 7, of which 6 were waited for; matrix products, arithmetic and copies ran while one was open for 4% of the time, Pallas kernels for 0%

profile of v4, /device:TPU:1, one launch (start us, length us, event | category | flops | bytes accessed | tf_op | source)
XLA Modules:
  0.0 158.3 jit_solution(15663371162095633785)
XLA Ops:
  0.6 12.6 %collective-permute-start.1 = (bf16[32,128,128]{2,1,0:T(8,128)(2,1)}, bf16[32,128,128]{2,1,0:T(8,128)(2,1)S(1)}, u32[]{:S(2)}, u32[]{:S(2)}) collective-permute-start(bf16[32,128,128]{2,1,0:T(8,128)(2,1)} %bitcast.52), channel_id=1, source_target_pairs={{0,1},{1,0},{2,3},{3,2},{4,5},{5,4},{6,7},{7,6},{8,9},{9,8},{10,11... | collective-permute-start | bytes 3145736 | tf_op jit(solution)/shard_map/ppermute | solution.py:94
  13.9 0.8 copy.12
  14.7 0.8 pad_add_fusion.4
  15.5 0.8 fusion.14
  16.3 1.3 fusion.6
  17.6 1.9 %collective-permute-start = (bf16[912,256]{1,0:T(8,128)(2,1)S(1)}, bf16[912,256]{1,0:T(8,128)(2,1)S(1)}, u32[]{:S(2)}, u32[]{:S(2)}) collective-permute-start(bf16[912,256]{1,0:T(8,128)(2,1)S(1)} %pad_maximum_fusion.1), channel_id=1, source_target_pairs={{0,1},{1,0},{2,3},{3,2},{4,5},{5,4},{6,7},{7,6},{8,9},{9,8},{10,11... | collective-permute-start | bytes 1400840 | tf_op jit(solution)/shard_map/ppermute | solution.py:94
  19.6 1.1 fusion.7
  21.3 80.9 %conditional.1 = (bf16[256,256]{1,0:T(8,128)(2,1)S(1)}, s32[2,65]{1,0:T(2,128)S(1)}, s32[1536]{0:T(1024)S(1)}) conditional(s32[]{:T(128)} %convert_element_type.4, (s32[16,256]{1,0:T(8,128)S(1)}, bf16[912,256]{1,0:T(8,128)(2,1)S(1)}, s32[]{:T(128)}, bf16[768,256]{1,0:T(8,128)(2,1)}, bf16[32,128,128]{2,1,0:T(8,128)(2,1)S(1)}, ...), branch_computations={%region_0.2_spmd, %region_2.4_spmd} | conditional | flops 538910144 | bytes 13429608 | solution.py:145
  21.3 9.0 %all-to-all-start = ((bf16[48,16,256]{2,1,0:T(8,128)(2,1)}), bf16[48,16,256]{2,1,0:T(8,128)(2,1)S(1)}, u32[]{:S(2)}, u32[]{:S(2)}) async-start(bf16[48,16,256]{2,1,0:T(8,128)(2,1)} %bitcast.1), calls=%async_computation | async-start | bytes 786432 | tf_op jit(solution)/shard_map/cond/branch_0_fun/all_to_all | solution.py:97
  30.4 0.8 slice.43
  31.1 15.5 %all-to-all-done = bf16[48,16,256]{2,1,0:T(8,128)(2,1)S(1)} async-done(((bf16[48,16,256]{2,1,0:T(8,128)(2,1)}), bf16[48,16,256]{2,1,0:T(8,128)(2,1)S(1)}, u32[]{:S(2)}, u32[]{:S(2)}) %all-to-all-start) | async-done | bytes 393248 | tf_op jit(solution)/shard_map/cond/branch_0_fun/all_to_all | solution.py:97
  46.7 11.0 %all-to-all-start.1 = ((bf16[48,16,256]{2,1,0:T(8,128)(2,1)}), bf16[48,16,256]{2,1,0:T(8,128)(2,1)S(1)}, u32[]{:S(2)}, u32[]{:S(2)}) async-start(bf16[48,16,256]{2,1,0:T(8,128)(2,1)} %bitcast.56), calls=%async_computation.1 | async-start | bytes 786432 | tf_op jit(solution)/shard_map/cond/branch_0_fun/all_to_all | solution.py:97
  57.9 15.0 %all-to-all-done.1 = bf16[48,16,256]{2,1,0:T(8,128)(2,1)S(1)} async-done(((bf16[48,16,256]{2,1,0:T(8,128)(2,1)}), bf16[48,16,256]{2,1,0:T(8,128)(2,1)S(1)}, u32[]{:S(2)}, u32[]{:S(2)}) %all-to-all-start.1) | async-done | bytes 393248 | tf_op jit(solution)/shard_map/cond/branch_0_fun/all_to_all | solution.py:97
  72.9 3.2 %branch_0_fun.1 = bf16[2048,256]{1,0:T(8,128)(2,1)} custom-call(s32[2,65]{1,0:T(2,128)S(1)} %xor_select_fusion.meta_ref, bf16[32,128,128]{2,1,0:T(8,128)(2,1)S(1)} %get-tuple-element.35.own_ref, bf16[32,128,128]{2,1,0:T(8,128)(2,1)S(1)} %get-tuple-element.36.other_ref, bf16[128,256]{1,0:T(8,128)(2,1)S(1)} %get-tuple-element.37.refs_0_, ...), custom_call_target="tpu_custom_call" | custom-call | flops 536870912 | bytes 4063232 | tf_op jit(solution)/shard_map/cond/branch_0_fun/pallas_call | solution.py:60
  76.1 6.8 %all-to-all-start.2 = ((bf16[8,256,256]{2,1,0:T(8,128)(2,1)}), bf16[8,256,256]{2,1,0:T(8,128)(2,1)}, u32[]{:S(2)}, u32[]{:S(2)}) async-start(bf16[8,256,256]{2,1,0:T(8,128)(2,1)} %bitcast.5), calls=%async_computation.2 | async-start | bytes 2097152 | tf_op jit(solution)/shard_map/cond/branch_0_fun/all_to_all | solution.py:126
  83.2 17.6 %all-to-all-done.2 = bf16[8,256,256]{2,1,0:T(8,128)(2,1)} async-done(((bf16[8,256,256]{2,1,0:T(8,128)(2,1)}), bf16[8,256,256]{2,1,0:T(8,128)(2,1)}, u32[]{:S(2)}, u32[]{:S(2)}) %all-to-all-start.2) | async-done | bytes 1048608 | tf_op jit(solution)/shard_map/cond/branch_0_fun/all_to_all | solution.py:126
  100.8 1.4 reduce_sum.33
  102.6 27.7 %all_to_all.30 = bf16[48,32,256]{2,1,0:T(8,128)(2,1)S(1)} all-to-all(bf16[48,32,256]{2,1,0:T(8,128)(2,1)S(1)} %bitcast.58), channel_id=1, replica_groups=mesh['rows'=48,'y'=8,'core'=2] {'rows'}, dimensions={0} | all-to-all | bytes 1572864 | tf_op jit(solution)/shard_map/all_to_all | solution.py:97
  130.3 3.2 %shard_map.95 = bf16[2048,256]{1,0:T(8,128)(2,1)} custom-call(s32[2,65]{1,0:T(2,128)S(1)} %get-tuple-element.54.meta_ref, bf16[32,128,128]{2,1,0:T(8,128)(2,1)S(1)} %bitcast.55, bf16[32,128,128]{2,1,0:T(8,128)(2,1)S(1)} %collective-permute-done.1.other_ref, bf16[256,256]{1,0:T(8,128)(2,1)S(1)} %get-tuple-element.53.refs_0_, bf16[1536,256]{1,0:T(8,128)(2,1)S(1)} %bitcast.49), custom_call_target="tpu_custom_call" | custom-call | flops 536870912 | bytes 4063232 | tf_op jit(solution)/shard_map/pallas_call | solution.py:60
  133.5 3.6 %all-to-all-start.6 = ((bf16[8,256,256]{2,1,0:T(8,128)(2,1)}), bf16[8,256,256]{2,1,0:T(8,128)(2,1)S(1)}, u32[]{:S(2)}, u32[]{:S(2)}) async-start(bf16[8,256,256]{2,1,0:T(8,128)(2,1)} %bitcast.21), calls=%async_computation.6 | async-start | bytes 2097152 | tf_op jit(solution)/shard_map/all_to_all | solution.py:126
  137.1 17.0 %all-to-all-done.6 = bf16[8,256,256]{2,1,0:T(8,128)(2,1)S(1)} async-done(((bf16[8,256,256]{2,1,0:T(8,128)(2,1)}), bf16[8,256,256]{2,1,0:T(8,128)(2,1)S(1)}, u32[]{:S(2)}, u32[]{:S(2)}) %all-to-all-start.6) | async-done | bytes 1048608 | tf_op jit(solution)/shard_map/all_to_all | solution.py:126
  154.3 1.9 %collective-permute-start.2 = (bf16[2,128,256]{2,1,0:T(8,128)(2,1)S(1)}, bf16[2,128,256]{2,1,0:T(8,128)(2,1)S(1)}, u32[]{:S(2)}, u32[]{:S(2)}) collective-permute-start(bf16[2,128,256]{2,1,0:T(8,128)(2,1)S(1)} %pad_maximum_fusion.2), channel_id=1, source_target_pairs={{0,1},{1,0},{2,3},{3,2},{4,5},{5,4},{6,7},{7,6},{8,9},{9,8},{10,11... | collective-permute-start | bytes 393224 | tf_op jit(solution)/shard_map/ppermute | solution.py:94
  156.2 1.3 collective-permute-done.2
  157.5 0.7 pad_maximum_fusion.3
  (28 shorter events, 1.9 us)
Async XLA Ops:
  0.6 18.9 %copy-start.1 = (bf16[128,512]{1,0:T(8,128)(2,1)S(1)}, bf16[128,512]{1,0:T(8,128)(2,1)}, u32[]{:S(2)}) copy-start(bf16[128,512]{1,0:T(8,128)(2,1)} %param.10) | copy-start | bytes 393220
  0.6 20.7 %collective-permute-start.1 = (bf16[32,128,128]{2,1,0:T(8,128)(2,1)}, bf16[32,128,128]{2,1,0:T(8,128)(2,1)S(1)}, u32[]{:S(2)}, u32[]{:S(2)}) collective-permute-start(bf16[32,128,128]{2,1,0:T(8,128)(2,1)} %bitcast.52), channel_id=1, source_target_pairs={{0,1},{1,0},{2,3},{3,2},{4,5},{5,4},{6,7},{7,6},{8,9},{9,8},{10,11... | collective-permute-start | bytes 3145736 | tf_op jit(solution)/shard_map/ppermute | solution.py:94
  16.3 5.1 %copy-start = (bf16[1,32,128,128]{3,2,1,0:T(8,128)(2,1)S(1)}, bf16[1,32,128,128]{3,2,1,0:T(8,128)(2,1)}, u32[]{:S(2)}) copy-start(bf16[1,32,128,128]{3,2,1,0:T(8,128)(2,1)} %param.11) | copy-start | bytes 3145732
  16.3 5.1 %copy-start.4 = (s32[2,1,1]{0,2,1:T(1,128)S(1)}, s32[2,1,1]{0,2,1:T(1,128)}, u32[]{:S(2)}) copy-start(s32[2,1,1]{0,2,1:T(1,128)} %constant.21.clone) | copy-start | bytes 28
  17.6 3.7 %collective-permute-start = (bf16[912,256]{1,0:T(8,128)(2,1)S(1)}, bf16[912,256]{1,0:T(8,128)(2,1)S(1)}, u32[]{:S(2)}, u32[]{:S(2)}) collective-permute-start(bf16[912,256]{1,0:T(8,128)(2,1)S(1)} %pad_maximum_fusion.1), channel_id=1, source_target_pairs={{0,1},{1,0},{2,3},{3,2},{4,5},{5,4},{6,7},{7,6},{8,9},{9,8},{10,11... | collective-permute-start | bytes 1400840 | tf_op jit(solution)/shard_map/ppermute | solution.py:94
  21.3 25.3 %all-to-all-start = ((bf16[48,16,256]{2,1,0:T(8,128)(2,1)}), bf16[48,16,256]{2,1,0:T(8,128)(2,1)S(1)}, u32[]{:S(2)}, u32[]{:S(2)}) async-start(bf16[48,16,256]{2,1,0:T(8,128)(2,1)} %bitcast.1), calls=%async_computation | async-start | bytes 786432 | tf_op jit(solution)/shard_map/cond/branch_0_fun/all_to_all | solution.py:97
  46.7 26.2 %all-to-all-start.1 = ((bf16[48,16,256]{2,1,0:T(8,128)(2,1)}), bf16[48,16,256]{2,1,0:T(8,128)(2,1)S(1)}, u32[]{:S(2)}, u32[]{:S(2)}) async-start(bf16[48,16,256]{2,1,0:T(8,128)(2,1)} %bitcast.56), calls=%async_computation.1 | async-start | bytes 786432 | tf_op jit(solution)/shard_map/cond/branch_0_fun/all_to_all | solution.py:97
  76.1 24.7 %all-to-all-start.2 = ((bf16[8,256,256]{2,1,0:T(8,128)(2,1)}), bf16[8,256,256]{2,1,0:T(8,128)(2,1)}, u32[]{:S(2)}, u32[]{:S(2)}) async-start(bf16[8,256,256]{2,1,0:T(8,128)(2,1)} %bitcast.5), calls=%async_computation.2 | async-start | bytes 2097152 | tf_op jit(solution)/shard_map/cond/branch_0_fun/all_to_all | solution.py:126
  133.5 20.5 %all-to-all-start.6 = ((bf16[8,256,256]{2,1,0:T(8,128)(2,1)}), bf16[8,256,256]{2,1,0:T(8,128)(2,1)S(1)}, u32[]{:S(2)}, u32[]{:S(2)}) async-start(bf16[8,256,256]{2,1,0:T(8,128)(2,1)} %bitcast.21), calls=%async_computation.6 | async-start | bytes 2097152 | tf_op jit(solution)/shard_map/all_to_all | solution.py:126
  154.3 3.2 %collective-permute-start.2 = (bf16[2,128,256]{2,1,0:T(8,128)(2,1)S(1)}, bf16[2,128,256]{2,1,0:T(8,128)(2,1)S(1)}, u32[]{:S(2)}, u32[]{:S(2)}) collective-permute-start(bf16[2,128,256]{2,1,0:T(8,128)(2,1)S(1)} %pad_maximum_fusion.2), channel_id=1, source_target_pairs={{0,1},{1,0},{2,3},{3,2},{4,5},{5,4},{6,7},{7,6},{8,9},{9,8},{10,11... | collective-permute-start | bytes 393224 | tf_op jit(solution)/shard_map/ppermute | solution.py:94

commit v5 on v4

--- a/solution.py
+++ b/solution.py
@@ -8,13 +8,14 @@
 from jax.sharding import Mesh, PartitionSpec as P
 
 GRP = 16
+ALONG_X = 4
 PAIR = [(0, 1), (1, 0)]
 VMEM_BYTES = 24 * 1024 * 1024
 
 
-def product_kernel(slots, cap, fields, meta_ref, own_ref, other_ref, *refs):
-    field, pieces = refs[:fields], refs[fields:-3]
-    out_ref, total, space = refs[-3:]
+def product_kernel(slots, cap, fields, order, meta_ref, own_ref, other_ref, *refs):
+    field = refs[:fields]
+    fetched, out_ref, total, space = refs[fields:]
     tile = own_ref.shape[1]
     tiles = space.shape[0] // 2
     for side in range(2):
@@ -23,13 +24,10 @@
         else:
             space[side * tiles] = field[0][pl.ds(side * tile, tile), :]
         for t in range(tiles - 1):
-            if len(pieces) == 2:
-                space[side * tiles + 1 + t] = pieces[side][pl.ds(t * tile, tile), :]
-                continue
             for place in range(tile // cap):
-                owner = t * (tile // cap) + place
-                space[side * tiles + 1 + t, pl.ds(place * cap, cap), :] = pieces[0][
-                    pl.ds((2 * owner + side) * cap, cap), :
+                source = 2 * order[t * (tile // cap) + place] + side
+                space[side * tiles + 1 + t, pl.ds(place * cap, cap), :] = fetched[
+                    pl.ds(source * cap, cap), :
                 ]
     total[...] = jnp.zeros_like(total)
     for side, ref in enumerate((own_ref, other_ref)):
@@ -52,15 +50,15 @@
         out_ref[pl.ds(row * tile, tile), :] = total[row].astype(out_ref.dtype)
 
 
-def product(meta, own, other, field, pieces, slab_tiles, cap):
+def product(meta, own, other, field, fetched, order, slab_tiles, cap):
     slots, tile = own.shape[0], own.shape[1]
     width = field[0].shape[1]
-    tiles = 2 + sum(v.shape[0] for v in pieces) // tile
+    tiles = 2 + fetched.shape[0] // tile
     anywhere = pl.BlockSpec(memory_space=pltpu.VMEM)
     return pl.pallas_call(
-        functools.partial(product_kernel, slots, cap, len(field)),
+        functools.partial(product_kernel, slots, cap, len(field), order),
         out_shape=jax.ShapeDtypeStruct((slab_tiles * tile, width), jnp.bfloat16),
-        in_specs=[pl.BlockSpec(memory_space=pltpu.SMEM)] + [anywhere] * (2 + len(field) + len(pieces)),
+        in_specs=[pl.BlockSpec(memory_space=pltpu.SMEM)] + [anywhere] * (3 + len(field)),
         out_specs=anywhere,
         scratch_shapes=[
             pltpu.VMEM((slab_tiles, tile, width), jnp.float32),
@@ -72,7 +70,7 @@
             bytes_accessed=2 * (2 * slots * tile * tile + (tiles + slab_tiles) * tile * width),
             transcendentals=0,
         ),
-    )(meta, own, other, *field, *pieces)
+    )(meta, own, other, *field, fetched)
 
 
 def one_hot(wanted, extent):
@@ -86,15 +84,16 @@
     rows, width = features.shape
     half = width // 2
     cap = send_rows.shape[2]
-    owners = lax.axis_size("rows")
+    along, across = lax.axis_size("x"), lax.axis_size("z")
+    owners = along * across
     slab_tiles = 2 * lax.axis_size("y")
     core = lax.axis_index("core")
 
     def swap(value):
         return lax.ppermute(value, "core", PAIR)
 
-    def exchange(picked):
-        got = lax.all_to_all(picked.reshape(owners, -1, half), "rows", 0, 0, tiled=True)
+    def exchange(picked, axes=("x", "z")):
+        got = lax.all_to_all(picked.reshape(lax.axis_size(axes), -1, half), axes, 0, 0, tiled=True)
         return got.reshape(-1, half)
 
     def pick(chosen, field):
@@ -121,31 +120,41 @@
         wanted = both[:, :, :owners] + jnp.array([[[0]], [[rows]]], jnp.int32)
         return meta, wanted.transpose(2, 0, 1).reshape(-1)
 
-    def multiply(field, pieces, meta, held, other_held):
-        partial_value = product(meta, held, other_held, field, pieces, slab_tiles, cap)
-        parts = lax.all_to_all(
-            partial_value.reshape(-1, 2 * rows, half), "y", 0, 0, tiled=True
-        )
+    def multiply(field, fetched, order, meta, held, other_held):
+        partial_value = product(meta, held, other_held, field, fetched, order, slab_tiles, cap)
+        return partial_value.reshape(-1, 2 * rows, half)
+
+    def combine(partial_value):
+        parts = lax.all_to_all(partial_value, "y", 0, 0, tiled=True)
         return jnp.sum(parts.astype(jnp.float32), 0).astype(jnp.bfloat16)
+
+    straight = tuple(range(owners))
+    turned = tuple(q % across * along + q // across for q in straight)
 
     def in_one(operands):
         mine, picked, given, numbers, *tiles = operands
         meta, wanted = places(given, numbers)
         mixed = [v.reshape(owners, cap, half) for v in (picked, given[: ends[0]])]
         fetched = exchange(jnp.concatenate(mixed, 1))
-        return multiply((mine, given[ends[0] : ends[1]]), (fetched,), meta, *tiles), meta, wanted
+        partial_value = multiply((mine, given[ends[0] : ends[1]]), fetched, straight, meta, *tiles)
+        partial_value, wanted = lax.optimization_barrier((partial_value, wanted))
+        return combine(partial_value), meta, wanted
 
-    def in_two(operands):
+    def in_steps(operands):
         mine, picked, given, numbers, *tiles = operands
         meta, wanted = places(given, numbers)
-        pieces = exchange(picked), exchange(given[: ends[0]])
-        return multiply((mine, given[ends[0] : ends[1]]), pieces, meta, *tiles), meta, wanted
+        shape = along, across, cap, half
+        moved = [exchange(v, "x").reshape(shape) for v in (picked, given[: ends[0]])]
+        fetched = exchange(jnp.stack(moved, 2).transpose(1, 0, 2, 3, 4), "z")
+        partial_value = multiply((mine, given[ends[0] : ends[1]]), fetched, turned, meta, *tiles)
+        partial_value, wanted = lax.optimization_barrier((partial_value, wanted))
+        return combine(partial_value), meta, wanted
 
     first, meta, wanted = lax.optimization_barrier(
-        lax.cond(core == 0, in_one, in_two, (mine, picked, given, numbers, held, other_held))
+        lax.cond(core == 0, in_one, in_steps, (mine, picked, given, numbers, held, other_held))
     )
     fetched = exchange(pick(one_hot(wanted, 2 * rows), first))
-    second = multiply((first,), (fetched,), meta, held, other_held)
+    second = combine(multiply((first,), fetched, straight, meta, held, other_held))
     others = swap(jnp.stack([first[rows:], second[rows:]])).reshape(2 * rows, half)
 
     def whole(kept, other):
@@ -158,21 +167,21 @@
 
 def solution(mesh):
     inner = Mesh(
-        mesh.devices.reshape(mesh.shape["rows"], -1, 2), ("rows", "y", "core")
+        mesh.devices.reshape(ALONG_X, mesh.shape["rows"] // ALONG_X, -1, 2), ("x", "z", "y", "core")
     )
-    cols = ("y", "core")
+    lines, cols = ("x", "z"), ("y", "core")
     placed = (
-        P(("rows", "y", "core"), None),
-        P("rows", cols, None, None),
-        P("rows", cols),
-        P("rows", cols),
-        P("rows", cols),
-        P("rows", cols, None),
+        P((*lines, *cols), None),
+        P(lines, cols, None, None),
+        P(lines, cols),
+        P(lines, cols),
+        P(lines, cols),
+        P(lines, cols, None),
     )
     return jax.shard_map(
         on_device,
         mesh=inner,
         in_specs=placed,
-        out_specs=(P(("rows", "y", "core"), None), P(("rows", "y", "core"), None)),
+        out_specs=(P((*lines, *cols), None), P((*lines, *cols), None)),
         check_vma=False,
     )

time: 159 us -> 160 us (level)
  blocking collectives: 27.7 us -> 63.7 us
  starting transfers between devices: 46.8 us -> 30.2 us
  waiting for transfers between devices: 67.1 us -> 50.9 us
    all_to_all x1 -> x3, blocking collectives: 27.7 us -> 63.7 us  [the longest x2 39.8 us: exchange(): lax.all_to_all(picked.reshape(lax.axis_size(axes), -1, half), axes, 0, 0,...]
    all_to_all x4 -> x3, starting transfers between devices: 30.4 us -> 13.8 us  [the longest x2 10.3 us: exchange(): lax.all_to_all(picked.reshape(lax.axis_size(axes), -1, half), axes, 0, 0,...]
    all_to_all x4 -> x3, waiting for transfers between devices: 65.1 us -> 48.9 us  [the longest x2 25.3 us: exchange(): lax.all_to_all(picked.reshape(lax.axis_size(axes), -1, half), axes, 0, 0,...]
  transfers between devices with their start and end apart: 7 -> 6, of which waited for: 6 -> 5; matrix products, arithmetic and copies ran while one was open for 4% -> 3% of each run, Pallas kernels for 0% -> 0%
where the time goes in v5:
time: 160 us; the launch traced here: 159 us
  blocking collectives  63.7 us (40%)
  waiting for transfers between devices  50.9 us (32%)
  starting transfers between devices  30.2 us (19%)
  Pallas kernels  5.31 us (3%)
  other arithmetic  2.86 us (2%)
  matrix products  2.8 us (2%)
  local copies, waits for them, and re-layouts  2.17 us (1%)
    all_to_all x2, blocking collectives, exchange(): lax.all_to_all(picked.reshape(lax.axis_size(axes), -1, half), axes, 0, 0,...  39.8 us
    all_to_all x2, waiting for transfers between devices, exchange(): lax.all_to_all(picked.reshape(lax.axis_size(axes), -1, half), axes, 0, 0,...  25.3 us
    all_to_all x1, blocking collectives, combine(): parts = lax.all_to_all(partial_value, 'y', 0, 0, tiled=True)  23.9 us
    all_to_all x1, waiting for transfers between devices, combine(): parts = lax.all_to_all(partial_value, 'y', 0, 0, tiled=True)  23.5 us
    ppermute x3, starting transfers between devices, swap(): return lax.ppermute(value, 'core', PAIR)  16.4 us
    all_to_all x2, starting transfers between devices, exchange(): lax.all_to_all(picked.reshape(lax.axis_size(axes), -1, half), axes, 0, 0,...  10.3 us
    pallas_call x2, Pallas kernels, product(): pl.pallas_call(functools.partial(product_kernel, slots, cap, len(field),...  5.31 us
    all_to_all x1, starting transfers between devices, combine(): parts = lax.all_to_all(partial_value, 'y', 0, 0, tiled=True)  3.56 us
  transfers between devices with their start and end apart: 6, of which 5 were waited for; matrix products, arithmetic and copies ran while one was open for 3% of the time, Pallas kernels for 0%

profile of v5, /device:TPU:1, one launch (start us, length us, event | category | flops | bytes accessed | tf_op | source)
XLA Modules:
  0.0 159.5 jit_solution(6051859725251257135)
XLA Ops:
  0.6 12.6 %collective-permute-start.1 = (bf16[32,128,128]{2,1,0:T(8,128)(2,1)}, bf16[32,128,128]{2,1,0:T(8,128)(2,1)S(1)}, u32[]{:S(2)}, u32[]{:S(2)}) collective-permute-start(bf16[32,128,128]{2,1,0:T(8,128)(2,1)} %bitcast.57), channel_id=1, source_target_pairs={{0,1},{1,0},{2,3},{3,2},{4,5},{5,4},{6,7},{7,6},{8,9},{9,8},{10,11... | collective-permute-start | bytes 3145736 | tf_op jit(solution)/shard_map/ppermute | solution.py:93
  13.9 0.8 copy.16
  14.7 0.8 pad_add_fusion.4
  15.5 0.8 fusion.14
  16.3 1.3 fusion.6
  17.6 1.9 %collective-permute-start = (bf16[912,256]{1,0:T(8,128)(2,1)S(1)}, bf16[912,256]{1,0:T(8,128)(2,1)S(1)}, u32[]{:S(2)}, u32[]{:S(2)}) collective-permute-start(bf16[912,256]{1,0:T(8,128)(2,1)S(1)} %pad_maximum_fusion.2), channel_id=1, source_target_pairs={{0,1},{1,0},{2,3},{3,2},{4,5},{5,4},{6,7},{7,6},{8,9},{9,8},{10,11... | collective-permute-start | bytes 1400840 | tf_op jit(solution)/shard_map/ppermute | solution.py:93
  19.6 1.1 fusion.7
  20.6 0.7 collective-permute-done
  21.3 72.7 %conditional.1 = (bf16[256,256]{1,0:T(8,128)(2,1)S(1)}, s32[2,65]{1,0:T(2,128)S(1)}, s32[1536]{0:T(1024)S(1)}) conditional(s32[]{:T(128)} %convert_element_type.4, (s32[16,256]{1,0:T(8,128)S(1)}, bf16[912,256]{1,0:T(8,128)(2,1)S(1)}, s32[]{:T(128)}, bf16[768,256]{1,0:T(8,128)(2,1)}, bf16[32,128,128]{2,1,0:T(8,128)(2,1)S(1)}, ...), branch_computations={%region_0.2_spmd, %region_2.4_spmd} | conditional | flops 538910144 | bytes 15915760 | solution.py:154
  21.3 3.5 %all-to-all-start = ((bf16[4,192,256]{2,1,0:T(8,128)(2,1)}), bf16[4,192,256]{2,1,0:T(8,128)(2,1)S(1)}, u32[]{:S(2)}, u32[]{:S(2)}) async-start(bf16[4,192,256]{2,1,0:T(8,128)(2,1)} %bitcast.1), calls=%async_computation | async-start | bytes 786432 | tf_op jit(solution)/shard_map/cond/branch_0_fun/all_to_all | solution.py:96
  24.9 6.2 %all-to-all-done = bf16[4,192,256]{2,1,0:T(8,128)(2,1)S(1)} async-done(((bf16[4,192,256]{2,1,0:T(8,128)(2,1)}), bf16[4,192,256]{2,1,0:T(8,128)(2,1)S(1)}, u32[]{:S(2)}, u32[]{:S(2)}) %all-to-all-start) | async-done | bytes 393248 | tf_op jit(solution)/shard_map/cond/branch_0_fun/all_to_all | solution.py:96
  31.0 9.3 %all_to_all.34 = bf16[4,192,256]{2,1,0:T(8,128)(2,1)S(1)} all-to-all(bf16[4,192,256]{2,1,0:T(8,128)(2,1)S(1)} %bitcast.62), channel_id=1, replica_groups=mesh['x'=4,'z'=12,'y'=8,'core'=2] {'x'}, dimensions={0} | all-to-all | bytes 786432 | tf_op jit(solution)/shard_map/cond/branch_0_fun/all_to_all | solution.py:96
  40.4 1.0 copy.17
  41.4 6.8 %all-to-all-start.2 = ((bf16[12,128,256]{2,1,0:T(8,128)(2,1)}), bf16[12,128,256]{2,1,0:T(8,128)(2,1)S(1)}, u32[]{:S(2)}, u32[]{:S(2)}) async-start(bf16[12,128,256]{2,1,0:T(8,128)(2,1)} %bitcast.61), calls=%async_computation.2 | async-start | bytes 1572864 | tf_op jit(solution)/shard_map/cond/branch_0_fun/all_to_all | solution.py:96
  48.6 19.2 %all-to-all-done.2 = bf16[12,128,256]{2,1,0:T(8,128)(2,1)S(1)} async-done(((bf16[12,128,256]{2,1,0:T(8,128)(2,1)}), bf16[12,128,256]{2,1,0:T(8,128)(2,1)S(1)}, u32[]{:S(2)}, u32[]{:S(2)}) %all-to-all-start.2) | async-done | bytes 786464 | tf_op jit(solution)/shard_map/cond/branch_0_fun/all_to_all | solution.py:96
  67.8 2.2 %branch_0_fun.1 = bf16[2048,256]{1,0:T(8,128)(2,1)S(1)} custom-call(s32[2,65]{1,0:T(2,128)S(1)} %xor_select_fusion.meta_ref, bf16[32,128,128]{2,1,0:T(8,128)(2,1)S(1)} %get-tuple-element.35.own_ref, bf16[32,128,128]{2,1,0:T(8,128)(2,1)S(1)} %get-tuple-element.36.other_ref, bf16[128,256]{1,0:T(8,128)(2,1)S(1)} %get-tuple-element.37.refs_0_, ...), custom_call_target="tpu_custom_call" | custom-call | flops 536870912 | bytes 4063232 | tf_op jit(solution)/shard_map/cond/branch_0_fun/pallas_call | solution.py:58
  70.0 23.9 %all_to_all.35 = bf16[8,256,256]{2,1,0:T(8,128)(2,1)S(1)} all-to-all(bf16[8,256,256]{2,1,0:T(8,128)(2,1)S(1)} %bitcast.52), channel_id=1, replica_groups=mesh['x'=4,'z'=12,'y'=8,'core'=2] {'y'}, dimensions={0} | all-to-all | bytes 2097152 | tf_op jit(solution)/shard_map/cond/branch_0_fun/all_to_all | solution.py:128
  94.5 30.5 %all_to_all.37 = bf16[48,32,256]{2,1,0:T(8,128)(2,1)S(1)} all-to-all(bf16[48,32,256]{2,1,0:T(8,128)(2,1)S(1)} %bitcast.66), channel_id=1, replica_groups=mesh['x'=4,'z'=12,'y'=8,'core'=2] {'x','z'}, dimensions={0} | all-to-all | bytes 1572864 | tf_op jit(solution)/shard_map/all_to_all | solution.py:96
  125.0 3.1 %shard_map.95 = bf16[2048,256]{1,0:T(8,128)(2,1)} custom-call(s32[2,65]{1,0:T(2,128)S(1)} %get-tuple-element.58.meta_ref, bf16[32,128,128]{2,1,0:T(8,128)(2,1)S(1)} %bitcast.60, bf16[32,128,128]{2,1,0:T(8,128)(2,1)S(1)} %collective-permute-done.1.other_ref, bf16[256,256]{1,0:T(8,128)(2,1)S(1)} %get-tuple-element.57.refs_0_, bf16[1536,256]{1,0:T(8,128)(2,1)S(1)} %bitcast.56), custom_call_target="tpu_custom_call" | custom-call | flops 536870912 | bytes 4063232 | tf_op jit(solution)/shard_map/pallas_call | solution.py:58
  128.2 3.6 %all-to-all-start.7 = ((bf16[8,256,256]{2,1,0:T(8,128)(2,1)}), bf16[8,256,256]{2,1,0:T(8,128)(2,1)S(1)}, u32[]{:S(2)}, u32[]{:S(2)}) async-start(bf16[8,256,256]{2,1,0:T(8,128)(2,1)} %bitcast.24), calls=%async_computation.7 | async-start | bytes 2097152 | tf_op jit(solution)/shard_map/all_to_all | solution.py:128
  131.7 23.5 %all-to-all-done.7 = bf16[8,256,256]{2,1,0:T(8,128)(2,1)S(1)} async-done(((bf16[8,256,256]{2,1,0:T(8,128)(2,1)}), bf16[8,256,256]{2,1,0:T(8,128)(2,1)S(1)}, u32[]{:S(2)}, u32[]{:S(2)}) %all-to-all-start.7) | async-done | bytes 1048608 | tf_op jit(solution)/shard_map/all_to_all | solution.py:128
  155.5 1.9 %collective-permute-start.2 = (bf16[2,128,256]{2,1,0:T(8,128)(2,1)S(1)}, bf16[2,128,256]{2,1,0:T(8,128)(2,1)S(1)}, u32[]{:S(2)}, u32[]{:S(2)}) collective-permute-start(bf16[2,128,256]{2,1,0:T(8,128)(2,1)S(1)} %pad_maximum_fusion.3), channel_id=1, source_target_pairs={{0,1},{1,0},{2,3},{3,2},{4,5},{5,4},{6,7},{7,6},{8,9},{9,8},{10,11... | collective-permute-start | bytes 393224 | tf_op jit(solution)/shard_map/ppermute | solution.py:93
  157.4 1.3 collective-permute-done.2
  158.7 0.7 pad_maximum_fusion.4
  (30 shorter events, 1.4 us)
Async XLA Ops:
  0.6 18.9 %copy-start.1 = (bf16[128,512]{1,0:T(8,128)(2,1)S(1)}, bf16[128,512]{1,0:T(8,128)(2,1)}, u32[]{:S(2)}) copy-start(bf16[128,512]{1,0:T(8,128)(2,1)} %param.10) | copy-start | bytes 393220
  0.6 20.7 %collective-permute-start.1 = (bf16[32,128,128]{2,1,0:T(8,128)(2,1)}, bf16[32,128,128]{2,1,0:T(8,128)(2,1)S(1)}, u32[]{:S(2)}, u32[]{:S(2)}) collective-permute-start(bf16[32,128,128]{2,1,0:T(8,128)(2,1)} %bitcast.57), channel_id=1, source_target_pairs={{0,1},{1,0},{2,3},{3,2},{4,5},{5,4},{6,7},{7,6},{8,9},{9,8},{10,11... | collective-permute-start | bytes 3145736 | tf_op jit(solution)/shard_map/ppermute | solution.py:93
  16.3 5.1 %copy-start = (bf16[1,32,128,128]{3,2,1,0:T(8,128)(2,1)S(1)}, bf16[1,32,128,128]{3,2,1,0:T(8,128)(2,1)}, u32[]{:S(2)}) copy-start(bf16[1,32,128,128]{3,2,1,0:T(8,128)(2,1)} %param.11) | copy-start | bytes 3145732
  16.3 5.1 %copy-start.5 = (s32[2,1,1]{0,2,1:T(1,128)S(1)}, s32[2,1,1]{0,2,1:T(1,128)}, u32[]{:S(2)}) copy-start(s32[2,1,1]{0,2,1:T(1,128)} %constant.21.clone) | copy-start | bytes 28
  17.6 3.7 %collective-permute-start = (bf16[912,256]{1,0:T(8,128)(2,1)S(1)}, bf16[912,256]{1,0:T(8,128)(2,1)S(1)}, u32[]{:S(2)}, u32[]{:S(2)}) collective-permute-start(bf16[912,256]{1,0:T(8,128)(2,1)S(1)} %pad_maximum_fusion.2), channel_id=1, source_target_pairs={{0,1},{1,0},{2,3},{3,2},{4,5},{5,4},{6,7},{7,6},{8,9},{9,8},{10,11... | collective-permute-start | bytes 1400840 | tf_op jit(solution)/shard_map/ppermute | solution.py:93
  21.3 9.7 %all-to-all-start = ((bf16[4,192,256]{2,1,0:T(8,128)(2,1)}), bf16[4,192,256]{2,1,0:T(8,128)(2,1)S(1)}, u32[]{:S(2)}, u32[]{:S(2)}) async-start(bf16[4,192,256]{2,1,0:T(8,128)(2,1)} %bitcast.1), calls=%async_computation | async-start | bytes 786432 | tf_op jit(solution)/shard_map/cond/branch_0_fun/all_to_all | solution.py:96
  41.4 26.4 %all-to-all-start.2 = ((bf16[12,128,256]{2,1,0:T(8,128)(2,1)}), bf16[12,128,256]{2,1,0:T(8,128)(2,1)S(1)}, u32[]{:S(2)}, u32[]{:S(2)}) async-start(bf16[12,128,256]{2,1,0:T(8,128)(2,1)} %bitcast.61), calls=%async_computation.2 | async-start | bytes 1572864 | tf_op jit(solution)/shard_map/cond/branch_0_fun/all_to_all | solution.py:96
  128.2 27.1 %all-to-all-start.7 = ((bf16[8,256,256]{2,1,0:T(8,128)(2,1)}), bf16[8,256,256]{2,1,0:T(8,128)(2,1)S(1)}, u32[]{:S(2)}, u32[]{:S(2)}) async-start(bf16[8,256,256]{2,1,0:T(8,128)(2,1)} %bitcast.24), calls=%async_computation.7 | async-start | bytes 2097152 | tf_op jit(solution)/shard_map/all_to_all | solution.py:128
  155.5 3.2 %collective-permute-start.2 = (bf16[2,128,256]{2,1,0:T(8,128)(2,1)S(1)}, bf16[2,128,256]{2,1,0:T(8,128)(2,1)S(1)}, u32[]{:S(2)}, u32[]{:S(2)}) collective-permute-start(bf16[2,128,256]{2,1,0:T(8,128)(2,1)S(1)} %pad_maximum_fusion.3), channel_id=1, source_target_pairs={{0,1},{1,0},{2,3},{3,2},{4,5},{5,4},{6,7},{7,6},{8,9},{9,8},{10,11... | collective-permute-start | bytes 393224 | tf_op jit(solution)/shard_map/ppermute | solution.py:93

commit v6 on v5

--- a/solution.py
+++ b/solution.py
@@ -10,7 +10,7 @@
 GRP = 16
 ALONG_X = 4
 PAIR = [(0, 1), (1, 0)]
-VMEM_BYTES = 24 * 1024 * 1024
+VMEM_BYTES = 16 * 1024 * 1024
 
 
 def product_kernel(slots, cap, fields, order, meta_ref, own_ref, other_ref, *refs):
@@ -73,6 +73,24 @@
     )(meta, own, other, *field, fetched)
 
 
+def mix_kernel(cap, mine_ref, given_ref, out_ref):
+    for owner in range(mine_ref.shape[0] // cap):
+        rows = pl.ds(owner * cap, cap)
+        out_ref[pl.ds(2 * owner * cap, cap), :] = mine_ref[rows, :]
+        out_ref[pl.ds((2 * owner + 1) * cap, cap), :] = given_ref[rows, :]
+
+
+def mix(mine, given, cap):
+    anywhere = pl.BlockSpec(memory_space=pltpu.VMEM)
+    return pl.pallas_call(
+        functools.partial(mix_kernel, cap),
+        out_shape=jax.ShapeDtypeStruct((2 * mine.shape[0], mine.shape[1]), mine.dtype),
+        in_specs=[anywhere, anywhere],
+        out_specs=anywhere,
+        compiler_params=pltpu.CompilerParams(vmem_limit_bytes=VMEM_BYTES),
+    )(mine, given)
+
+
 def one_hot(wanted, extent):
     place = lax.broadcasted_iota(jnp.int32, (1, extent), 1)
     return (wanted.reshape(-1, 1) == place).astype(jnp.bfloat16)
@@ -134,8 +152,7 @@
     def in_one(operands):
         mine, picked, given, numbers, *tiles = operands
         meta, wanted = places(given, numbers)
-        mixed = [v.reshape(owners, cap, half) for v in (picked, given[: ends[0]])]
-        fetched = exchange(jnp.concatenate(mixed, 1))
+        fetched = exchange(mix(picked, given, cap))
         partial_value = multiply((mine, given[ends[0] : ends[1]]), fetched, straight, meta, *tiles)
         partial_value, wanted = lax.optimization_barrier((partial_value, wanted))
         return combine(partial_value), meta, wanted
@@ -143,6 +160,7 @@
     def in_steps(operands):
         mine, picked, given, numbers, *tiles = operands
         meta, wanted = places(given, numbers)
+        meta, wanted, picked, given = lax.optimization_barrier((meta, wanted, picked, given))
         shape = along, across, cap, half
         moved = [exchange(v, "x").reshape(shape) for v in (picked, given[: ends[0]])]
         fetched = exchange(jnp.stack(moved, 2).transpose(1, 0, 2, 3, 4), "z")
@@ -154,8 +172,10 @@
         lax.cond(core == 0, in_one, in_steps, (mine, picked, given, numbers, held, other_held))
     )
     fetched = exchange(pick(one_hot(wanted, 2 * rows), first))
-    second = combine(multiply((first,), fetched, straight, meta, held, other_held))
-    others = swap(jnp.stack([first[rows:], second[rows:]])).reshape(2 * rows, half)
+    partial_value = multiply((first,), fetched, straight, meta, held, other_held)
+    partial_value, first_back = lax.optimization_barrier((partial_value, first[rows:]))
+    second = combine(partial_value)
+    others = swap(jnp.stack([first_back, second[rows:]])).reshape(2 * rows, half)
 
     def whole(kept, other):
         return jnp.concatenate(

time: 160 us -> 161 us (level)
  Pallas kernels: 5.31 us -> 3.47 us
    all_to_all x2 -> x1, blocking collectives: 39.8 us -> 9.26 us  [exchange(): lax.all_to_all(picked.reshape(lax.axis_size(axes), -1, half), axes, 0, 0,...]
    all_to_all x1 -> x2, blocking collectives: 23.9 us -> 53.5 us  [combine(): parts = lax.all_to_all(partial_value, 'y', 0, 0, tiled=True)]
    all_to_all x2 -> x3, waiting for transfers between devices: 25.3 us -> 50.3 us  [exchange(): lax.all_to_all(picked.reshape(lax.axis_size(axes), -1, half), axes, 0, 0,...]
    all_to_all x1 -> x0, waiting for transfers between devices: 23.5 us -> none  [combine(): parts = lax.all_to_all(partial_value, 'y', 0, 0, tiled=True)]
    all_to_all x2 -> x3, starting transfers between devices: 10.3 us -> 15.4 us  [exchange(): lax.all_to_all(picked.reshape(lax.axis_size(axes), -1, half), axes, 0, 0,...]
    all_to_all x1 -> x0, starting transfers between devices: 3.56 us -> none  [combine(): parts = lax.all_to_all(partial_value, 'y', 0, 0, tiled=True)]
    pallas_call x2, Pallas kernels: 5.31 us -> 3.47 us  [product(): pl.pallas_call(functools.partial(product_kernel, slots, cap, len(field),...]
where the time goes in v6:
time: 161 us
  blocking collectives  62.7 us (39%)
  waiting for transfers between devices  52.3 us (32%)
  starting transfers between devices  31.8 us (20%)
  matrix products  3.69 us (2%)
  Pallas kernels  3.47 us (2%)
  other arithmetic  2.86 us (2%)
  local copies, waits for them, and re-layouts  2.15 us (1%)
    all_to_all x2, blocking collectives, combine(): parts = lax.all_to_all(partial_value, 'y', 0, 0, tiled=True)  53.5 us
    all_to_all x3, waiting for transfers between devices, exchange(): lax.all_to_all(picked.reshape(lax.axis_size(axes), -1, half), axes, 0, 0,...  50.3 us
    ppermute x3, starting transfers between devices, swap(): return lax.ppermute(value, 'core', PAIR)  16.4 us
    all_to_all x3, starting transfers between devices, exchange(): lax.all_to_all(picked.reshape(lax.axis_size(axes), -1, half), axes, 0, 0,...  15.4 us
    all_to_all x1, blocking collectives, exchange(): lax.all_to_all(picked.reshape(lax.axis_size(axes), -1, half), axes, 0, 0,...  9.26 us
    dot_general x3, matrix products, pick(): return jnp.dot(chosen, field, preferred_element_type=jnp.bfloat16)  3.69 us
    pallas_call x2, Pallas kernels, product(): pl.pallas_call(functools.partial(product_kernel, slots, cap, len(field),...  3.47 us
  transfers between devices with their start and end apart: 6, of which 5 were waited for; matrix products, arithmetic and copies ran while one was open for 3% of the time, Pallas kernels for 0%

profile of v6, /device:TPU:1, one launch (start us, length us, event | category | flops | bytes accessed | tf_op | source)
XLA Modules:
  0.0 160.5 jit_solution(16183422600156839817)
XLA Ops:
  0.6 12.6 %collective-permute-start.1 = (bf16[32,128,128]{2,1,0:T(8,128)(2,1)}, bf16[32,128,128]{2,1,0:T(8,128)(2,1)S(1)}, u32[]{:S(2)}, u32[]{:S(2)}) collective-permute-start(bf16[32,128,128]{2,1,0:T(8,128)(2,1)} %bitcast.56), channel_id=1, source_target_pairs={{0,1},{1,0},{2,3},{3,2},{4,5},{5,4},{6,7},{7,6},{8,9},{9,8},{10,11... | collective-permute-start | bytes 3145736 | tf_op jit(solution)/shard_map/ppermute | solution.py:111
  13.9 0.8 copy.16
  14.7 0.8 pad_add_fusion.4
  15.5 0.8 fusion.14
  16.3 1.3 fusion.6
  17.6 1.9 %collective-permute-start = (bf16[912,256]{1,0:T(8,128)(2,1)S(1)}, bf16[912,256]{1,0:T(8,128)(2,1)S(1)}, u32[]{:S(2)}, u32[]{:S(2)}) collective-permute-start(bf16[912,256]{1,0:T(8,128)(2,1)S(1)} %pad_maximum_fusion.1), channel_id=1, source_target_pairs={{0,1},{1,0},{2,3},{3,2},{4,5},{5,4},{6,7},{7,6},{8,9},{9,8},{10,11... | collective-permute-start | bytes 1400840 | tf_op jit(solution)/shard_map/ppermute | solution.py:111
  19.6 1.1 fusion.7
  21.3 73.1 %conditional.1 = (bf16[256,256]{1,0:T(8,128)(2,1)S(1)}, s32[2,65]{1,0:T(2,128)S(1)}, s32[1536]{0:T(1024)S(1)}) conditional(s32[]{:T(128)} %convert_element_type.4, (s32[16,256]{1,0:T(8,128)S(1)}, bf16[912,256]{1,0:T(8,128)(2,1)S(1)}, s32[]{:T(128)}, s32[2,1,1]{0,2,1:T(1,128)S(1)}, bf16[768,256]{1,0:T(8,128)(2,1)}, ...), branch_computations={%region_0.2_spmd, %region_2.4_spmd} | conditional | flops 537730496 | bytes 15915760 | solution.py:172
  21.8 3.5 %all-to-all-start = ((bf16[4,192,256]{2,1,0:T(8,128)(2,1)}), bf16[4,192,256]{2,1,0:T(8,128)(2,1)S(1)}, u32[]{:S(2)}, u32[]{:S(2)}) async-start(bf16[4,192,256]{2,1,0:T(8,128)(2,1)} %bitcast.3), calls=%async_computation | async-start | bytes 786432 | tf_op jit(solution)/shard_map/cond/branch_0_fun/all_to_all | solution.py:114
  25.3 6.2 %all-to-all-done = bf16[4,192,256]{2,1,0:T(8,128)(2,1)S(1)} async-done(((bf16[4,192,256]{2,1,0:T(8,128)(2,1)}), bf16[4,192,256]{2,1,0:T(8,128)(2,1)S(1)}, u32[]{:S(2)}, u32[]{:S(2)}) %all-to-all-start) | async-done | bytes 393248 | tf_op jit(solution)/shard_map/cond/branch_0_fun/all_to_all | solution.py:114
  31.4 9.3 %all_to_all.34 = bf16[4,192,256]{2,1,0:T(8,128)(2,1)S(1)} all-to-all(bf16[4,192,256]{2,1,0:T(8,128)(2,1)S(1)} %bitcast.61), channel_id=1, replica_groups=mesh['x'=4,'z'=12,'y'=8,'core'=2] {'x'}, dimensions={0} | all-to-all | bytes 786432 | tf_op jit(solution)/shard_map/cond/branch_0_fun/all_to_all | solution.py:114
  40.8 1.0 copy.17
  41.8 6.8 %all-to-all-start.2 = ((bf16[12,128,256]{2,1,0:T(8,128)(2,1)}), bf16[12,128,256]{2,1,0:T(8,128)(2,1)S(1)}, u32[]{:S(2)}, u32[]{:S(2)}) async-start(bf16[12,128,256]{2,1,0:T(8,128)(2,1)} %bitcast.60), calls=%async_computation.2 | async-start | bytes 1572864 | tf_op jit(solution)/shard_map/cond/branch_0_fun/all_to_all | solution.py:114
  48.6 19.2 %all-to-all-done.2 = bf16[12,128,256]{2,1,0:T(8,128)(2,1)S(1)} async-done(((bf16[12,128,256]{2,1,0:T(8,128)(2,1)}), bf16[12,128,256]{2,1,0:T(8,128)(2,1)S(1)}, u32[]{:S(2)}, u32[]{:S(2)}) %all-to-all-start.2) | async-done | bytes 786464 | tf_op jit(solution)/shard_map/cond/branch_0_fun/all_to_all | solution.py:114
  67.8 1.7 %branch_0_fun.1 = bf16[2048,256]{1,0:T(8,128)(2,1)S(1)} custom-call(s32[2,65]{1,0:T(2,128)S(1)} %xor_select_fusion.meta_ref, bf16[32,128,128]{2,1,0:T(8,128)(2,1)S(1)} %get-tuple-element.38.own_ref, bf16[32,128,128]{2,1,0:T(8,128)(2,1)S(1)} %get-tuple-element.39.other_ref, bf16[128,256]{1,0:T(8,128)(2,1)S(1)} %get-tuple-element.40.refs_0_, ...), custom_call_target="tpu_custom_call" | custom-call | flops 536870912 | bytes 4063232 | tf_op jit(solution)/shard_map/cond/branch_0_fun/pallas_call | solution.py:58
  69.5 24.8 %all_to_all.35 = bf16[8,256,256]{2,1,0:T(8,128)(2,1)S(1)} all-to-all(bf16[8,256,256]{2,1,0:T(8,128)(2,1)S(1)} %bitcast.51), channel_id=1, replica_groups=mesh['x'=4,'z'=12,'y'=8,'core'=2] {'y'}, dimensions={0} | all-to-all | bytes 2097152 | tf_op jit(solution)/shard_map/cond/branch_0_fun/all_to_all | solution.py:146
  94.5 1.3 fusion.4
  95.8 5.2 %all-to-all-start.6 = ((bf16[48,32,256]{2,1,0:T(8,128)(2,1)}), bf16[48,32,256]{2,1,0:T(8,128)(2,1)S(1)}, u32[]{:S(2)}, u32[]{:S(2)}) async-start(bf16[48,32,256]{2,1,0:T(8,128)(2,1)} %bitcast.64), calls=%async_computation.6 | async-start | bytes 1572864 | tf_op jit(solution)/shard_map/all_to_all | solution.py:114
  101.0 25.0 %all-to-all-done.6 = bf16[48,32,256]{2,1,0:T(8,128)(2,1)S(1)} async-done(((bf16[48,32,256]{2,1,0:T(8,128)(2,1)}), bf16[48,32,256]{2,1,0:T(8,128)(2,1)S(1)}, u32[]{:S(2)}, u32[]{:S(2)}) %all-to-all-start.6) | async-done | bytes 786464 | tf_op jit(solution)/shard_map/all_to_all | solution.py:114
  126.0 1.7 %shard_map.95 = bf16[2048,256]{1,0:T(8,128)(2,1)S(1)} custom-call(s32[2,65]{1,0:T(2,128)S(1)} %get-tuple-element.64.meta_ref, bf16[32,128,128]{2,1,0:T(8,128)(2,1)S(1)} %bitcast.59, bf16[32,128,128]{2,1,0:T(8,128)(2,1)S(1)} %collective-permute-done.1.other_ref, bf16[256,256]{1,0:T(8,128)(2,1)S(1)} %get-tuple-element.63.refs_0_, bf16[1536,256]{1,0:T(8,128)(2,1)S(1)} %bitcast.54), custom_call_target="tpu_custom_call" | custom-call | flops 536870912 | bytes 4063232 | tf_op jit(solution)/shard_map/pallas_call | solution.py:58
  127.7 28.6 %all_to_all.37 = bf16[8,256,256]{2,1,0:T(8,128)(2,1)S(1)} all-to-all(bf16[8,256,256]{2,1,0:T(8,128)(2,1)S(1)} %bitcast.50), channel_id=1, replica_groups=mesh['x'=4,'z'=12,'y'=8,'core'=2] {'y'}, dimensions={0} | all-to-all | bytes 2097152 | tf_op jit(solution)/shard_map/all_to_all | solution.py:146
  156.5 1.9 %collective-permute-start.2 = (bf16[2,128,256]{2,1,0:T(8,128)(2,1)S(1)}, bf16[2,128,256]{2,1,0:T(8,128)(2,1)S(1)}, u32[]{:S(2)}, u32[]{:S(2)}) collective-permute-start(bf16[2,128,256]{2,1,0:T(8,128)(2,1)S(1)} %pad_maximum_fusion.2), channel_id=1, source_target_pairs={{0,1},{1,0},{2,3},{3,2},{4,5},{5,4},{6,7},{7,6},{8,9},{9,8},{10,11... | collective-permute-start | bytes 393224 | tf_op jit(solution)/shard_map/ppermute | solution.py:111
  158.5 1.3 collective-permute-done.2
  159.8 0.7 pad_maximum_fusion.3
  (30 shorter events, 1.7 us)
Async XLA Ops:
  0.6 18.9 %copy-start.1 = (bf16[128,512]{1,0:T(8,128)(2,1)S(1)}, bf16[128,512]{1,0:T(8,128)(2,1)}, u32[]{:S(2)}) copy-start(bf16[128,512]{1,0:T(8,128)(2,1)} %param.10) | copy-start | bytes 393220
  0.6 20.7 %collective-permute-start.1 = (bf16[32,128,128]{2,1,0:T(8,128)(2,1)}, bf16[32,128,128]{2,1,0:T(8,128)(2,1)S(1)}, u32[]{:S(2)}, u32[]{:S(2)}) collective-permute-start(bf16[32,128,128]{2,1,0:T(8,128)(2,1)} %bitcast.56), channel_id=1, source_target_pairs={{0,1},{1,0},{2,3},{3,2},{4,5},{5,4},{6,7},{7,6},{8,9},{9,8},{10,11... | collective-permute-start | bytes 3145736 | tf_op jit(solution)/shard_map/ppermute | solution.py:111
  16.3 5.1 %copy-start = (bf16[1,32,128,128]{3,2,1,0:T(8,128)(2,1)S(1)}, bf16[1,32,128,128]{3,2,1,0:T(8,128)(2,1)}, u32[]{:S(2)}) copy-start(bf16[1,32,128,128]{3,2,1,0:T(8,128)(2,1)} %param.11) | copy-start | bytes 3145732
  16.3 5.1 %copy-start.4 = (s32[2,1,1]{0,2,1:T(1,128)S(1)}, s32[2,1,1]{0,2,1:T(1,128)}, u32[]{:S(2)}) copy-start(s32[2,1,1]{0,2,1:T(1,128)} %constant.21.clone) | copy-start | bytes 28
  17.6 3.7 %collective-permute-start = (bf16[912,256]{1,0:T(8,128)(2,1)S(1)}, bf16[912,256]{1,0:T(8,128)(2,1)S(1)}, u32[]{:S(2)}, u32[]{:S(2)}) collective-permute-start(bf16[912,256]{1,0:T(8,128)(2,1)S(1)} %pad_maximum_fusion.1), channel_id=1, source_target_pairs={{0,1},{1,0},{2,3},{3,2},{4,5},{5,4},{6,7},{7,6},{8,9},{9,8},{10,11... | collective-permute-start | bytes 1400840 | tf_op jit(solution)/shard_map/ppermute | solution.py:111
  21.8 9.7 %all-to-all-start = ((bf16[4,192,256]{2,1,0:T(8,128)(2,1)}), bf16[4,192,256]{2,1,0:T(8,128)(2,1)S(1)}, u32[]{:S(2)}, u32[]{:S(2)}) async-start(bf16[4,192,256]{2,1,0:T(8,128)(2,1)} %bitcast.3), calls=%async_computation | async-start | bytes 786432 | tf_op jit(solution)/shard_map/cond/branch_0_fun/all_to_all | solution.py:114
  41.8 26.0 %all-to-all-start.2 = ((bf16[12,128,256]{2,1,0:T(8,128)(2,1)}), bf16[12,128,256]{2,1,0:T(8,128)(2,1)S(1)}, u32[]{:S(2)}, u32[]{:S(2)}) async-start(bf16[12,128,256]{2,1,0:T(8,128)(2,1)} %bitcast.60), calls=%async_computation.2 | async-start | bytes 1572864 | tf_op jit(solution)/shard_map/cond/branch_0_fun/all_to_all | solution.py:114
  95.8 30.2 %all-to-all-start.6 = ((bf16[48,32,256]{2,1,0:T(8,128)(2,1)}), bf16[48,32,256]{2,1,0:T(8,128)(2,1)S(1)}, u32[]{:S(2)}, u32[]{:S(2)}) async-start(bf16[48,32,256]{2,1,0:T(8,128)(2,1)} %bitcast.64), calls=%async_computation.6 | async-start | bytes 1572864 | tf_op jit(solution)/shard_map/all_to_all | solution.py:114
  156.5 3.2 %collective-permute-start.2 = (bf16[2,128,256]{2,1,0:T(8,128)(2,1)S(1)}, bf16[2,128,256]{2,1,0:T(8,128)(2,1)S(1)}, u32[]{:S(2)}, u32[]{:S(2)}) collective-permute-start(bf16[2,128,256]{2,1,0:T(8,128)(2,1)S(1)} %pad_maximum_fusion.2), channel_id=1, source_target_pairs={{0,1},{1,0},{2,3},{3,2},{4,5},{5,4},{6,7},{7,6},{8,9},{9,8},{10,11... | collective-permute-start | bytes 393224 | tf_op jit(solution)/shard_map/ppermute | solution.py:111

commit v7 on v4

v7 whole, which is shorter than its diff:
```python
import functools

import jax
import jax.numpy as jnp
from jax import lax
from jax.experimental import pallas as pl
from jax.experimental.pallas import tpu as pltpu
from jax.sharding import Mesh, PartitionSpec as P

GRP = 16
PAIR = [(0, 1), (1, 0)]
VMEM_BYTES = 16 * 1024 * 1024


def product_kernel(slots, cap, fields, meta_ref, own_ref, other_ref, *refs):
    starts = fields
    field, fetched = refs[: len(starts)], refs[len(starts) : -3]
    out_ref, total, space = refs[-3:]
    tile = own_ref.shape[1]
    tiles = space.shape[0] // 2
    for side in range(2):
        if len(field) == 2:
            space[side * tiles] = field[side][pl.ds(starts[side], tile), :]
        else:
            space[side * tiles] = field[0][pl.ds(side * tile, tile), :]
        for t in range(tiles - 1):
            if len(fetched) == 2:
                space[side * tiles + 1 + t] = fetched[side][pl.ds(t * tile, tile), :]
                continue
            for place in range(tile // cap):
                source = 2 * (t * (tile // cap) + place) + side
                space[side * tiles + 1 + t, pl.ds(place * cap, cap), :] = fetched[0][
                    pl.ds(source * cap, cap), :
                ]
    total[...] = jnp.zeros_like(total)
    for side, ref in enumerate((own_ref, other_ref)):
        count = meta_ref[side, 2 * slots]

        def group(index, carry, side=side, ref=ref, count=count):
            products = []
            for step in range(GRP):
                k = index * GRP + step
                held = jnp.where(k < count, ref[k], jnp.zeros((tile, tile), ref.dtype))
                source = space[side * tiles + meta_ref[side, slots + k]]
                product = jnp.dot(held, source, preferred_element_type=jnp.float32)
                products.append((meta_ref[side, k], product))
            for row, product in products:
                total[row] += product
            return carry

        lax.fori_loop(0, (count + GRP - 1) // GRP, group, 0)
    for row in range(total.shape[0]):
        out_ref[pl.ds(row * tile, tile), :] = total[row].astype(out_ref.dtype)


def product(meta, own, other, field, starts, fetched, slab_tiles, cap):
    slots, tile = own.shape[0], own.shape[1]
    width = field[0].shape[1]
    tiles = 2 + sum(v.shape[0] for v in fetched) // tile
    anywhere = pl.BlockSpec(memory_space=pltpu.VMEM)
    return pl.pallas_call(
        functools.partial(product_kernel, slots, cap, starts),
        out_shape=jax.ShapeDtypeStruct((slab_tiles * tile, width), jnp.bfloat16),
        in_specs=[pl.BlockSpec(memory_space=pltpu.SMEM)] + [anywhere] * (2 + len(field) + len(fetched)),
        out_specs=anywhere,
        scratch_shapes=[
            pltpu.VMEM((slab_tiles, tile, width), jnp.float32),
            pltpu.VMEM((tiles, tile, width), jnp.bfloat16),
        ],
        compiler_params=pltpu.CompilerParams(vmem_limit_bytes=VMEM_BYTES),
        cost_estimate=pl.CostEstimate(
            flops=4 * slots * tile * tile * width,
            bytes_accessed=2 * (2 * slots * tile * tile + (tiles + slab_tiles) * tile * width),
            transcendentals=0,
        ),
    )(meta, own, other, *field, *fetched)


def mix_kernel(cap, mine_ref, given_ref, out_ref):
    for owner in range(mine_ref.shape[0] // cap):
        rows = pl.ds(owner * cap, cap)
        out_ref[pl.ds(2 * owner * cap, cap), :] = mine_ref[rows, :]
        out_ref[pl.ds((2 * owner + 1) * cap, cap), :] = given_ref[rows, :]


def mix(mine, given, cap):
    anywhere = pl.BlockSpec(memory_space=pltpu.VMEM)
    return pl.pallas_call(
        functools.partial(mix_kernel, cap),
        out_shape=jax.ShapeDtypeStruct((2 * mine.shape[0], mine.shape[1]), mine.dtype),
        in_specs=[anywhere, anywhere],
        out_specs=anywhere,
        compiler_params=pltpu.CompilerParams(vmem_limit_bytes=VMEM_BYTES),
    )(mine, given)


def pick_kernel(core_ref, features_ref, lists_ref, rows_ref, cols_ref, count_ref, mine_ref, sent_ref, chosen, numbers):
    cap, owners = lists_ref.shape
    rows, half = features_ref.shape[0], mine_ref.shape[1]
    place = lax.broadcasted_iota(jnp.int32, (cap, rows), 1)
    for owner in range(owners):
        wanted = lists_ref[:, pl.ds(owner, 1)]
        chosen[pl.ds(owner * cap, cap), :] = jnp.where(wanted == place, 1.0, 0.0).astype(chosen.dtype)
    core = core_ref[0]
    mine = features_ref[:, pl.ds(pl.multiple_of(core * half, half), half)]
    theirs = features_ref[:, pl.ds(pl.multiple_of((1 - core) * half, half), half)]
    ends = mine_ref.shape[0], mine_ref.shape[0] + rows
    sent_ref[pl.ds(0, ends[0]), :] = jnp.dot(
        chosen[...], theirs, preferred_element_type=jnp.float32
    ).astype(sent_ref.dtype)
    sent_ref[pl.ds(ends[0], rows), :] = theirs
    numbers[...] = jnp.zeros_like(numbers)
    numbers[:, pl.ds(0, owners)] = lists_ref[...]
    slots = rows_ref.shape[1]
    numbers[pl.ds(0, 1), pl.ds(rows, slots)] = rows_ref[...]
    numbers[pl.ds(1, 1), pl.ds(rows, slots)] = cols_ref[...]
    numbers[pl.ds(2, 1), pl.ds(rows, 1)] = count_ref[...]
    sent_ref[pl.ds(ends[1], cap), :] = numbers[...].astype(jnp.float32).astype(sent_ref.dtype)
    mine_ref[...] = jnp.dot(chosen[...], mine, preferred_element_type=jnp.float32).astype(mine_ref.dtype)


def pick_own(core, features, lists, block_rows, block_cols, block_count):
    cap, owners = lists.shape
    rows, half = features.shape[0], features.shape[1] // 2
    anywhere = pl.BlockSpec(memory_space=pltpu.VMEM)
    return pl.pallas_call(
        pick_kernel,
        out_shape=(
            jax.ShapeDtypeStruct((owners * cap, half), features.dtype),
            jax.ShapeDtypeStruct((owners * cap + rows + cap, half), features.dtype),
        ),
        in_specs=[pl.BlockSpec(memory_space=pltpu.SMEM)] + [anywhere] * 5,
        out_specs=(anywhere, anywhere),
        scratch_shapes=[
            pltpu.VMEM((owners * cap, rows), jnp.bfloat16),
            pltpu.VMEM((cap, half), jnp.int32),
        ],
        compiler_params=pltpu.CompilerParams(vmem_limit_bytes=VMEM_BYTES),
    )(core.reshape(1), features, lists, block_rows, block_cols, block_count)


def one_hot(wanted, extent):
    place = lax.broadcasted_iota(jnp.int32, (1, extent), 1)
    return (wanted.reshape(-1, 1) == place).astype(jnp.bfloat16)


def on_device(features, blocks, block_rows, block_cols, block_count, send_rows):
    held = blocks[0]
    slots, tile = held.shape[0], held.shape[1]
    rows, width = features.shape
    half = width // 2
    cap = send_rows.shape[2]
    owners = lax.axis_size("rows")
    slab_tiles = 2 * lax.axis_size("y")
    core = lax.axis_index("core")

    def swap(value):
        return lax.ppermute(value, "core", PAIR)

    def exchange(picked):
        got = lax.all_to_all(picked.reshape(owners, -1, half), "rows", 0, 0, tiled=True)
        return got.reshape(-1, half)

    def pick(chosen, field):
        return jnp.dot(chosen, field, preferred_element_type=jnp.bfloat16)

    other_held = swap(held)
    lists = send_rows[0].T
    picked, sent = pick_own(core, features, lists, block_rows, block_cols, block_count)
    given = swap(sent)
    mine = jnp.where(core == 0, features[:, :half], features[:, half:])
    ends = owners * cap, owners * cap + rows

    def places(given):
        numbers = given[ends[1] :].astype(jnp.int32)
        other = [numbers[:1, rows : rows + slots], numbers[1:2, rows : rows + slots], numbers[2:3, rows : rows + 1]]
        meta = jnp.concatenate([jnp.concatenate([block_rows, block_cols, block_count], 1), jnp.concatenate(other, 1)], 0)
        is_row = lax.broadcasted_iota(jnp.int32, meta.shape, 1) < slots
        meta = jnp.where(is_row, meta ^ core, meta)
        wanted = jnp.stack([lists, numbers[:, :owners] + rows])
        return meta, wanted.transpose(2, 0, 1).reshape(-1)

    def multiply(field, starts, fetched, meta, held, other_held):
        partial_value = product(meta, held, other_held, field, starts, fetched, slab_tiles, cap)
        return partial_value.reshape(-1, 2 * rows, half)

    def combine(partial_value):
        parts = lax.all_to_all(partial_value, "y", 0, 0, tiled=True)
        return jnp.sum(parts.astype(jnp.float32), 0).astype(jnp.bfloat16)

    def in_one(operands):
        mine, picked, given, *tiles = operands
        meta, wanted = places(given)
        meta, wanted, picked, given, mine = lax.optimization_barrier((meta, wanted, picked, given, mine))
        fetched = exchange(mix(picked, given, cap))
        partial_value = multiply((mine, given), (0, ends[0]), (fetched,), meta, *tiles)
        return combine(partial_value), meta, wanted

    def in_two(operands):
        mine, picked, given, *tiles = operands
        meta, wanted = places(given)
        pieces = exchange(picked), exchange(given[: ends[0]])
        partial_value = multiply((mine, given), (0, ends[0]), pieces, meta, *tiles)
        partial_value, wanted = lax.optimization_barrier((partial_value, wanted))
        return combine(partial_value), meta, wanted

    first, meta, wanted = lax.optimization_barrier(
        lax.cond(core == 0, in_one, in_two, (mine, picked, given, held, other_held))
    )
    fetched = exchange(pick(one_hot(wanted, 2 * rows), first))
    partial_value = multiply((first,), (0,), (fetched,), meta, held, other_held)
    partial_value, first_back = lax.optimization_barrier((partial_value, first[rows:]))
    second = combine(partial_value)
    others = swap(jnp.stack([first_back, second[rows:]])).reshape(2 * rows, half)

    def whole(kept, other):
        return jnp.concatenate(
            [jnp.where(core == 0, kept, other), jnp.where(core == 0, other, kept)], 1
        )

    return (whole(first[:rows], others[:rows]), whole(second[:rows], others[rows:]))


def solution(mesh):
    inner = Mesh(
        mesh.devices.reshape(mesh.shape["rows"], -1, 2), ("rows", "y", "core")
    )
    cols = ("y", "core")
    placed = (
        P(("rows", "y", "core"), None),
        P("rows", cols, None, None),
        P("rows", cols),
        P("rows", cols),
        P("rows", cols),
        P("rows", cols, None),
    )
    return jax.shard_map(
        on_device,
        mesh=inner,
        in_specs=placed,
        out_specs=(P(("rows", "y", "core"), None), P(("rows", "y", "core"), None)),
        check_vma=False,
    )
```

time: 159 us -> 169 us (1.063)
  blocking collectives: 27.7 us -> 55.8 us
  waiting for transfers between devices: 67.1 us -> 57.8 us
  starting transfers between devices: 46.8 us -> 38.7 us
    all_to_all x2 -> x0, waiting for transfers between devices: 34.6 us -> none  [multiply(): lax.all_to_all(partial_value.reshape(-1, 2 * rows, half), 'y', 0, 0, tile...]
    all_to_all x1 -> x2, blocking collectives: 27.7 us -> 55.8 us  [combine(): parts = lax.all_to_all(partial_value, 'y', 0, 0, tiled=True)]
    all_to_all x2 -> x3, waiting for transfers between devices: 30.5 us -> 55.6 us  [exchange(): lax.all_to_all(picked.reshape(owners, -1, half), 'rows', 0, 0, tiled=True)]
    all_to_all x2 -> x0, starting transfers between devices: 10.4 us -> none  [multiply(): lax.all_to_all(partial_value.reshape(-1, 2 * rows, half), 'y', 0, 0, tile...]
    all_to_all x2 -> x3, starting transfers between devices: 20 us -> 22.4 us  [exchange(): lax.all_to_all(picked.reshape(owners, -1, half), 'rows', 0, 0, tiled=True)]
    pallas_call x2 -> x3, Pallas kernels: 6.4 us -> 7.63 us  [the longest x2 5.71 us: product(): pl.pallas_call(functools.partial(product_kernel, slots, cap, starts), out...]
  transfers between devices with their start and end apart: 7 -> 6, of which waited for: 6 -> 5; matrix products, arithmetic and copies ran while one was open for 4% -> 2% of each run, Pallas kernels for 0% -> 1%
where the time goes in v7:
time: 169 us; the launch traced here: 168 us
  waiting for transfers between devices  57.8 us (34%)
  blocking collectives  55.8 us (33%)
  starting transfers between devices  38.7 us (23%)
  Pallas kernels  7.63 us (5%)
  other arithmetic  3.32 us (2%)
  local copies, waits for them, and re-layouts  2.44 us (1%)
    all_to_all x2, blocking collectives, combine(): parts = lax.all_to_all(partial_value, 'y', 0, 0, tiled=True)  55.8 us
    all_to_all x3, waiting for transfers between devices, exchange(): lax.all_to_all(picked.reshape(owners, -1, half), 'rows', 0, 0, tiled=True)  55.6 us
    all_to_all x3, starting transfers between devices, exchange(): lax.all_to_all(picked.reshape(owners, -1, half), 'rows', 0, 0, tiled=True)  22.4 us
    ppermute x3, starting transfers between devices, swap(): return lax.ppermute(value, 'core', PAIR)  16.3 us
    pallas_call x2, Pallas kernels, product(): pl.pallas_call(functools.partial(product_kernel, slots, cap, starts), out...  5.71 us
  transfers between devices with their start and end apart: 6, of which 5 were waited for; matrix products, arithmetic and copies ran while one was open for 2% of the time, Pallas kernels for 1%

profile of v7, /device:TPU:1, one launch (start us, length us, event | category | flops | bytes accessed | tf_op | source)
XLA Modules:
  0.0 168.5 jit_solution(3495163482218345562)
XLA Ops:
  0.6 12.4 %collective-permute-start.1 = (bf16[32,128,128]{2,1,0:T(8,128)(2,1)}, bf16[32,128,128]{2,1,0:T(8,128)(2,1)}, u32[]{:S(2)}, u32[]{:S(2)}) collective-permute-start(bf16[32,128,128]{2,1,0:T(8,128)(2,1)} %bitcast.50), channel_id=1, source_target_pairs={{0,1},{1,0},{2,3},{3,2},{4,5},{5,4},{6,7},{7,6},{8,9},{9,8},{10,11... | collective-permute-start | bytes 3145736 | tf_op jit(solution)/shard_map/ppermute | solution.py:158
  13.7 0.9 copy-done
  14.6 1.9 %shard_map.77 = (bf16[768,256]{1,0:T(8,128)(2,1)}, bf16[912,256]{1,0:T(8,128)(2,1)S(1)}) custom-call(s32[1]{0:T(128)} %bitcast.14.core_ref, bf16[128,512]{1,0:T(8,128)(2,1)S(1)} %copy-done, s32[16,48]{1,0:T(8,128)} %bitcast.55, s32[1,32]{1,0:T(1,128)} %rows_ref.1, s32[1,32]{1,0:T(1,128)} %cols_ref.1, s32[1,1]{1,0:T(1,128)S(6)} %copy.16.count_ref), custom_call_target="tpu_custom_call" | custom-call | tf_op jit(solution)/shard_map/pallas_call | solution.py:126
  16.5 1.9 %collective-permute-start = (bf16[912,256]{1,0:T(8,128)(2,1)S(1)}, bf16[912,256]{1,0:T(8,128)(2,1)S(1)}, u32[]{:S(2)}, u32[]{:S(2)}) collective-permute-start(bf16[912,256]{1,0:T(8,128)(2,1)S(1)} %get-tuple-element.76), channel_id=1, source_target_pairs={{0,1},{1,0},{2,3},{3,2},{4,5},{5,4},{6,7},{7,6},{8,9},{9,8},{10,11... | collective-permute-start | bytes 1400840 | tf_op jit(solution)/shard_map/ppermute | solution.py:158
  18.5 0.9 slice_select_fusion
  19.3 0.9 collective-permute-done
  20.3 76.6 %conditional.1 = (bf16[256,256]{1,0:T(8,128)(2,1)S(1)}, s32[2,65]{1,0:T(2,128)S(1)}, s32[1536]{0:T(1024)S(1)}) conditional(s32[]{:T(128)} %convert_element_type.9, (s32[1,32]{1,0:T(1,128)}, s32[1,32]{1,0:T(1,128)}, s32[1,1]{1,0:T(1,128)}, bf16[912,256]{1,0:T(8,128)(2,1)S(1)}, s32[]{:T(128)}, /*index=5*/bf16[768,256]{1,0:T(8,128)(2,1)}, ...), branch_computations={%region_0.2_spmd, %region_2.4_spmd} | conditional | flops 537337024 | bytes 14762856 | solution.py:208
  20.3 9.1 %all-to-all-start = ((bf16[48,16,256]{2,1,0:T(8,128)(2,1)}), bf16[48,16,256]{2,1,0:T(8,128)(2,1)S(1)}, u32[]{:S(2)}, u32[]{:S(2)}) async-start(bf16[48,16,256]{2,1,0:T(8,128)(2,1)} %bitcast), calls=%async_computation | async-start | bytes 786432 | tf_op jit(solution)/shard_map/cond/branch_0_fun/all_to_all | solution.py:161
  29.4 0.8 slice.46
  30.2 14.6 %all-to-all-done = bf16[48,16,256]{2,1,0:T(8,128)(2,1)S(1)} async-done(((bf16[48,16,256]{2,1,0:T(8,128)(2,1)}), bf16[48,16,256]{2,1,0:T(8,128)(2,1)S(1)}, u32[]{:S(2)}, u32[]{:S(2)}) %all-to-all-start) | async-done | bytes 393248 | tf_op jit(solution)/shard_map/cond/branch_0_fun/all_to_all | solution.py:161
  44.8 7.4 %all-to-all-start.1 = ((bf16[48,16,256]{2,1,0:T(8,128)(2,1)}), bf16[48,16,256]{2,1,0:T(8,128)(2,1)S(1)}, u32[]{:S(2)}, u32[]{:S(2)}) async-start(bf16[48,16,256]{2,1,0:T(8,128)(2,1)} %bitcast.2), calls=%async_computation.1 | async-start | bytes 786432 | tf_op jit(solution)/shard_map/cond/branch_0_fun/all_to_all | solution.py:161
  52.2 0.5 slice.75
  53.0 1.4 xor_select_fusion.meta_ref
  54.4 13.2 %all-to-all-done.1 = bf16[48,16,256]{2,1,0:T(8,128)(2,1)S(1)} async-done(((bf16[48,16,256]{2,1,0:T(8,128)(2,1)}), bf16[48,16,256]{2,1,0:T(8,128)(2,1)S(1)}, u32[]{:S(2)}, u32[]{:S(2)}) %all-to-all-start.1) | async-done | bytes 393248 | tf_op jit(solution)/shard_map/cond/branch_0_fun/all_to_all | solution.py:161
  67.5 2.9 %branch_0_fun.1 = bf16[2048,256]{1,0:T(8,128)(2,1)S(1)} custom-call(s32[2,65]{1,0:T(2,128)S(1)} %xor_select_fusion.meta_ref, bf16[32,128,128]{2,1,0:T(8,128)(2,1)S(1)} %copy-done.2, bf16[32,128,128]{2,1,0:T(8,128)(2,1)} %get-tuple-element.46.other_ref, bf16[128,256]{1,0:T(8,128)(2,1)S(1)} %get-tuple-element.47.refs_0_, ...), custom_call_target="tpu_custom_call" | custom-call | flops 536870912 | bytes 4063232 | tf_op jit(solution)/shard_map/cond/branch_0_fun/pallas_call | solution.py:61
  70.4 26.4 %all_to_all.30 = bf16[8,256,256]{2,1,0:T(8,128)(2,1)S(1)} all-to-all(bf16[8,256,256]{2,1,0:T(8,128)(2,1)S(1)} %bitcast.43), channel_id=1, replica_groups=mesh['rows'=48,'y'=8,'core'=2] {'y'}, dimensions={0} | all-to-all | bytes 2097152 | tf_op jit(solution)/shard_map/cond/branch_0_fun/all_to_all | solution.py:188
  96.9 1.4 fusion.2
  98.3 5.8 %all-to-all-start.5 = ((bf16[48,32,256]{2,1,0:T(8,128)(2,1)}), bf16[48,32,256]{2,1,0:T(8,128)(2,1)S(1)}, u32[]{:S(2)}, u32[]{:S(2)}) async-start(bf16[48,32,256]{2,1,0:T(8,128)(2,1)} %bitcast.19), calls=%async_computation.5 | async-start | bytes 1572864 | tf_op jit(solution)/shard_map/all_to_all | solution.py:161
  104.1 27.8 %all-to-all-done.5 = bf16[48,32,256]{2,1,0:T(8,128)(2,1)S(1)} async-done(((bf16[48,32,256]{2,1,0:T(8,128)(2,1)}), bf16[48,32,256]{2,1,0:T(8,128)(2,1)S(1)}, u32[]{:S(2)}, u32[]{:S(2)}) %all-to-all-start.5) | async-done | bytes 786464 | tf_op jit(solution)/shard_map/all_to_all | solution.py:161
  132.0 2.9 %shard_map.78 = bf16[2048,256]{1,0:T(8,128)(2,1)S(1)} custom-call(s32[2,65]{1,0:T(2,128)S(1)} %get-tuple-element.79.meta_ref, bf16[32,128,128]{2,1,0:T(8,128)(2,1)S(1)} %bitcast.53, bf16[32,128,128]{2,1,0:T(8,128)(2,1)} %collective-permute-done.1.other_ref, bf16[256,256]{1,0:T(8,128)(2,1)S(1)} %get-tuple-element.78.refs_0_, bf16[1536,256]{1,0:T(8,128)(2,1)S(1)} %bitcast.45), custom_call_target="tpu_custom_call" | custom-call | flops 536870912 | bytes 4063232 | tf_op jit(solution)/shard_map/pallas_call | solution.py:61
  134.8 29.5 %all_to_all.33 = bf16[8,256,256]{2,1,0:T(8,128)(2,1)S(1)} all-to-all(bf16[8,256,256]{2,1,0:T(8,128)(2,1)S(1)} %bitcast.42), channel_id=1, replica_groups=mesh['rows'=48,'y'=8,'core'=2] {'y'}, dimensions={0} | all-to-all | bytes 2097152 | tf_op jit(solution)/shard_map/all_to_all | solution.py:188
  164.5 1.9 %collective-permute-start.2 = (bf16[2,128,256]{2,1,0:T(8,128)(2,1)S(1)}, bf16[2,128,256]{2,1,0:T(8,128)(2,1)S(1)}, u32[]{:S(2)}, u32[]{:S(2)}) collective-permute-start(bf16[2,128,256]{2,1,0:T(8,128)(2,1)S(1)} %pad_maximum_fusion), channel_id=1, source_target_pairs={{0,1},{1,0},{2,3},{3,2},{4,5},{5,4},{6,7},{7,6},{8,9},{9,8},{10,11... | collective-permute-start | bytes 393224 | tf_op jit(solution)/shard_map/ppermute | solution.py:158
  166.4 1.3 collective-permute-done.2
  167.8 0.7 pad_maximum_fusion.1
  (25 shorter events, 0.6 us)
Async XLA Ops:
  0.6 19.6 %collective-permute-start.1 = (bf16[32,128,128]{2,1,0:T(8,128)(2,1)}, bf16[32,128,128]{2,1,0:T(8,128)(2,1)}, u32[]{:S(2)}, u32[]{:S(2)}) collective-permute-start(bf16[32,128,128]{2,1,0:T(8,128)(2,1)} %bitcast.50), channel_id=1, source_target_pairs={{0,1},{1,0},{2,3},{3,2},{4,5},{5,4},{6,7},{7,6},{8,9},{9,8},{10,11... | collective-permute-start | bytes 3145736 | tf_op jit(solution)/shard_map/ppermute | solution.py:158
  13.7 0.9 copy-start
  16.5 3.7 %collective-permute-start = (bf16[912,256]{1,0:T(8,128)(2,1)S(1)}, bf16[912,256]{1,0:T(8,128)(2,1)S(1)}, u32[]{:S(2)}, u32[]{:S(2)}) collective-permute-start(bf16[912,256]{1,0:T(8,128)(2,1)S(1)} %get-tuple-element.76), channel_id=1, source_target_pairs={{0,1},{1,0},{2,3},{3,2},{4,5},{5,4},{6,7},{7,6},{8,9},{9,8},{10,11... | collective-permute-start | bytes 1400840 | tf_op jit(solution)/shard_map/ppermute | solution.py:158
  20.3 32.5 %copy-start.4 = (s32[16,48]{1,0:T(8,128)S(1)}, s32[16,48]{1,0:T(8,128)}, u32[]{:S(2)}) copy-start(s32[16,48]{1,0:T(8,128)} %get-tuple-element.49) | copy-start | bytes 9220 | tf_op jit(solution)/shard_map/cond
  20.3 24.5 %all-to-all-start = ((bf16[48,16,256]{2,1,0:T(8,128)(2,1)}), bf16[48,16,256]{2,1,0:T(8,128)(2,1)S(1)}, u32[]{:S(2)}, u32[]{:S(2)}) async-start(bf16[48,16,256]{2,1,0:T(8,128)(2,1)} %bitcast), calls=%async_computation | async-start | bytes 786432 | tf_op jit(solution)/shard_map/cond/branch_0_fun/all_to_all | solution.py:161
  29.4 23.6 %copy-start.7 = (s32[1,32]{1,0:T(1,128)S(1)}, s32[1,32]{1,0:T(1,128)}, u32[]{:S(2)}) copy-start(s32[1,32]{1,0:T(1,128)} %get-tuple-element.40) | copy-start | bytes 388 | tf_op jit(solution)/shard_map/cond
  29.4 23.6 %copy-start.8 = (s32[1,32]{1,0:T(1,128)S(1)}, s32[1,32]{1,0:T(1,128)}, u32[]{:S(2)}) copy-start(s32[1,32]{1,0:T(1,128)} %get-tuple-element.41) | copy-start | bytes 388 | tf_op jit(solution)/shard_map/cond
  29.4 38.1 %copy-start.2 = (bf16[32,128,128]{2,1,0:T(8,128)(2,1)S(1)}, bf16[32,128,128]{2,1,0:T(8,128)(2,1)}, u32[]{:S(2)}) copy-start(bf16[32,128,128]{2,1,0:T(8,128)(2,1)} %get-tuple-element.45.own_ref) | copy-start | bytes 3145732 | tf_op jit(solution)/shard_map/cond
  44.8 22.8 %all-to-all-start.1 = ((bf16[48,16,256]{2,1,0:T(8,128)(2,1)}), bf16[48,16,256]{2,1,0:T(8,128)(2,1)S(1)}, u32[]{:S(2)}, u32[]{:S(2)}) async-start(bf16[48,16,256]{2,1,0:T(8,128)(2,1)} %bitcast.2), calls=%async_computation.1 | async-start | bytes 786432 | tf_op jit(solution)/shard_map/cond/branch_0_fun/all_to_all | solution.py:161
  98.3 33.7 %copy-start.1 = (bf16[1,32,128,128]{3,2,1,0:T(8,128)(2,1)S(1)}, bf16[1,32,128,128]{3,2,1,0:T(8,128)(2,1)}, u32[]{:S(2)}) copy-start(bf16[1,32,128,128]{3,2,1,0:T(8,128)(2,1)} %param.9) | copy-start | bytes 3145732
  98.3 33.7 %all-to-all-start.5 = ((bf16[48,32,256]{2,1,0:T(8,128)(2,1)}), bf16[48,32,256]{2,1,0:T(8,128)(2,1)S(1)}, u32[]{:S(2)}, u32[]{:S(2)}) async-start(bf16[48,32,256]{2,1,0:T(8,128)(2,1)} %bitcast.19), calls=%async_computation.5 | async-start | bytes 1572864 | tf_op jit(solution)/shard_map/all_to_all | solution.py:161
  164.5 3.2 %collective-permute-start.2 = (bf16[2,128,256]{2,1,0:T(8,128)(2,1)S(1)}, bf16[2,128,256]{2,1,0:T(8,128)(2,1)S(1)}, u32[]{:S(2)}, u32[]{:S(2)}) collective-permute-start(bf16[2,128,256]{2,1,0:T(8,128)(2,1)S(1)} %pad_maximum_fusion), channel_id=1, source_target_pairs={{0,1},{1,0},{2,3},{3,2},{4,5},{5,4},{6,7},{7,6},{8,9},{9,8},{10,11... | collective-permute-start | bytes 393224 | tf_op jit(solution)/shard_map/ppermute | solution.py:158

commit v8 on v7

--- a/solution.py
+++ b/solution.py
@@ -8,14 +8,14 @@
 from jax.sharding import Mesh, PartitionSpec as P
 
 GRP = 16
+ALONG_X = 4
 PAIR = [(0, 1), (1, 0)]
 VMEM_BYTES = 16 * 1024 * 1024
 
 
-def product_kernel(slots, cap, fields, meta_ref, own_ref, other_ref, *refs):
-    starts = fields
-    field, fetched = refs[: len(starts)], refs[len(starts) : -3]
-    out_ref, total, space = refs[-3:]
+def product_kernel(slots, cap, starts, order, meta_ref, own_ref, other_ref, *refs):
+    field = refs[: len(starts)]
+    fetched, out_ref, total, space = refs[len(starts) :]
     tile = own_ref.shape[1]
     tiles = space.shape[0] // 2
     for side in range(2):
@@ -24,12 +24,9 @@
         else:
             space[side * tiles] = field[0][pl.ds(side * tile, tile), :]
         for t in range(tiles - 1):
-            if len(fetched) == 2:
-                space[side * tiles + 1 + t] = fetched[side][pl.ds(t * tile, tile), :]
-                continue
             for place in range(tile // cap):
-                source = 2 * (t * (tile // cap) + place) + side
-                space[side * tiles + 1 + t, pl.ds(place * cap, cap), :] = fetched[0][
+                source = 2 * order[t * (tile // cap) + place] + side
+                space[side * tiles + 1 + t, pl.ds(place * cap, cap), :] = fetched[
                     pl.ds(source * cap, cap), :
                 ]
     total[...] = jnp.zeros_like(total)
@@ -53,15 +50,15 @@
         out_ref[pl.ds(row * tile, tile), :] = total[row].astype(out_ref.dtype)
 
 
-def product(meta, own, other, field, starts, fetched, slab_tiles, cap):
+def product(meta, own, other, field, starts, fetched, order, slab_tiles, cap):
     slots, tile = own.shape[0], own.shape[1]
     width = field[0].shape[1]
-    tiles = 2 + sum(v.shape[0] for v in fetched) // tile
+    tiles = 2 + fetched.shape[0] // tile
     anywhere = pl.BlockSpec(memory_space=pltpu.VMEM)
     return pl.pallas_call(
-        functools.partial(product_kernel, slots, cap, starts),
+        functools.partial(product_kernel, slots, cap, starts, order),
         out_shape=jax.ShapeDtypeStruct((slab_tiles * tile, width), jnp.bfloat16),
-        in_specs=[pl.BlockSpec(memory_space=pltpu.SMEM)] + [anywhere] * (2 + len(field) + len(fetched)),
+        in_specs=[pl.BlockSpec(memory_space=pltpu.SMEM)] + [anywhere] * (3 + len(field)),
         out_specs=anywhere,
         scratch_shapes=[
             pltpu.VMEM((slab_tiles, tile, width), jnp.float32),
@@ -73,7 +70,7 @@
             bytes_accessed=2 * (2 * slots * tile * tile + (tiles + slab_tiles) * tile * width),
             transcendentals=0,
         ),
-    )(meta, own, other, *field, *fetched)
+    )(meta, own, other, *field, fetched)
 
 
 def mix_kernel(cap, mine_ref, given_ref, out_ref):
@@ -150,15 +147,16 @@
     rows, width = features.shape
     half = width // 2
     cap = send_rows.shape[2]
-    owners = lax.axis_size("rows")
+    along, across = lax.axis_size("x"), lax.axis_size("z")
+    owners = along * across
     slab_tiles = 2 * lax.axis_size("y")
     core = lax.axis_index("core")
 
     def swap(value):
         return lax.ppermute(value, "core", PAIR)
 
-    def exchange(picked):
-        got = lax.all_to_all(picked.reshape(owners, -1, half), "rows", 0, 0, tiled=True)
+    def exchange(picked, axes=("x", "z")):
+        got = lax.all_to_all(picked.reshape(lax.axis_size(axes), -1, half), axes, 0, 0, tiled=True)
         return got.reshape(-1, half)
 
     def pick(chosen, field):
@@ -180,38 +178,42 @@
         wanted = jnp.stack([lists, numbers[:, :owners] + rows])
         return meta, wanted.transpose(2, 0, 1).reshape(-1)
 
-    def multiply(field, starts, fetched, meta, held, other_held):
-        partial_value = product(meta, held, other_held, field, starts, fetched, slab_tiles, cap)
+    def multiply(field, starts, fetched, order, meta, held, other_held):
+        partial_value = product(meta, held, other_held, field, starts, fetched, order, slab_tiles, cap)
         return partial_value.reshape(-1, 2 * rows, half)
 
     def combine(partial_value):
         parts = lax.all_to_all(partial_value, "y", 0, 0, tiled=True)
         return jnp.sum(parts.astype(jnp.float32), 0).astype(jnp.bfloat16)
 
+    straight = tuple(range(owners))
+    turned = tuple(q % across * along + q // across for q in straight)
+
     def in_one(operands):
         mine, picked, given, *tiles = operands
         meta, wanted = places(given)
-        meta, wanted, picked, given, mine = lax.optimization_barrier((meta, wanted, picked, given, mine))
         fetched = exchange(mix(picked, given, cap))
-        partial_value = multiply((mine, given), (0, ends[0]), (fetched,), meta, *tiles)
+        partial_value = multiply((mine, given), (0, ends[0]), fetched, straight, meta, *tiles)
+        partial_value, wanted = lax.optimization_barrier((partial_value, wanted))
         return combine(partial_value), meta, wanted
 
-    def in_two(operands):
+    def in_steps(operands):
         mine, picked, given, *tiles = operands
         meta, wanted = places(given)
-        pieces = exchange(picked), exchange(given[: ends[0]])
-        partial_value = multiply((mine, given), (0, ends[0]), pieces, meta, *tiles)
-        partial_value, wanted = lax.optimization_barrier((partial_value, wanted))
+        meta, wanted, picked, given = lax.optimization_barrier((meta, wanted, picked, given))
+        shape = along, across, cap, half
+        moved = [exchange(v, "x").reshape(shape) for v in (picked, given[: ends[0]])]
+        fetched = exchange(jnp.stack(moved, 2).transpose(1, 0, 2, 3, 4), "z")
+        partial_value = multiply((mine, given), (0, ends[0]), fetched, turned, meta, *tiles)
         return combine(partial_value), meta, wanted
 
     first, meta, wanted = lax.optimization_barrier(
-        lax.cond(core == 0, in_one, in_two, (mine, picked, given, held, other_held))
+        lax.cond(core == 0, in_one, in_steps, (mine, picked, given, held, other_held))
     )
     fetched = exchange(pick(one_hot(wanted, 2 * rows), first))
-    partial_value = multiply((first,), (0,), (fetched,), meta, held, other_held)
-    partial_value, first_back = lax.optimization_barrier((partial_value, first[rows:]))
-    second = combine(partial_value)
-    others = swap(jnp.stack([first_back, second[rows:]])).reshape(2 * rows, half)
+    second = combine(multiply((first,), (0,), fetched, straight, meta, held, other_held))
+    kept_back = lax.optimization_barrier((first, second))
+    others = swap(jnp.stack([v[rows:] for v in kept_back])).reshape(2 * rows, half)
 
     def whole(kept, other):
         return jnp.concatenate(
@@ -223,21 +225,21 @@
 
 def solution(mesh):
     inner = Mesh(
-        mesh.devices.reshape(mesh.shape["rows"], -1, 2), ("rows", "y", "core")
-    )
-    cols = ("y", "core")
+        mesh.devices.reshape(ALONG_X, mesh.shape["rows"] // ALONG_X, -1, 2), ("x", "z", "y", "core")
+    )
+    lines, cols = ("x", "z"), ("y", "core")
     placed = (
-        P(("rows", "y", "core"), None),
-        P("rows", cols, None, None),
-        P("rows", cols),
-        P("rows", cols),
-        P("rows", cols),
-        P("rows", cols, None),
+        P((*lines, *cols), None),
+        P(lines, cols, None, None),
+        P(lines, cols),
+        P(lines, cols),
+        P(lines, cols),
+        P(lines, cols, None),
     )
     return jax.shard_map(
         on_device,
         mesh=inner,
         in_specs=placed,
-        out_specs=(P(("rows", "y", "core"), None), P(("rows", "y", "core"), None)),
+        out_specs=(P((*lines, *cols), None), P((*lines, *cols), None)),
         check_vma=False,
     )

time: 169 us -> 153 us (0.905)
  blocking collectives: 55.8 us -> 107 us
  waiting for transfers between devices: 57.8 us -> 8.38 us
  starting transfers between devices: 38.7 us -> 19.7 us
  other arithmetic: 3.32 us -> 5.38 us
    all_to_all x0 -> x3, blocking collectives: none -> 63.2 us  [exchange(): lax.all_to_all(picked.reshape(lax.axis_size(axes), -1, half), axes, 0, 0,...]
    all_to_all x3 -> x1, waiting for transfers between devices: 55.6 us -> 6.16 us  [exchange(): lax.all_to_all(picked.reshape(lax.axis_size(axes), -1, half), axes, 0, 0,...]
    all_to_all x3 -> x1, starting transfers between devices: 22.4 us -> 3.46 us  [exchange(): lax.all_to_all(picked.reshape(lax.axis_size(axes), -1, half), axes, 0, 0,...]
    all_to_all x2, blocking collectives: 55.8 us -> 44 us  [combine(): parts = lax.all_to_all(partial_value, 'y', 0, 0, tiled=True)]
  transfers between devices with their start and end apart: 6 -> 4, of which waited for: 5 -> 3; matrix products, arithmetic and copies ran while one was open for 2% -> 1% of each run, Pallas kernels for 1% -> 1%
where the time goes in v8:
time: 153 us
  blocking collectives  107 us (70%)
  starting transfers between devices  19.7 us (13%)
  waiting for transfers between devices  8.38 us (5%)
  Pallas kernels  7.12 us (5%)
  other arithmetic  5.38 us (4%)
  local copies, waits for them, and re-layouts  2.37 us (2%)
    all_to_all x3, blocking collectives, exchange(): lax.all_to_all(picked.reshape(lax.axis_size(axes), -1, half), axes, 0, 0,...  63.2 us
    all_to_all x2, blocking collectives, combine(): parts = lax.all_to_all(partial_value, 'y', 0, 0, tiled=True)  44 us
    ppermute x3, starting transfers between devices, swap(): return lax.ppermute(value, 'core', PAIR)  16.3 us
    all_to_all x1, waiting for transfers between devices, exchange(): lax.all_to_all(picked.reshape(lax.axis_size(axes), -1, half), axes, 0, 0,...  6.16 us
    pallas_call x2, Pallas kernels, product(): pl.pallas_call(functools.partial(product_kernel, slots, cap, starts, orde...  5.23 us
    all_to_all x1, starting transfers between devices, exchange(): lax.all_to_all(picked.reshape(lax.axis_size(axes), -1, half), axes, 0, 0,...  3.46 us
  transfers between devices with their start and end apart: 4, of which 3 were waited for; matrix products, arithmetic and copies ran while one was open for 1% of the time, Pallas kernels for 1%

profile of v8, /device:TPU:1, one launch (start us, length us, event | category | flops | bytes accessed | tf_op | source)
XLA Modules:
  0.0 152.8 jit_solution(715553783253558866)
XLA Ops:
  0.6 12.4 %collective-permute-start.1 = (bf16[32,128,128]{2,1,0:T(8,128)(2,1)}, bf16[32,128,128]{2,1,0:T(8,128)(2,1)S(1)}, u32[]{:S(2)}, u32[]{:S(2)}) collective-permute-start(bf16[32,128,128]{2,1,0:T(8,128)(2,1)} %bitcast.53), channel_id=1, source_target_pairs={{0,1},{1,0},{2,3},{3,2},{4,5},{5,4},{6,7},{7,6},{8,9},{9,8},{10,11... | collective-permute-start | bytes 3145736 | tf_op jit(solution)/shard_map/ppermute | solution.py:156
  13.7 0.9 copy-done
  14.6 1.9 %shard_map.77 = (bf16[768,256]{1,0:T(8,128)(2,1)}, bf16[912,256]{1,0:T(8,128)(2,1)S(1)}) custom-call(s32[1]{0:T(128)} %bitcast.17.core_ref, bf16[128,512]{1,0:T(8,128)(2,1)S(1)} %copy-done, s32[16,48]{1,0:T(8,128)} %bitcast.62, s32[1,32]{1,0:T(1,128)} %rows_ref.1, s32[1,32]{1,0:T(1,128)} %cols_ref.1, s32[1,1]{1,0:T(1,128)S(6)} %copy.21.count_ref), custom_call_target="tpu_custom_call" | custom-call | tf_op jit(solution)/shard_map/pallas_call | solution.py:123
  16.5 1.9 %collective-permute-start = (bf16[912,256]{1,0:T(8,128)(2,1)S(1)}, bf16[912,256]{1,0:T(8,128)(2,1)S(1)}, u32[]{:S(2)}, u32[]{:S(2)}) collective-permute-start(bf16[912,256]{1,0:T(8,128)(2,1)S(1)} %get-tuple-element.75), channel_id=1, source_target_pairs={{0,1},{1,0},{2,3},{3,2},{4,5},{5,4},{6,7},{7,6},{8,9},{9,8},{10,11... | collective-permute-start | bytes 1400840 | tf_op jit(solution)/shard_map/ppermute | solution.py:156
  18.4 0.9 slice_select_fusion
  19.3 0.9 collective-permute-done
  20.2 77.2 %conditional.1 = (bf16[256,256]{1,0:T(8,128)(2,1)S(1)}, s32[2,65]{1,0:T(2,128)S(1)}, s32[1536]{0:T(1024)}) conditional(s32[]{:T(128)} %convert_element_type.9, (s32[1,32]{1,0:T(1,128)}, s32[1,32]{1,0:T(1,128)}, s32[1,1]{1,0:T(1,128)}, bf16[912,256]{1,0:T(8,128)(2,1)S(1)}, s32[]{:T(128)}, /*index=5*/s32[16,48]{1,0:T(8,128)}, ...), branch_computations={%region_0.2_spmd, %region_2.4_spmd} | conditional | flops 537730240 | bytes 19074804 | solution.py:211
  20.8 0.7 add_bitcast_fusion
  21.6 0.7 reshape.41
  22.3 2.0 %xor_select_fusion.meta_ref = s32[2,65]{1,0:T(2,128)S(1)} fusion(s32[1,1]{1,0:T(1,128)} %slice.75, s32[1,32]{1,0:T(1,128)S(1)} %get-tuple-element.83, s32[1,32]{1,0:T(1,128)S(1)} %get-tuple-element.82, s32[1,1]{1,0:T(1,128)} %get-tuple-element.42, s32[1,32]{1,0:T(1,128)} %get-tuple-element.41, s32[1,32]{1,0:T(1,128)} %get-tuple-element.40, ...), kind=kLoop, calls=%fused_computation.5 | loop fusion | flops 910 | bytes 1109 | tf_op jit(solution)/shard_map/cond/branch_0_fun/jit(_where)/select_n | solution.py:177
  24.3 3.5 %all-to-all-start = ((bf16[4,192,256]{2,1,0:T(8,128)(2,1)}), bf16[4,192,256]{2,1,0:T(8,128)(2,1)S(1)}, u32[]{:S(2)}, u32[]{:S(2)}) async-start(bf16[4,192,256]{2,1,0:T(8,128)(2,1)} %bitcast.3), calls=%async_computation | async-start | bytes 786432 | tf_op jit(solution)/shard_map/cond/branch_0_fun/all_to_all | solution.py:159
  27.8 6.2 %all-to-all-done = bf16[4,192,256]{2,1,0:T(8,128)(2,1)S(1)} async-done(((bf16[4,192,256]{2,1,0:T(8,128)(2,1)}), bf16[4,192,256]{2,1,0:T(8,128)(2,1)S(1)}, u32[]{:S(2)}, u32[]{:S(2)}) %all-to-all-start) | async-done | bytes 393248 | tf_op jit(solution)/shard_map/cond/branch_0_fun/all_to_all | solution.py:159
  34.0 10.6 %all_to_all.34 = bf16[4,192,256]{2,1,0:T(8,128)(2,1)S(1)} all-to-all(bf16[4,192,256]{2,1,0:T(8,128)(2,1)S(1)} %bitcast.58), channel_id=1, replica_groups=mesh['x'=4,'z'=12,'y'=8,'core'=2] {'x'}, dimensions={0} | all-to-all | bytes 786432 | tf_op jit(solution)/shard_map/cond/branch_0_fun/all_to_all | solution.py:159
  44.8 26.0 %all_to_all.35 = bf16[12,128,256]{2,1,0:T(8,128)(2,1)S(1)} all-to-all(bf16[12,128,256]{2,1,0:T(8,128)(2,1)S(1)} %bitcast.57), channel_id=1, replica_groups=mesh['x'=4,'z'=12,'y'=8,'core'=2] {'z'}, dimensions={0} | all-to-all | bytes 1572864 | tf_op jit(solution)/shard_map/cond/branch_0_fun/all_to_all | solution.py:159
  70.8 2.6 %branch_0_fun.1 = bf16[2048,256]{1,0:T(8,128)(2,1)S(1)} custom-call(s32[2,65]{1,0:T(2,128)S(1)} %xor_select_fusion.meta_ref, bf16[32,128,128]{2,1,0:T(8,128)(2,1)S(1)} %copy-done.2, bf16[32,128,128]{2,1,0:T(8,128)(2,1)S(1)} %get-tuple-element.49.other_ref, bf16[128,256]{1,0:T(8,128)(2,1)S(1)} %get-tuple-element.50.refs_0_, ...), custom_call_target="tpu_custom_call" | custom-call | flops 536870912 | bytes 4063232 | tf_op jit(solution)/shard_map/cond/branch_0_fun/pallas_call | solution.py:58
  73.4 23.8 %all_to_all.36 = bf16[8,256,256]{2,1,0:T(8,128)(2,1)S(1)} all-to-all(bf16[8,256,256]{2,1,0:T(8,128)(2,1)S(1)} %bitcast.48), channel_id=1, replica_groups=mesh['x'=4,'z'=12,'y'=8,'core'=2] {'y'}, dimensions={0} | all-to-all | bytes 2097152 | tf_op jit(solution)/shard_map/cond/branch_0_fun/all_to_all | solution.py:186
  97.4 1.2 fusion.2
  98.6 26.6 %all_to_all.38 = bf16[48,32,256]{2,1,0:T(8,128)(2,1)S(1)} all-to-all(bf16[48,32,256]{2,1,0:T(8,128)(2,1)S(1)} %bitcast.61), channel_id=1, replica_groups=mesh['x'=4,'z'=12,'y'=8,'core'=2] {'x','z'}, dimensions={0} | all-to-all | bytes 1572864 | tf_op jit(solution)/shard_map/all_to_all | solution.py:159
  125.2 2.6 %shard_map.78 = bf16[2048,256]{1,0:T(8,128)(2,1)S(1)} custom-call(s32[2,65]{1,0:T(2,128)S(1)} %get-tuple-element.78.meta_ref, bf16[32,128,128]{2,1,0:T(8,128)(2,1)S(1)} %bitcast.56, bf16[32,128,128]{2,1,0:T(8,128)(2,1)S(1)} %collective-permute-done.1.other_ref, bf16[256,256]{1,0:T(8,128)(2,1)S(1)} %get-tuple-element.80.refs_0_, bf16[1536,256]{1,0:T(8,128)(2,1)S(1)} %bitcast.51), custom_call_target="tpu_custom_call" | custom-call | flops 536870912 | bytes 4063232 | tf_op jit(solution)/shard_map/pallas_call | solution.py:58
  127.8 20.2 %all_to_all.39 = bf16[8,256,256]{2,1,0:T(8,128)(2,1)S(1)} all-to-all(bf16[8,256,256]{2,1,0:T(8,128)(2,1)S(1)} %bitcast.47), channel_id=1, replica_groups=mesh['x'=4,'z'=12,'y'=8,'core'=2] {'y'}, dimensions={0} | all-to-all | bytes 2097152 | tf_op jit(solution)/shard_map/all_to_all | solution.py:186
  148.2 1.9 %collective-permute-start.2 = (bf16[2,128,256]{2,1,0:T(8,128)(2,1)S(1)}, bf16[2,128,256]{2,1,0:T(8,128)(2,1)S(1)}, u32[]{:S(2)}, u32[]{:S(2)}) collective-permute-start(bf16[2,128,256]{2,1,0:T(8,128)(2,1)S(1)} %pad_maximum_fusion.1), channel_id=1, source_target_pairs={{0,1},{1,0},{2,3},{3,2},{4,5},{5,4},{6,7},{7,6},{8,9},{9,8},{10,11... | collective-permute-start | bytes 393224 | tf_op jit(solution)/shard_map/ppermute | solution.py:156
  150.1 1.3 collective-permute-done.2
  151.5 0.7 pad_maximum_fusion.3
  152.1 0.7 pad_maximum_fusion.2
  (20 shorter events, 1.2 us)
Async XLA Ops:
  0.6 19.6 %collective-permute-start.1 = (bf16[32,128,128]{2,1,0:T(8,128)(2,1)}, bf16[32,128,128]{2,1,0:T(8,128)(2,1)S(1)}, u32[]{:S(2)}, u32[]{:S(2)}) collective-permute-start(bf16[32,128,128]{2,1,0:T(8,128)(2,1)} %bitcast.53), channel_id=1, source_target_pairs={{0,1},{1,0},{2,3},{3,2},{4,5},{5,4},{6,7},{7,6},{8,9},{9,8},{10,11... | collective-permute-start | bytes 3145736 | tf_op jit(solution)/shard_map/ppermute | solution.py:156
  13.7 0.9 copy-start
  16.5 3.7 %collective-permute-start = (bf16[912,256]{1,0:T(8,128)(2,1)S(1)}, bf16[912,256]{1,0:T(8,128)(2,1)S(1)}, u32[]{:S(2)}, u32[]{:S(2)}) collective-permute-start(bf16[912,256]{1,0:T(8,128)(2,1)S(1)} %get-tuple-element.75), channel_id=1, source_target_pairs={{0,1},{1,0},{2,3},{3,2},{4,5},{5,4},{6,7},{7,6},{8,9},{9,8},{10,11... | collective-permute-start | bytes 1400840 | tf_op jit(solution)/shard_map/ppermute | solution.py:156
  24.3 9.7 %all-to-all-start = ((bf16[4,192,256]{2,1,0:T(8,128)(2,1)}), bf16[4,192,256]{2,1,0:T(8,128)(2,1)S(1)}, u32[]{:S(2)}, u32[]{:S(2)}) async-start(bf16[4,192,256]{2,1,0:T(8,128)(2,1)} %bitcast.3), calls=%async_computation | async-start | bytes 786432 | tf_op jit(solution)/shard_map/cond/branch_0_fun/all_to_all | solution.py:159
  44.8 26.0 %copy-start.2 = (bf16[32,128,128]{2,1,0:T(8,128)(2,1)S(1)}, bf16[32,128,128]{2,1,0:T(8,128)(2,1)}, u32[]{:S(2)}) copy-start(bf16[32,128,128]{2,1,0:T(8,128)(2,1)} %get-tuple-element.48.own_ref) | copy-start | bytes 3145732 | tf_op jit(solution)/shard_map/cond
  97.4 27.8 %copy-start.1 = (bf16[1,32,128,128]{3,2,1,0:T(8,128)(2,1)S(1)}, bf16[1,32,128,128]{3,2,1,0:T(8,128)(2,1)}, u32[]{:S(2)}) copy-start(bf16[1,32,128,128]{3,2,1,0:T(8,128)(2,1)} %param.9) | copy-start | bytes 3145732
  148.2 3.2 %collective-permute-start.2 = (bf16[2,128,256]{2,1,0:T(8,128)(2,1)S(1)}, bf16[2,128,256]{2,1,0:T(8,128)(2,1)S(1)}, u32[]{:S(2)}, u32[]{:S(2)}) collective-permute-start(bf16[2,128,256]{2,1,0:T(8,128)(2,1)S(1)} %pad_maximum_fusion.1), channel_id=1, source_target_pairs={{0,1},{1,0},{2,3},{3,2},{4,5},{5,4},{6,7},{7,6},{8,9},{9,8},{10,11... | collective-permute-start | bytes 393224 | tf_op jit(solution)/shard_map/ppermute | solution.py:156

commit v9 on v8

--- a/solution.py
+++ b/solution.py
@@ -7,7 +7,7 @@
 from jax.experimental.pallas import tpu as pltpu
 from jax.sharding import Mesh, PartitionSpec as P
 
-GRP = 16
+GRP = 32
 ALONG_X = 4
 PAIR = [(0, 1), (1, 0)]
 VMEM_BYTES = 16 * 1024 * 1024
@@ -136,6 +136,28 @@
     )(core.reshape(1), features, lists, block_rows, block_cols, block_count)
 
 
+def finish_kernel(core_ref, first_ref, second_ref, others_ref, out_first_ref, out_second_ref):
+    rows, half = others_ref.shape[1], others_ref.shape[2]
+    core = core_ref[0]
+    here = pl.ds(pl.multiple_of(core * half, half), half)
+    there = pl.ds(pl.multiple_of((1 - core) * half, half), half)
+    for place, (ref, out_ref) in enumerate(((first_ref, out_first_ref), (second_ref, out_second_ref))):
+        out_ref[:, here] = ref[pl.ds(0, rows), :]
+        out_ref[:, there] = others_ref[place]
+
+
+def finish(core, first, second, others):
+    anywhere = pl.BlockSpec(memory_space=pltpu.VMEM)
+    shape = jax.ShapeDtypeStruct((others.shape[1], 2 * others.shape[2]), first.dtype)
+    return pl.pallas_call(
+        finish_kernel,
+        out_shape=(shape, shape),
+        in_specs=[pl.BlockSpec(memory_space=pltpu.SMEM)] + [anywhere] * 3,
+        out_specs=(anywhere, anywhere),
+        compiler_params=pltpu.CompilerParams(vmem_limit_bytes=VMEM_BYTES),
+    )(core.reshape(1), first, second, others)
+
+
 def one_hot(wanted, extent):
     place = lax.broadcasted_iota(jnp.int32, (1, extent), 1)
     return (wanted.reshape(-1, 1) == place).astype(jnp.bfloat16)
@@ -213,14 +235,8 @@
     fetched = exchange(pick(one_hot(wanted, 2 * rows), first))
     second = combine(multiply((first,), (0,), fetched, straight, meta, held, other_held))
     kept_back = lax.optimization_barrier((first, second))
-    others = swap(jnp.stack([v[rows:] for v in kept_back])).reshape(2 * rows, half)
-
-    def whole(kept, other):
-        return jnp.concatenate(
-            [jnp.where(core == 0, kept, other), jnp.where(core == 0, other, kept)], 1
-        )
-
-    return (whole(first[:rows], others[:rows]), whole(second[:rows], others[rows:]))
+    others = swap(jnp.stack([v[rows:] for v in kept_back]))
+    return finish(core, first, second, others)
 
 
 def solution(mesh):

time: 153 us -> 152 us (level)
  no operation moved by 1% of the time
where the time goes in v9:
time: 152 us; the launch traced here: 151 us
  blocking collectives  107 us (70%)
  starting transfers between devices  19.7 us (13%)
  waiting for transfers between devices  8.38 us (6%)
  Pallas kernels  7.21 us (5%)
  other arithmetic  4.02 us (3%)
  local copies, waits for them, and re-layouts  2.37 us (2%)
    all_to_all x3, blocking collectives, exchange(): lax.all_to_all(picked.reshape(lax.axis_size(axes), -1, half), axes, 0, 0,...  61.8 us
    all_to_all x2, blocking collectives, combine(): parts = lax.all_to_all(partial_value, 'y', 0, 0, tiled=True)  44.9 us
    ppermute x3, starting transfers between devices, swap(): return lax.ppermute(value, 'core', PAIR)  16.3 us
    all_to_all x1, waiting for transfers between devices, exchange(): lax.all_to_all(picked.reshape(lax.axis_size(axes), -1, half), axes, 0, 0,...  6.16 us
    pallas_call x2, Pallas kernels, product(): pl.pallas_call(functools.partial(product_kernel, slots, cap, starts, orde...  4.59 us
    all_to_all x1, starting transfers between devices, exchange(): lax.all_to_all(picked.reshape(lax.axis_size(axes), -1, half), axes, 0, 0,...  3.46 us
  transfers between devices with their start and end apart: 4, of which 3 were waited for; matrix products, arithmetic and copies ran while one was open for 1% of the time, Pallas kernels for 1%

profile of v9, /device:TPU:1, one launch (start us, length us, event | category | flops | bytes accessed | tf_op | source)
XLA Modules:
  0.0 151.0 jit_solution(11908546636895994908)
XLA Ops:
  0.6 12.4 %collective-permute-start.1 = (bf16[32,128,128]{2,1,0:T(8,128)(2,1)}, bf16[32,128,128]{2,1,0:T(8,128)(2,1)S(1)}, u32[]{:S(2)}, u32[]{:S(2)}) collective-permute-start(bf16[32,128,128]{2,1,0:T(8,128)(2,1)} %bitcast.41), channel_id=1, source_target_pairs={{0,1},{1,0},{2,3},{3,2},{4,5},{5,4},{6,7},{7,6},{8,9},{9,8},{10,11... | collective-permute-start | bytes 3145736 | tf_op jit(solution)/shard_map/ppermute | solution.py:178
  13.7 0.9 copy-done
  14.6 1.9 %shard_map.77 = (bf16[768,256]{1,0:T(8,128)(2,1)}, bf16[912,256]{1,0:T(8,128)(2,1)S(1)}) custom-call(s32[1]{0:T(128)} %bitcast.17.core_ref, bf16[128,512]{1,0:T(8,128)(2,1)S(1)} %copy-done, s32[16,48]{1,0:T(8,128)} %bitcast.50, s32[1,32]{1,0:T(1,128)} %rows_ref.1, s32[1,32]{1,0:T(1,128)} %cols_ref.1, s32[1,1]{1,0:T(1,128)S(6)} %copy.21.count_ref), custom_call_target="tpu_custom_call" | custom-call | tf_op jit(solution)/shard_map/pallas_call | solution.py:123
  16.5 1.9 %collective-permute-start = (bf16[912,256]{1,0:T(8,128)(2,1)S(1)}, bf16[912,256]{1,0:T(8,128)(2,1)S(1)}, u32[]{:S(2)}, u32[]{:S(2)}) collective-permute-start(bf16[912,256]{1,0:T(8,128)(2,1)S(1)} %get-tuple-element.75), channel_id=1, source_target_pairs={{0,1},{1,0},{2,3},{3,2},{4,5},{5,4},{6,7},{7,6},{8,9},{9,8},{10,11... | collective-permute-start | bytes 1400840 | tf_op jit(solution)/shard_map/ppermute | solution.py:178
  18.5 0.9 slice_select_fusion
  19.3 0.9 collective-permute-done
  20.2 77.7 %conditional.1 = (bf16[256,256]{1,0:T(8,128)(2,1)S(1)}, s32[2,65]{1,0:T(2,128)S(1)}, s32[1536]{0:T(1024)}) conditional(s32[]{:T(128)} %convert_element_type.9, (s32[1,32]{1,0:T(1,128)}, s32[1,32]{1,0:T(1,128)}, s32[1,1]{1,0:T(1,128)}, bf16[912,256]{1,0:T(8,128)(2,1)S(1)}, s32[]{:T(128)}, /*index=5*/s32[16,48]{1,0:T(8,128)}, ...), branch_computations={%region_0.2_spmd, %region_2.4_spmd} | conditional | flops 537730240 | bytes 19074804 | solution.py:233
  20.3 0.5 slice.51
  20.8 0.7 add_bitcast_fusion
  21.6 0.7 reshape.37
  22.3 2.0 %xor_select_fusion.meta_ref = s32[2,65]{1,0:T(2,128)S(1)} fusion(s32[1,1]{1,0:T(1,128)} %slice.51, s32[1,32]{1,0:T(1,128)S(1)} %get-tuple-element.83, s32[1,32]{1,0:T(1,128)S(1)} %get-tuple-element.82, s32[1,1]{1,0:T(1,128)} %get-tuple-element.42, s32[1,32]{1,0:T(1,128)} %get-tuple-element.41, s32[1,32]{1,0:T(1,128)} %get-tuple-element.40, ...), kind=kLoop, calls=%fused_computation.5 | loop fusion | flops 910 | bytes 1109 | tf_op jit(solution)/shard_map/cond/branch_0_fun/jit(_where)/select_n | solution.py:199
  24.3 3.5 %all-to-all-start = ((bf16[4,192,256]{2,1,0:T(8,128)(2,1)}), bf16[4,192,256]{2,1,0:T(8,128)(2,1)S(1)}, u32[]{:S(2)}, u32[]{:S(2)}) async-start(bf16[4,192,256]{2,1,0:T(8,128)(2,1)} %bitcast.3), calls=%async_computation | async-start | bytes 786432 | tf_op jit(solution)/shard_map/cond/branch_0_fun/all_to_all | solution.py:181
  27.8 6.2 %all-to-all-done = bf16[4,192,256]{2,1,0:T(8,128)(2,1)S(1)} async-done(((bf16[4,192,256]{2,1,0:T(8,128)(2,1)}), bf16[4,192,256]{2,1,0:T(8,128)(2,1)S(1)}, u32[]{:S(2)}, u32[]{:S(2)}) %all-to-all-start) | async-done | bytes 393248 | tf_op jit(solution)/shard_map/cond/branch_0_fun/all_to_all | solution.py:181
  34.0 10.6 %all_to_all.34 = bf16[4,192,256]{2,1,0:T(8,128)(2,1)S(1)} all-to-all(bf16[4,192,256]{2,1,0:T(8,128)(2,1)S(1)} %bitcast.46), channel_id=1, replica_groups=mesh['x'=4,'z'=12,'y'=8,'core'=2] {'x'}, dimensions={0} | all-to-all | bytes 786432 | tf_op jit(solution)/shard_map/cond/branch_0_fun/all_to_all | solution.py:181
  44.8 26.0 %all_to_all.35 = bf16[12,128,256]{2,1,0:T(8,128)(2,1)S(1)} all-to-all(bf16[12,128,256]{2,1,0:T(8,128)(2,1)S(1)} %bitcast.45), channel_id=1, replica_groups=mesh['x'=4,'z'=12,'y'=8,'core'=2] {'z'}, dimensions={0} | all-to-all | bytes 1572864 | tf_op jit(solution)/shard_map/cond/branch_0_fun/all_to_all | solution.py:181
  70.8 2.3 %branch_0_fun.1 = bf16[2048,256]{1,0:T(8,128)(2,1)S(1)} custom-call(s32[2,65]{1,0:T(2,128)S(1)} %xor_select_fusion.meta_ref, bf16[32,128,128]{2,1,0:T(8,128)(2,1)S(1)} %copy-done.2, bf16[32,128,128]{2,1,0:T(8,128)(2,1)S(1)} %get-tuple-element.49.other_ref, bf16[128,256]{1,0:T(8,128)(2,1)S(1)} %get-tuple-element.50.refs_0_, ...), custom_call_target="tpu_custom_call" | custom-call | flops 536870912 | bytes 4063232 | tf_op jit(solution)/shard_map/cond/branch_0_fun/pallas_call | solution.py:58
  73.1 24.7 %all_to_all.36 = bf16[8,256,256]{2,1,0:T(8,128)(2,1)S(1)} all-to-all(bf16[8,256,256]{2,1,0:T(8,128)(2,1)S(1)} %bitcast.36), channel_id=1, replica_groups=mesh['x'=4,'z'=12,'y'=8,'core'=2] {'y'}, dimensions={0} | all-to-all | bytes 2097152 | tf_op jit(solution)/shard_map/cond/branch_0_fun/all_to_all | solution.py:208
  98.0 1.2 fusion.2
  99.2 25.2 %all_to_all.38 = bf16[48,32,256]{2,1,0:T(8,128)(2,1)S(1)} all-to-all(bf16[48,32,256]{2,1,0:T(8,128)(2,1)S(1)} %bitcast.49), channel_id=1, replica_groups=mesh['x'=4,'z'=12,'y'=8,'core'=2] {'x','z'}, dimensions={0} | all-to-all | bytes 1572864 | tf_op jit(solution)/shard_map/all_to_all | solution.py:181
  124.4 2.3 %shard_map.78 = bf16[2048,256]{1,0:T(8,128)(2,1)S(1)} custom-call(s32[2,65]{1,0:T(2,128)S(1)} %get-tuple-element.78.meta_ref, bf16[32,128,128]{2,1,0:T(8,128)(2,1)S(1)} %bitcast.44, bf16[32,128,128]{2,1,0:T(8,128)(2,1)S(1)} %collective-permute-done.1.other_ref, bf16[256,256]{1,0:T(8,128)(2,1)S(1)} %get-tuple-element.80.refs_0_.first_ref, ...), custom_call_target="tpu_custom_call" | custom-call | flops 536870912 | bytes 4063232 | tf_op jit(solution)/shard_map/pallas_call | solution.py:58
  126.7 20.2 %all_to_all.39 = bf16[8,256,256]{2,1,0:T(8,128)(2,1)S(1)} all-to-all(bf16[8,256,256]{2,1,0:T(8,128)(2,1)S(1)} %bitcast.35), channel_id=1, replica_groups=mesh['x'=4,'z'=12,'y'=8,'core'=2] {'y'}, dimensions={0} | all-to-all | bytes 2097152 | tf_op jit(solution)/shard_map/all_to_all | solution.py:208
  147.1 1.9 %collective-permute-start.2 = (bf16[2,128,256]{2,1,0:T(8,128)(2,1)S(1)}, bf16[2,128,256]{2,1,0:T(8,128)(2,1)S(1)}, u32[]{:S(2)}, u32[]{:S(2)}) collective-permute-start(bf16[2,128,256]{2,1,0:T(8,128)(2,1)S(1)} %pad_maximum_fusion.1), channel_id=1, source_target_pairs={{0,1},{1,0},{2,3},{3,2},{4,5},{5,4},{6,7},{7,6},{8,9},{9,8},{10,11... | collective-permute-start | bytes 393224 | tf_op jit(solution)/shard_map/ppermute | solution.py:178
  149.0 1.3 collective-permute-done.2.others_ref
  150.3 0.7 shard_map.79
  (18 shorter events, 0.6 us)
Async XLA Ops:
  0.6 19.6 %collective-permute-start.1 = (bf16[32,128,128]{2,1,0:T(8,128)(2,1)}, bf16[32,128,128]{2,1,0:T(8,128)(2,1)S(1)}, u32[]{:S(2)}, u32[]{:S(2)}) collective-permute-start(bf16[32,128,128]{2,1,0:T(8,128)(2,1)} %bitcast.41), channel_id=1, source_target_pairs={{0,1},{1,0},{2,3},{3,2},{4,5},{5,4},{6,7},{7,6},{8,9},{9,8},{10,11... | collective-permute-start | bytes 3145736 | tf_op jit(solution)/shard_map/ppermute | solution.py:178
  13.7 0.9 copy-start
  16.5 3.7 %collective-permute-start = (bf16[912,256]{1,0:T(8,128)(2,1)S(1)}, bf16[912,256]{1,0:T(8,128)(2,1)S(1)}, u32[]{:S(2)}, u32[]{:S(2)}) collective-permute-start(bf16[912,256]{1,0:T(8,128)(2,1)S(1)} %get-tuple-element.75), channel_id=1, source_target_pairs={{0,1},{1,0},{2,3},{3,2},{4,5},{5,4},{6,7},{7,6},{8,9},{9,8},{10,11... | collective-permute-start | bytes 1400840 | tf_op jit(solution)/shard_map/ppermute | solution.py:178
  24.3 9.7 %all-to-all-start = ((bf16[4,192,256]{2,1,0:T(8,128)(2,1)}), bf16[4,192,256]{2,1,0:T(8,128)(2,1)S(1)}, u32[]{:S(2)}, u32[]{:S(2)}) async-start(bf16[4,192,256]{2,1,0:T(8,128)(2,1)} %bitcast.3), calls=%async_computation | async-start | bytes 786432 | tf_op jit(solution)/shard_map/cond/branch_0_fun/all_to_all | solution.py:181
  44.8 26.0 %copy-start.2 = (bf16[32,128,128]{2,1,0:T(8,128)(2,1)S(1)}, bf16[32,128,128]{2,1,0:T(8,128)(2,1)}, u32[]{:S(2)}) copy-start(bf16[32,128,128]{2,1,0:T(8,128)(2,1)} %get-tuple-element.48.own_ref) | copy-start | bytes 3145732 | tf_op jit(solution)/shard_map/cond
  98.0 26.5 %copy-start.1 = (bf16[1,32,128,128]{3,2,1,0:T(8,128)(2,1)S(1)}, bf16[1,32,128,128]{3,2,1,0:T(8,128)(2,1)}, u32[]{:S(2)}) copy-start(bf16[1,32,128,128]{3,2,1,0:T(8,128)(2,1)} %param.9) | copy-start | bytes 3145732
  147.1 3.2 %collective-permute-start.2 = (bf16[2,128,256]{2,1,0:T(8,128)(2,1)S(1)}, bf16[2,128,256]{2,1,0:T(8,128)(2,1)S(1)}, u32[]{:S(2)}, u32[]{:S(2)}) collective-permute-start(bf16[2,128,256]{2,1,0:T(8,128)(2,1)S(1)} %pad_maximum_fusion.1), channel_id=1, source_target_pairs={{0,1},{1,0},{2,3},{3,2},{4,5},{5,4},{6,7},{7,6},{8,9},{9,8},{10,11... | collective-permute-start | bytes 393224 | tf_op jit(solution)/shard_map/ppermute | solution.py:178

commit v10 on v9

--- a/solution.py
+++ b/solution.py
@@ -7,7 +7,7 @@
 from jax.experimental.pallas import tpu as pltpu
 from jax.sharding import Mesh, PartitionSpec as P
 
-GRP = 32
+GRP = 16
 ALONG_X = 4
 PAIR = [(0, 1), (1, 0)]
 VMEM_BYTES = 16 * 1024 * 1024

time: 152 us -> 151 us (level)
  no operation moved by 1% of the time
where the time goes in v10:
time: 151 us; the launch traced here: 150 us
  blocking collectives  106 us (70%)
  starting transfers between devices  19.7 us (13%)
  waiting for transfers between devices  8.38 us (6%)
  Pallas kernels  6.97 us (5%)
  other arithmetic  4.02 us (3%)
  local copies, waits for them, and re-layouts  2.37 us (2%)
    all_to_all x3, blocking collectives, exchange(): lax.all_to_all(picked.reshape(lax.axis_size(axes), -1, half), axes, 0, 0,...  60.9 us
    all_to_all x2, blocking collectives, combine(): parts = lax.all_to_all(partial_value, 'y', 0, 0, tiled=True)  45.3 us
    ppermute x3, starting transfers between devices, swap(): return lax.ppermute(value, 'core', PAIR)  16.3 us
    all_to_all x1, waiting for transfers between devices, exchange(): lax.all_to_all(picked.reshape(lax.axis_size(axes), -1, half), axes, 0, 0,...  6.16 us
    pallas_call x2, Pallas kernels, product(): pl.pallas_call(functools.partial(product_kernel, slots, cap, starts, orde...  4.34 us
    all_to_all x1, starting transfers between devices, exchange(): lax.all_to_all(picked.reshape(lax.axis_size(axes), -1, half), axes, 0, 0,...  3.46 us
  transfers between devices with their start and end apart: 4, of which 3 were waited for; matrix products, arithmetic and copies ran while one was open for 1% of the time, Pallas kernels for 1%

profile of v10, /device:TPU:1, one launch (start us, length us, event | category | flops | bytes accessed | tf_op | source)
XLA Modules:
  0.0 150.3 jit_solution(9805449718502920741)
XLA Ops:
  0.6 12.4 %collective-permute-start.1 = (bf16[32,128,128]{2,1,0:T(8,128)(2,1)}, bf16[32,128,128]{2,1,0:T(8,128)(2,1)S(1)}, u32[]{:S(2)}, u32[]{:S(2)}) collective-permute-start(bf16[32,128,128]{2,1,0:T(8,128)(2,1)} %bitcast.41), channel_id=1, source_target_pairs={{0,1},{1,0},{2,3},{3,2},{4,5},{5,4},{6,7},{7,6},{8,9},{9,8},{10,11... | collective-permute-start | bytes 3145736 | tf_op jit(solution)/shard_map/ppermute | solution.py:178
  13.7 0.9 copy-done
  14.6 1.9 %shard_map.77 = (bf16[768,256]{1,0:T(8,128)(2,1)}, bf16[912,256]{1,0:T(8,128)(2,1)S(1)}) custom-call(s32[1]{0:T(128)} %bitcast.17.core_ref, bf16[128,512]{1,0:T(8,128)(2,1)S(1)} %copy-done, s32[16,48]{1,0:T(8,128)} %bitcast.50, s32[1,32]{1,0:T(1,128)} %rows_ref.1, s32[1,32]{1,0:T(1,128)} %cols_ref.1, s32[1,1]{1,0:T(1,128)S(6)} %copy.21.count_ref), custom_call_target="tpu_custom_call" | custom-call | tf_op jit(solution)/shard_map/pallas_call | solution.py:123
  16.5 1.9 %collective-permute-start = (bf16[912,256]{1,0:T(8,128)(2,1)S(1)}, bf16[912,256]{1,0:T(8,128)(2,1)S(1)}, u32[]{:S(2)}, u32[]{:S(2)}) collective-permute-start(bf16[912,256]{1,0:T(8,128)(2,1)S(1)} %get-tuple-element.75), channel_id=1, source_target_pairs={{0,1},{1,0},{2,3},{3,2},{4,5},{5,4},{6,7},{7,6},{8,9},{9,8},{10,11... | collective-permute-start | bytes 1400840 | tf_op jit(solution)/shard_map/ppermute | solution.py:178
  18.5 0.9 slice_select_fusion
  19.3 0.9 collective-permute-done
  20.2 78.0 %conditional.1 = (bf16[256,256]{1,0:T(8,128)(2,1)S(1)}, s32[2,65]{1,0:T(2,128)S(1)}, s32[1536]{0:T(1024)}) conditional(s32[]{:T(128)} %convert_element_type.9, (s32[1,32]{1,0:T(1,128)}, s32[1,32]{1,0:T(1,128)}, s32[1,1]{1,0:T(1,128)}, bf16[912,256]{1,0:T(8,128)(2,1)S(1)}, s32[]{:T(128)}, /*index=5*/s32[16,48]{1,0:T(8,128)}, ...), branch_computations={%region_0.2_spmd, %region_2.4_spmd} | conditional | flops 537730240 | bytes 19074804 | solution.py:233
  20.3 0.5 slice.51
  20.8 0.7 add_bitcast_fusion
  21.6 0.7 reshape.37
  22.3 2.0 %xor_select_fusion.meta_ref = s32[2,65]{1,0:T(2,128)S(1)} fusion(s32[1,1]{1,0:T(1,128)} %slice.51, s32[1,32]{1,0:T(1,128)S(1)} %get-tuple-element.83, s32[1,32]{1,0:T(1,128)S(1)} %get-tuple-element.82, s32[1,1]{1,0:T(1,128)} %get-tuple-element.42, s32[1,32]{1,0:T(1,128)} %get-tuple-element.41, s32[1,32]{1,0:T(1,128)} %get-tuple-element.40, ...), kind=kLoop, calls=%fused_computation.5 | loop fusion | flops 910 | bytes 1109 | tf_op jit(solution)/shard_map/cond/branch_0_fun/jit(_where)/select_n | solution.py:199
  24.3 3.5 %all-to-all-start = ((bf16[4,192,256]{2,1,0:T(8,128)(2,1)}), bf16[4,192,256]{2,1,0:T(8,128)(2,1)S(1)}, u32[]{:S(2)}, u32[]{:S(2)}) async-start(bf16[4,192,256]{2,1,0:T(8,128)(2,1)} %bitcast.3), calls=%async_computation | async-start | bytes 786432 | tf_op jit(solution)/shard_map/cond/branch_0_fun/all_to_all | solution.py:181
  27.8 6.2 %all-to-all-done = bf16[4,192,256]{2,1,0:T(8,128)(2,1)S(1)} async-done(((bf16[4,192,256]{2,1,0:T(8,128)(2,1)}), bf16[4,192,256]{2,1,0:T(8,128)(2,1)S(1)}, u32[]{:S(2)}, u32[]{:S(2)}) %all-to-all-start) | async-done | bytes 393248 | tf_op jit(solution)/shard_map/cond/branch_0_fun/all_to_all | solution.py:181
  34.0 10.6 %all_to_all.34 = bf16[4,192,256]{2,1,0:T(8,128)(2,1)S(1)} all-to-all(bf16[4,192,256]{2,1,0:T(8,128)(2,1)S(1)} %bitcast.46), channel_id=1, replica_groups=mesh['x'=4,'z'=12,'y'=8,'core'=2] {'x'}, dimensions={0} | all-to-all | bytes 786432 | tf_op jit(solution)/shard_map/cond/branch_0_fun/all_to_all | solution.py:181
  44.8 26.0 %all_to_all.35 = bf16[12,128,256]{2,1,0:T(8,128)(2,1)S(1)} all-to-all(bf16[12,128,256]{2,1,0:T(8,128)(2,1)S(1)} %bitcast.45), channel_id=1, replica_groups=mesh['x'=4,'z'=12,'y'=8,'core'=2] {'z'}, dimensions={0} | all-to-all | bytes 1572864 | tf_op jit(solution)/shard_map/cond/branch_0_fun/all_to_all | solution.py:181
  70.8 2.2 %branch_0_fun.1 = bf16[2048,256]{1,0:T(8,128)(2,1)S(1)} custom-call(s32[2,65]{1,0:T(2,128)S(1)} %xor_select_fusion.meta_ref, bf16[32,128,128]{2,1,0:T(8,128)(2,1)S(1)} %copy-done.2, bf16[32,128,128]{2,1,0:T(8,128)(2,1)S(1)} %get-tuple-element.49.other_ref, bf16[128,256]{1,0:T(8,128)(2,1)S(1)} %get-tuple-element.50.refs_0_, ...), custom_call_target="tpu_custom_call" | custom-call | flops 536870912 | bytes 4063232 | tf_op jit(solution)/shard_map/cond/branch_0_fun/pallas_call | solution.py:58
  73.0 25.1 %all_to_all.36 = bf16[8,256,256]{2,1,0:T(8,128)(2,1)S(1)} all-to-all(bf16[8,256,256]{2,1,0:T(8,128)(2,1)S(1)} %bitcast.36), channel_id=1, replica_groups=mesh['x'=4,'z'=12,'y'=8,'core'=2] {'y'}, dimensions={0} | all-to-all | bytes 2097152 | tf_op jit(solution)/shard_map/cond/branch_0_fun/all_to_all | solution.py:208
  98.3 1.2 fusion.2
  99.5 24.3 %all_to_all.38 = bf16[48,32,256]{2,1,0:T(8,128)(2,1)S(1)} all-to-all(bf16[48,32,256]{2,1,0:T(8,128)(2,1)S(1)} %bitcast.49), channel_id=1, replica_groups=mesh['x'=4,'z'=12,'y'=8,'core'=2] {'x','z'}, dimensions={0} | all-to-all | bytes 1572864 | tf_op jit(solution)/shard_map/all_to_all | solution.py:181
  123.8 2.2 %shard_map.78 = bf16[2048,256]{1,0:T(8,128)(2,1)S(1)} custom-call(s32[2,65]{1,0:T(2,128)S(1)} %get-tuple-element.78.meta_ref, bf16[32,128,128]{2,1,0:T(8,128)(2,1)S(1)} %bitcast.44, bf16[32,128,128]{2,1,0:T(8,128)(2,1)S(1)} %collective-permute-done.1.other_ref, bf16[256,256]{1,0:T(8,128)(2,1)S(1)} %get-tuple-element.80.refs_0_.first_ref, ...), custom_call_target="tpu_custom_call" | custom-call | flops 536870912 | bytes 4063232 | tf_op jit(solution)/shard_map/pallas_call | solution.py:58
  126.0 20.2 %all_to_all.39 = bf16[8,256,256]{2,1,0:T(8,128)(2,1)S(1)} all-to-all(bf16[8,256,256]{2,1,0:T(8,128)(2,1)S(1)} %bitcast.35), channel_id=1, replica_groups=mesh['x'=4,'z'=12,'y'=8,'core'=2] {'y'}, dimensions={0} | all-to-all | bytes 2097152 | tf_op jit(solution)/shard_map/all_to_all | solution.py:208
  146.4 1.9 %collective-permute-start.2 = (bf16[2,128,256]{2,1,0:T(8,128)(2,1)S(1)}, bf16[2,128,256]{2,1,0:T(8,128)(2,1)S(1)}, u32[]{:S(2)}, u32[]{:S(2)}) collective-permute-start(bf16[2,128,256]{2,1,0:T(8,128)(2,1)S(1)} %pad_maximum_fusion.1), channel_id=1, source_target_pairs={{0,1},{1,0},{2,3},{3,2},{4,5},{5,4},{6,7},{7,6},{8,9},{9,8},{10,11... | collective-permute-start | bytes 393224 | tf_op jit(solution)/shard_map/ppermute | solution.py:178
  148.3 1.3 collective-permute-done.2.others_ref
  149.6 0.7 shard_map.79
  (18 shorter events, 0.6 us)
Async XLA Ops:
  0.6 19.6 %collective-permute-start.1 = (bf16[32,128,128]{2,1,0:T(8,128)(2,1)}, bf16[32,128,128]{2,1,0:T(8,128)(2,1)S(1)}, u32[]{:S(2)}, u32[]{:S(2)}) collective-permute-start(bf16[32,128,128]{2,1,0:T(8,128)(2,1)} %bitcast.41), channel_id=1, source_target_pairs={{0,1},{1,0},{2,3},{3,2},{4,5},{5,4},{6,7},{7,6},{8,9},{9,8},{10,11... | collective-permute-start | bytes 3145736 | tf_op jit(solution)/shard_map/ppermute | solution.py:178
  13.7 0.9 copy-start
  16.5 3.7 %collective-permute-start = (bf16[912,256]{1,0:T(8,128)(2,1)S(1)}, bf16[912,256]{1,0:T(8,128)(2,1)S(1)}, u32[]{:S(2)}, u32[]{:S(2)}) collective-permute-start(bf16[912,256]{1,0:T(8,128)(2,1)S(1)} %get-tuple-element.75), channel_id=1, source_target_pairs={{0,1},{1,0},{2,3},{3,2},{4,5},{5,4},{6,7},{7,6},{8,9},{9,8},{10,11... | collective-permute-start | bytes 1400840 | tf_op jit(solution)/shard_map/ppermute | solution.py:178
  24.3 9.7 %all-to-all-start = ((bf16[4,192,256]{2,1,0:T(8,128)(2,1)}), bf16[4,192,256]{2,1,0:T(8,128)(2,1)S(1)}, u32[]{:S(2)}, u32[]{:S(2)}) async-start(bf16[4,192,256]{2,1,0:T(8,128)(2,1)} %bitcast.3), calls=%async_computation | async-start | bytes 786432 | tf_op jit(solution)/shard_map/cond/branch_0_fun/all_to_all | solution.py:181
  44.8 26.0 %copy-start.2 = (bf16[32,128,128]{2,1,0:T(8,128)(2,1)S(1)}, bf16[32,128,128]{2,1,0:T(8,128)(2,1)}, u32[]{:S(2)}) copy-start(bf16[32,128,128]{2,1,0:T(8,128)(2,1)} %get-tuple-element.48.own_ref) | copy-start | bytes 3145732 | tf_op jit(solution)/shard_map/cond
  98.3 25.5 %copy-start.1 = (bf16[1,32,128,128]{3,2,1,0:T(8,128)(2,1)S(1)}, bf16[1,32,128,128]{3,2,1,0:T(8,128)(2,1)}, u32[]{:S(2)}) copy-start(bf16[1,32,128,128]{3,2,1,0:T(8,128)(2,1)} %param.9) | copy-start | bytes 3145732
  146.4 3.2 %collective-permute-start.2 = (bf16[2,128,256]{2,1,0:T(8,128)(2,1)S(1)}, bf16[2,128,256]{2,1,0:T(8,128)(2,1)S(1)}, u32[]{:S(2)}, u32[]{:S(2)}) collective-permute-start(bf16[2,128,256]{2,1,0:T(8,128)(2,1)S(1)} %pad_maximum_fusion.1), channel_id=1, source_target_pairs={{0,1},{1,0},{2,3},{3,2},{4,5},{5,4},{6,7},{7,6},{8,9},{9,8},{10,11... | collective-permute-start | bytes 393224 | tf_op jit(solution)/shard_map/ppermute | solution.py:178

commit v11 on v10

--- a/solution.py
+++ b/solution.py
@@ -91,7 +91,7 @@
     )(mine, given)
 
 
-def pick_kernel(core_ref, features_ref, lists_ref, rows_ref, cols_ref, count_ref, mine_ref, sent_ref, chosen, numbers):
+def pick_kernel(core_ref, features_ref, lists_ref, rows_ref, cols_ref, count_ref, own_ref, mine_ref, sent_ref, chosen, numbers):
     cap, owners = lists_ref.shape
     rows, half = features_ref.shape[0], mine_ref.shape[1]
     place = lax.broadcasted_iota(jnp.int32, (cap, rows), 1)
@@ -113,6 +113,7 @@
     numbers[pl.ds(1, 1), pl.ds(rows, slots)] = cols_ref[...]
     numbers[pl.ds(2, 1), pl.ds(rows, 1)] = count_ref[...]
     sent_ref[pl.ds(ends[1], cap), :] = numbers[...].astype(jnp.float32).astype(sent_ref.dtype)
+    own_ref[...] = mine
     mine_ref[...] = jnp.dot(chosen[...], mine, preferred_element_type=jnp.float32).astype(mine_ref.dtype)
 
 
@@ -123,11 +124,12 @@
     return pl.pallas_call(
         pick_kernel,
         out_shape=(
+            jax.ShapeDtypeStruct((rows, half), features.dtype),
             jax.ShapeDtypeStruct((owners * cap, half), features.dtype),
             jax.ShapeDtypeStruct((owners * cap + rows + cap, half), features.dtype),
         ),
         in_specs=[pl.BlockSpec(memory_space=pltpu.SMEM)] + [anywhere] * 5,
-        out_specs=(anywhere, anywhere),
+        out_specs=(anywhere, anywhere, anywhere),
         scratch_shapes=[
             pltpu.VMEM((owners * cap, rows), jnp.bfloat16),
             pltpu.VMEM((cap, half), jnp.int32),
@@ -186,9 +188,8 @@
 
     other_held = swap(held)
     lists = send_rows[0].T
-    picked, sent = pick_own(core, features, lists, block_rows, block_cols, block_count)
+    mine, picked, sent = pick_own(core, features, lists, block_rows, block_cols, block_count)
     given = swap(sent)
-    mine = jnp.where(core == 0, features[:, :half], features[:, half:])
     ends = owners * cap, owners * cap + rows
 
     def places(given):

time: 151 us -> 152 us (level)
    all_to_all x3, blocking collectives: 60.9 us -> 63.1 us  [exchange(): lax.all_to_all(picked.reshape(lax.axis_size(axes), -1, half), axes, 0, 0,...]
  transfers between devices with their start and end apart: 4 -> 4, of which waited for: 3 -> 3; matrix products, arithmetic and copies ran while one was open for 1% -> 0% of each run, Pallas kernels for 1% -> 1%
where the time goes in v11:
time: 152 us
  blocking collectives  107 us (70%)
  starting transfers between devices  19.7 us (13%)
  waiting for transfers between devices  9.27 us (6%)
  Pallas kernels  7.86 us (5%)
  other arithmetic  3.14 us (2%)
  local copies, waits for them, and re-layouts  2.37 us (2%)
    all_to_all x3, blocking collectives, exchange(): lax.all_to_all(picked.reshape(lax.axis_size(axes), -1, half), axes, 0, 0,...  63.1 us
    all_to_all x2, blocking collectives, combine(): parts = lax.all_to_all(partial_value, 'y', 0, 0, tiled=True)  44.1 us
    ppermute x3, starting transfers between devices, swap(): return lax.ppermute(value, 'core', PAIR)  16.3 us
    all_to_all x1, waiting for transfers between devices, exchange(): lax.all_to_all(picked.reshape(lax.axis_size(axes), -1, half), axes, 0, 0,...  6.16 us
    pallas_call x2, Pallas kernels, product(): pl.pallas_call(functools.partial(product_kernel, slots, cap, starts, orde...  5.22 us
    all_to_all x1, starting transfers between devices, exchange(): lax.all_to_all(picked.reshape(lax.axis_size(axes), -1, half), axes, 0, 0,...  3.46 us
    ppermute x3, waiting for transfers between devices, swap(): return lax.ppermute(value, 'core', PAIR)  3.1 us
  transfers between devices with their start and end apart: 4, of which 3 were waited for; matrix products, arithmetic and copies ran while one was open for 0% of the time, Pallas kernels for 1%

profile of v11, /device:TPU:1, one launch (start us, length us, event | category | flops | bytes accessed | tf_op | source)
XLA Modules:
  0.0 152.2 jit_solution(3082930976245393137)
XLA Ops:
  0.6 12.4 %collective-permute-start.1 = (bf16[32,128,128]{2,1,0:T(8,128)(2,1)}, bf16[32,128,128]{2,1,0:T(8,128)(2,1)S(1)}, u32[]{:S(2)}, u32[]{:S(2)}) collective-permute-start(bf16[32,128,128]{2,1,0:T(8,128)(2,1)} %bitcast.41), channel_id=1, source_target_pairs={{0,1},{1,0},{2,3},{3,2},{4,5},{5,4},{6,7},{7,6},{8,9},{9,8},{10,11... | collective-permute-start | bytes 3145736 | tf_op jit(solution)/shard_map/ppermute | solution.py:180
  13.7 0.9 copy-done
  14.6 1.9 %shard_map.77 = (bf16[128,256]{1,0:T(8,128)(2,1)S(1)}, bf16[768,256]{1,0:T(8,128)(2,1)}, bf16[912,256]{1,0:T(8,128)(2,1)S(1)}) custom-call(s32[1]{0:T(128)} %bitcast.17.core_ref, bf16[128,512]{1,0:T(8,128)(2,1)S(1)} %copy-done, s32[16,48]{1,0:T(8,128)} %bitcast.50, s32[1,32]{1,0:T(1,128)} %rows_ref.1, s32[1,32]{1,0:T(1,128)} %cols_ref.1, ...), custom_call_target="tpu_custom_call" | custom-call | tf_op jit(solution)/shard_map/pallas_call | solution.py:124
  16.5 1.9 %collective-permute-start = (bf16[912,256]{1,0:T(8,128)(2,1)S(1)}, bf16[912,256]{1,0:T(8,128)(2,1)S(1)}, u32[]{:S(2)}, u32[]{:S(2)}) collective-permute-start(bf16[912,256]{1,0:T(8,128)(2,1)S(1)} %get-tuple-element.76), channel_id=1, source_target_pairs={{0,1},{1,0},{2,3},{3,2},{4,5},{5,4},{6,7},{7,6},{8,9},{9,8},{10,11... | collective-permute-start | bytes 1400840 | tf_op jit(solution)/shard_map/ppermute | solution.py:180
  18.5 1.8 %collective-permute-done = bf16[912,256]{1,0:T(8,128)(2,1)S(1)} collective-permute-done((bf16[912,256]{1,0:T(8,128)(2,1)S(1)}, bf16[912,256]{1,0:T(8,128)(2,1)S(1)}, u32[]{:S(2)}, u32[]{:S(2)}) %collective-permute-start) | collective-permute-done | bytes 466976 | tf_op jit(solution)/shard_map/ppermute | solution.py:180
  20.3 77.3 %conditional.1 = (bf16[256,256]{1,0:T(8,128)(2,1)S(1)}, s32[2,65]{1,0:T(2,128)S(1)}, s32[1536]{0:T(1024)}) conditional(s32[]{:T(128)} %convert_element_type.9, (s32[1,32]{1,0:T(1,128)}, s32[1,32]{1,0:T(1,128)}, s32[1,1]{1,0:T(1,128)}, bf16[912,256]{1,0:T(8,128)(2,1)S(1)}, s32[]{:T(128)}, /*index=5*/s32[16,48]{1,0:T(8,128)}, ...), branch_computations={%region_0.2_spmd, %region_2.4_spmd} | conditional | flops 537730240 | bytes 19074804 | solution.py:234
  20.3 0.5 slice.43
  20.8 0.7 add_bitcast_fusion
  21.6 0.7 reshape.37
  22.3 2.0 %xor_select_fusion.meta_ref = s32[2,65]{1,0:T(2,128)S(1)} fusion(s32[1,1]{1,0:T(1,128)} %slice.43, s32[1,32]{1,0:T(1,128)S(1)} %get-tuple-element.85, s32[1,32]{1,0:T(1,128)S(1)} %get-tuple-element.84, s32[1,1]{1,0:T(1,128)} %get-tuple-element.42, s32[1,32]{1,0:T(1,128)} %get-tuple-element.41, s32[1,32]{1,0:T(1,128)} %get-tuple-element.40, ...), kind=kLoop, calls=%fused_computation.5 | loop fusion | flops 910 | bytes 1109 | tf_op jit(solution)/shard_map/cond/branch_0_fun/jit(_where)/select_n | solution.py:200
  24.3 3.5 %all-to-all-start = ((bf16[4,192,256]{2,1,0:T(8,128)(2,1)}), bf16[4,192,256]{2,1,0:T(8,128)(2,1)S(1)}, u32[]{:S(2)}, u32[]{:S(2)}) async-start(bf16[4,192,256]{2,1,0:T(8,128)(2,1)} %bitcast.3), calls=%async_computation | async-start | bytes 786432 | tf_op jit(solution)/shard_map/cond/branch_0_fun/all_to_all | solution.py:183
  27.9 6.2 %all-to-all-done = bf16[4,192,256]{2,1,0:T(8,128)(2,1)S(1)} async-done(((bf16[4,192,256]{2,1,0:T(8,128)(2,1)}), bf16[4,192,256]{2,1,0:T(8,128)(2,1)S(1)}, u32[]{:S(2)}, u32[]{:S(2)}) %all-to-all-start) | async-done | bytes 393248 | tf_op jit(solution)/shard_map/cond/branch_0_fun/all_to_all | solution.py:183
  34.0 10.6 %all_to_all.34 = bf16[4,192,256]{2,1,0:T(8,128)(2,1)S(1)} all-to-all(bf16[4,192,256]{2,1,0:T(8,128)(2,1)S(1)} %bitcast.46), channel_id=1, replica_groups=mesh['x'=4,'z'=12,'y'=8,'core'=2] {'x'}, dimensions={0} | all-to-all | bytes 786432 | tf_op jit(solution)/shard_map/cond/branch_0_fun/all_to_all | solution.py:183
  44.8 26.0 %all_to_all.35 = bf16[12,128,256]{2,1,0:T(8,128)(2,1)S(1)} all-to-all(bf16[12,128,256]{2,1,0:T(8,128)(2,1)S(1)} %bitcast.45), channel_id=1, replica_groups=mesh['x'=4,'z'=12,'y'=8,'core'=2] {'z'}, dimensions={0} | all-to-all | bytes 1572864 | tf_op jit(solution)/shard_map/cond/branch_0_fun/all_to_all | solution.py:183
  70.8 2.6 %branch_0_fun.1 = bf16[2048,256]{1,0:T(8,128)(2,1)S(1)} custom-call(s32[2,65]{1,0:T(2,128)S(1)} %xor_select_fusion.meta_ref, bf16[32,128,128]{2,1,0:T(8,128)(2,1)S(1)} %copy-done.2, bf16[32,128,128]{2,1,0:T(8,128)(2,1)S(1)} %get-tuple-element.49.other_ref, bf16[128,256]{1,0:T(8,128)(2,1)S(1)} %get-tuple-element.50.refs_0_, ...), custom_call_target="tpu_custom_call" | custom-call | flops 536870912 | bytes 4063232 | tf_op jit(solution)/shard_map/cond/branch_0_fun/pallas_call | solution.py:58
  73.5 23.9 %all_to_all.36 = bf16[8,256,256]{2,1,0:T(8,128)(2,1)S(1)} all-to-all(bf16[8,256,256]{2,1,0:T(8,128)(2,1)S(1)} %bitcast.36), channel_id=1, replica_groups=mesh['x'=4,'z'=12,'y'=8,'core'=2] {'y'}, dimensions={0} | all-to-all | bytes 2097152 | tf_op jit(solution)/shard_map/cond/branch_0_fun/all_to_all | solution.py:209
  97.4 0.1 reduce_sum.33
  97.6 1.2 fusion.2
  98.8 26.4 %all_to_all.38 = bf16[48,32,256]{2,1,0:T(8,128)(2,1)S(1)} all-to-all(bf16[48,32,256]{2,1,0:T(8,128)(2,1)S(1)} %bitcast.49), channel_id=1, replica_groups=mesh['x'=4,'z'=12,'y'=8,'core'=2] {'x','z'}, dimensions={0} | all-to-all | bytes 1572864 | tf_op jit(solution)/shard_map/all_to_all | solution.py:183
  125.2 2.6 %shard_map.78 = bf16[2048,256]{1,0:T(8,128)(2,1)S(1)} custom-call(s32[2,65]{1,0:T(2,128)S(1)} %get-tuple-element.80.meta_ref, bf16[32,128,128]{2,1,0:T(8,128)(2,1)S(1)} %bitcast.44, bf16[32,128,128]{2,1,0:T(8,128)(2,1)S(1)} %collective-permute-done.1.other_ref, bf16[256,256]{1,0:T(8,128)(2,1)S(1)} %get-tuple-element.82.refs_0_.first_ref, ...), custom_call_target="tpu_custom_call" | custom-call | flops 536870912 | bytes 4063232 | tf_op jit(solution)/shard_map/pallas_call | solution.py:58
  127.9 20.2 %all_to_all.39 = bf16[8,256,256]{2,1,0:T(8,128)(2,1)S(1)} all-to-all(bf16[8,256,256]{2,1,0:T(8,128)(2,1)S(1)} %bitcast.35), channel_id=1, replica_groups=mesh['x'=4,'z'=12,'y'=8,'core'=2] {'y'}, dimensions={0} | all-to-all | bytes 2097152 | tf_op jit(solution)/shard_map/all_to_all | solution.py:209
  148.2 1.9 %collective-permute-start.2 = (bf16[2,128,256]{2,1,0:T(8,128)(2,1)S(1)}, bf16[2,128,256]{2,1,0:T(8,128)(2,1)S(1)}, u32[]{:S(2)}, u32[]{:S(2)}) collective-permute-start(bf16[2,128,256]{2,1,0:T(8,128)(2,1)S(1)} %pad_maximum_fusion.1), channel_id=1, source_target_pairs={{0,1},{1,0},{2,3},{3,2},{4,5},{5,4},{6,7},{7,6},{8,9},{9,8},{10,11... | collective-permute-start | bytes 393224 | tf_op jit(solution)/shard_map/ppermute | solution.py:180
  150.2 1.3 collective-permute-done.2.others_ref
  151.5 0.7 shard_map.79
  (17 shorter events, 0.5 us)
Async XLA Ops:
  0.6 19.6 %collective-permute-start.1 = (bf16[32,128,128]{2,1,0:T(8,128)(2,1)}, bf16[32,128,128]{2,1,0:T(8,128)(2,1)S(1)}, u32[]{:S(2)}, u32[]{:S(2)}) collective-permute-start(bf16[32,128,128]{2,1,0:T(8,128)(2,1)} %bitcast.41), channel_id=1, source_target_pairs={{0,1},{1,0},{2,3},{3,2},{4,5},{5,4},{6,7},{7,6},{8,9},{9,8},{10,11... | collective-permute-start | bytes 3145736 | tf_op jit(solution)/shard_map/ppermute | solution.py:180
  13.7 0.9 copy-start
  16.5 3.7 %collective-permute-start = (bf16[912,256]{1,0:T(8,128)(2,1)S(1)}, bf16[912,256]{1,0:T(8,128)(2,1)S(1)}, u32[]{:S(2)}, u32[]{:S(2)}) collective-permute-start(bf16[912,256]{1,0:T(8,128)(2,1)S(1)} %get-tuple-element.76), channel_id=1, source_target_pairs={{0,1},{1,0},{2,3},{3,2},{4,5},{5,4},{6,7},{7,6},{8,9},{9,8},{10,11... | collective-permute-start | bytes 1400840 | tf_op jit(solution)/shard_map/ppermute | solution.py:180
  24.3 9.7 %all-to-all-start = ((bf16[4,192,256]{2,1,0:T(8,128)(2,1)}), bf16[4,192,256]{2,1,0:T(8,128)(2,1)S(1)}, u32[]{:S(2)}, u32[]{:S(2)}) async-start(bf16[4,192,256]{2,1,0:T(8,128)(2,1)} %bitcast.3), calls=%async_computation | async-start | bytes 786432 | tf_op jit(solution)/shard_map/cond/branch_0_fun/all_to_all | solution.py:183
  44.8 26.0 %copy-start.2 = (bf16[32,128,128]{2,1,0:T(8,128)(2,1)S(1)}, bf16[32,128,128]{2,1,0:T(8,128)(2,1)}, u32[]{:S(2)}) copy-start(bf16[32,128,128]{2,1,0:T(8,128)(2,1)} %get-tuple-element.48.own_ref) | copy-start | bytes 3145732 | tf_op jit(solution)/shard_map/cond
  97.6 27.7 %copy-start.1 = (bf16[1,32,128,128]{3,2,1,0:T(8,128)(2,1)S(1)}, bf16[1,32,128,128]{3,2,1,0:T(8,128)(2,1)}, u32[]{:S(2)}) copy-start(bf16[1,32,128,128]{3,2,1,0:T(8,128)(2,1)} %param.9) | copy-start | bytes 3145732
  148.2 3.2 %collective-permute-start.2 = (bf16[2,128,256]{2,1,0:T(8,128)(2,1)S(1)}, bf16[2,128,256]{2,1,0:T(8,128)(2,1)S(1)}, u32[]{:S(2)}, u32[]{:S(2)}) collective-permute-start(bf16[2,128,256]{2,1,0:T(8,128)(2,1)S(1)} %pad_maximum_fusion.1), channel_id=1, source_target_pairs={{0,1},{1,0},{2,3},{3,2},{4,5},{5,4},{6,7},{7,6},{8,9},{9,8},{10,11... | collective-permute-start | bytes 393224 | tf_op jit(solution)/shard_map/ppermute | solution.py:180
